TPU v7x, 128 devices: a whole 4x4x4 slice. The times are simulated.
128 devices in a mesh: row: 8 (over z, core), col: 16 (over y, x).
Axes of the slice: x: 4, y: 4, z: 4, core: 2. Of those that a mesh axis runs over, the one named last changes fastest.
Arguments:
- load_vectors: float32 [2, 64, 98304], P(None, 'col', 'row'), may hold values from -6 to 6
- panel_factor: float32 [2, 16, 8, 8, 98304], P(None, 'col', None, None, 'row'), may hold values from -0.125 to 0.125
- diag_inverse: float32 [2, 8, 128, 128], replicated, may hold values from -1.4 to 1.4
- trail_adjoint: float32 [2, 64, 97280], P(None, 'col', 'row'), may hold values from -0.615587 to 0.615587
- adjoint_loads: float32 [2, 64, 1024], replicated, may hold values from -6 to 6
Outputs:
- solution: float32 [2, 64, 1024], P(None, 'col')
- trail_residual: float32 [2, 64, 97280], P(None, 'col', 'row')
- adjoint_solution: float32 [2, 64, 1024], P(None, 'col')
All inputs are finite; a program needn't handle non-finite values.
Results may differ from a plain program's by a relative error of at most 0.0001.
Values sent between devices are 32-bit elements; how exact they have to be, the bound alone decides.
No kernel may reach another device: no remote copies, remote signals or barrier semaphores. Data moves between devices by JAX's collectives and lax.ppermute only.
A program may use at most 128 MiB of HBM per device.

v0:
```python
import jax
import jax.numpy as jnp
from jax import lax
from jax.sharding import PartitionSpec as P

NB = 128
STEPS = 8
NRHS = 64


def from_root(array, axis, root):
    mine = lax.axis_index(axis) == root
    return lax.psum(jnp.where(mine, array, jnp.zeros_like(array)), axis)


def complex_product(pattern, former, latter, conjugate=False):
    highest = lax.Precision.HIGHEST
    former_re = former[0]
    former_im = former[1]
    if conjugate:
        former_im = -former_im
    real_part = jnp.einsum(pattern, former_re, latter[0], precision=highest) - jnp.einsum(
        pattern, former_im, latter[1], precision=highest
    )
    imag_part = jnp.einsum(pattern, former_re, latter[1], precision=highest) + jnp.einsum(
        pattern, former_im, latter[0], precision=highest
    )
    return jnp.stack([real_part, imag_part])


def body(load_vectors, panel_factor, diag_inverse, trail_adjoint, adjoint_loads):
    row_index = lax.axis_index("row")
    col_index = lax.axis_index("col")
    row_count = lax.axis_size("row")
    per_col = load_vectors.shape[1]
    width = panel_factor.shape[3]
    depth = STEPS // row_count
    window = depth * NB
    first_rhs = col_index * per_col
    factor = panel_factor[:, 0]
    factor_window = factor[..., :window]
    factor_trail = factor[..., window:]
    zsums = complex_product(
        "kir,br->bki", factor_trail, lax.all_gather(trail_adjoint, "col", axis=1, tiled=True), True
    )
    levels = (
        jnp.arange(depth, dtype=jnp.int32)[:, None] * row_count
        + row_index
        + jnp.zeros((1, NB), jnp.int32)
    ).reshape(window)
    accum = lax.dynamic_update_slice(
        jnp.zeros((2, NRHS, window), jnp.float32), load_vectors[:, :, :window], (0, first_rhs, 0)
    )
    adjoint_window = jnp.zeros((2, NRHS, window), jnp.float32)
    forward_parts = [None] * STEPS
    own_parts = [None] * STEPS
    adjoint_parts = [None] * STEPS
    for offset in range(STEPS):
        forward_accum = accum
        forward_owner_row = offset % row_count
        residual_block = forward_accum
        summed = lax.psum(residual_block, "col")
        forward_solved = from_root(
            complex_product("bl,jl->bj", summed, diag_inverse[:, offset]), "row", forward_owner_row
        )
        own_part = lax.dynamic_slice_in_dim(forward_solved, col_index * width, width, 2)
        update = complex_product("bi,ir->br", own_part, factor_window[:, offset])
        forward_accum = forward_accum - update * (levels > offset).astype(jnp.float32)
        accum, forward_parts[offset], own_parts[offset] = (forward_accum, forward_solved, own_part)
    for offset in range(STEPS):
        backward = STEPS - 1 - offset
        adjoint_adjoint_window = adjoint_window
        owner_row = backward % row_count
        masked = adjoint_adjoint_window * (levels > backward).astype(jnp.float32)
        partial_sum = zsums[:, :, backward] + complex_product(
            "ir,br->bi", factor_window[:, backward], masked, True
        )
        reduced = lax.psum(partial_sum, "row")
        gathered = lax.all_gather(reduced, "col", axis=2, tiled=True)
        vector = adjoint_loads[:, :, backward * NB : (backward + 1) * NB] - gathered
        solved = complex_product("lj,bl->bj", diag_inverse[:, backward], vector, True)
        current = adjoint_adjoint_window
        adjoint_adjoint_window = jnp.where(row_index == owner_row, solved, current)
        adjoint_window, adjoint_parts[backward] = (adjoint_adjoint_window, solved)
    stacked_own = jnp.stack(own_parts, 2)
    solution = lax.dynamic_slice_in_dim(
        jnp.stack(forward_parts, 2).reshape(2, NRHS, STEPS * NB), first_rhs, per_col, 1
    )
    adjoint_solution = lax.dynamic_slice_in_dim(
        jnp.stack(adjoint_parts, 2).reshape(2, NRHS, STEPS * NB), first_rhs, per_col, 1
    )
    trail_term = -complex_product("bki,kir->br", stacked_own, factor_trail)
    trail_residual = (
        lax.psum_scatter(trail_term, "col", scatter_dimension=1, tiled=True)
        + load_vectors[:, :, window:]
    )
    return (solution, trail_residual, adjoint_solution)


def solution(mesh):
    in_specs = (
        P(None, "col", "row"),
        P(None, "col", None, None, "row"),
        P(),
        P(None, "col", "row"),
        P(),
    )
    out_specs = (P(None, "col", None), P(None, "col", "row"), P(None, "col", None))
    return jax.shard_map(body, mesh=mesh, in_specs=in_specs, out_specs=out_specs, check_vma=False)
```

profile of v0, /device:TPU:8, one launch (start us, length us, event | category | flops | bytes accessed | tf_op | source)
XLA Modules:
  0.0 1733.8 jit_solution(3567037335746368436)
XLA Ops:
  8.7 9.2 copy.149
  17.8 76.6 %all-reduce.19.cloned.1.call-done = f32[2,64,128]{2,1,0:T(8,128)} async-done(((f32[2,64,128]{2,1,0:T(8,128)}), f32[2,64,128]{2,1,0:T(8,128)}) %all-reduce.19.cloned.1.call-update) | async-done | bytes 65552 | tf_op jit(solution)/shard_map/psum | solution.py:62
  100.1 57.9 %all-reduce.21.cloned.1.call-done = f32[2,64,128]{2,1,0:T(8,128)} async-done(((f32[2,64,128]{2,1,0:T(8,128)}), f32[2,64,128]{2,1,0:T(8,128)}) %all-reduce.21.cloned.1.call-update) | async-done | bytes 65552 | tf_op jit(solution)/shard_map/psum | solution.py:13
  158.0 1.1 fusion.290
  162.8 79.3 %all-reduce.23.cloned.1.call-done = f32[2,64,128]{2,1,0:T(8,128)} async-done(((f32[2,64,128]{2,1,0:T(8,128)}), f32[2,64,128]{2,1,0:T(8,128)}) %all-reduce.23.cloned.1.call-update) | async-done | bytes 65552 | tf_op jit(solution)/shard_map/psum | solution.py:62
  246.8 58.8 %all-reduce.25.cloned.1.call-done = f32[2,64,128]{2,1,0:T(8,128)} async-done(((f32[2,64,128]{2,1,0:T(8,128)}), f32[2,64,128]{2,1,0:T(8,128)}) %all-reduce.25.cloned.1.call-update) | async-done | bytes 65552 | tf_op jit(solution)/shard_map/psum | solution.py:13
  305.6 1.1 fusion.292
  310.4 79.3 %all-reduce.27.cloned.1.call-done = f32[2,64,128]{2,1,0:T(8,128)} async-done(((f32[2,64,128]{2,1,0:T(8,128)}), f32[2,64,128]{2,1,0:T(8,128)}) %all-reduce.27.cloned.1.call-update) | async-done | bytes 65552 | tf_op jit(solution)/shard_map/psum | solution.py:62
  394.4 2.0 slice_negate_fusion.7
  396.4 56.7 %all-reduce.29.cloned.1.call-done = f32[2,64,128]{2,1,0:T(8,128)} async-done(((f32[2,64,128]{2,1,0:T(8,128)}), f32[2,64,128]{2,1,0:T(8,128)}) %all-reduce.29.cloned.1.call-update) | async-done | bytes 65552 | tf_op jit(solution)/shard_map/psum | solution.py:13
  453.2 1.1 fusion.294
  458.0 79.3 %all-reduce.31.cloned.1.call-done = f32[2,64,128]{2,1,0:T(8,128)} async-done(((f32[2,64,128]{2,1,0:T(8,128)}), f32[2,64,128]{2,1,0:T(8,128)}) %all-reduce.31.cloned.1.call-update) | async-done | bytes 65552 | tf_op jit(solution)/shard_map/psum | solution.py:62
  542.0 58.8 %all-reduce.33.cloned.1.call-done = f32[2,64,128]{2,1,0:T(8,128)} async-done(((f32[2,64,128]{2,1,0:T(8,128)}), f32[2,64,128]{2,1,0:T(8,128)}) %all-reduce.33.cloned.1.call-update) | async-done | bytes 65552 | tf_op jit(solution)/shard_map/psum | solution.py:13
  600.8 1.1 fusion.296
  605.6 79.3 %all-reduce.35.cloned.1.call-done = f32[2,64,128]{2,1,0:T(8,128)} async-done(((f32[2,64,128]{2,1,0:T(8,128)}), f32[2,64,128]{2,1,0:T(8,128)}) %all-reduce.35.cloned.1.call-update) | async-done | bytes 65552 | tf_op jit(solution)/shard_map/psum | solution.py:62
  689.8 58.6 %all-reduce.37.cloned.1.call-done = f32[2,64,128]{2,1,0:T(8,128)} async-done(((f32[2,64,128]{2,1,0:T(8,128)}), f32[2,64,128]{2,1,0:T(8,128)}) %all-reduce.37.cloned.1.call-update) | async-done | bytes 65552 | tf_op jit(solution)/shard_map/psum | solution.py:13
  748.4 1.1 fusion.298
  753.3 79.2 %all-reduce.39.cloned.1.call-done = f32[2,64,128]{2,1,0:T(8,128)} async-done(((f32[2,64,128]{2,1,0:T(8,128)}), f32[2,64,128]{2,1,0:T(8,128)}) %all-reduce.39.cloned.1.call-update) | async-done | bytes 65552 | tf_op jit(solution)/shard_map/psum | solution.py:62
  835.5 1.0 fusion.53
  837.4 58.6 %all-reduce.41.cloned.1.call-done = f32[2,64,128]{2,1,0:T(8,128)} async-done(((f32[2,64,128]{2,1,0:T(8,128)}), f32[2,64,128]{2,1,0:T(8,128)}) %all-reduce.41.cloned.1.call-update) | async-done | bytes 65552 | tf_op jit(solution)/shard_map/psum | solution.py:13
  896.0 1.1 fusion.300
  901.0 79.2 %all-reduce.43.cloned.1.call-done = f32[2,64,128]{2,1,0:T(8,128)} async-done(((f32[2,64,128]{2,1,0:T(8,128)}), f32[2,64,128]{2,1,0:T(8,128)}) %all-reduce.43.cloned.1.call-update) | async-done | bytes 65552 | tf_op jit(solution)/shard_map/psum | solution.py:62
  985.0 58.6 %all-reduce.45.cloned.1.call-done = f32[2,64,128]{2,1,0:T(8,128)} async-done(((f32[2,64,128]{2,1,0:T(8,128)}), f32[2,64,128]{2,1,0:T(8,128)}) %all-reduce.45.cloned.1.call-update) | async-done | bytes 65552 | tf_op jit(solution)/shard_map/psum | solution.py:13
  1048.5 79.2 %all-reduce.47.cloned.1.call-done = f32[2,64,128]{2,1,0:T(8,128)} async-done(((f32[2,64,128]{2,1,0:T(8,128)}), f32[2,64,128]{2,1,0:T(8,128)}) %all-reduce.47.cloned.1.call-update) | async-done | bytes 65552 | tf_op jit(solution)/shard_map/psum | solution.py:62
  1133.9 57.3 %all-reduce.49.cloned.1.call-done = f32[2,64,128]{2,1,0:T(8,128)} async-done(((f32[2,64,128]{2,1,0:T(8,128)}), f32[2,64,128]{2,1,0:T(8,128)}) %all-reduce.49.cloned.1.call-update) | async-done | bytes 65552 | tf_op jit(solution)/shard_map/psum | solution.py:13
  1191.2 1.1 dynamic-slice_bitcast_fusion
  1192.5 4.9 convolution_bitcast_fusion
  1197.4 4.7 convolution_bitcast_fusion.2
  1202.1 2.9 fusion.3
  1205.0 2.9 fusion.1
  1208.0 3.2 maximum_negate_fusion
  1221.3 5.0 negate_bitcast_fusion
  1227.1 104.3 %all-reduce.51.cloned.1.call-done = f32[2,64,12160]{2,1,0:T(8,128)} async-done(((f32[2,64,12160]{2,1,0:T(8,128)}), f32[2,64,12160]{2,1,0:T(8,128)}) %all-reduce.51.cloned.1.call-update) | async-done | bytes 6225936
  1331.4 2.1 dynamic-slice_add_fusion
  1333.4 60.8 %all-gather.2.cloned.1.call-done = f32[2,64,12160]{2,0,1:T(2,128)} async-done(((f32[2,4,12160]{2,0,1:T(2,128)}), f32[2,64,12160]{2,0,1:T(2,128)}) %all-gather.2.cloned.1.call-update) | async-done | bytes 6225936 | tf_op jit(solution)/shard_map/all_gather | solution.py:44
  1394.3 12.6 fusion.364
  1406.9 5.3 fusion.7
  1412.2 3.5 fusion.6
  1415.7 3.3 fusion.19
  1419.0 3.3 fusion.25
  1422.3 15.2 psum.184
  1437.5 21.6 %all_gather.28 = f32[2,64,128]{1,2,0:T(8,128)S(1)} all-gather(f32[2,64,8]{1,2,0:T(8,128)S(1)} %psum.184), channel_id=1, replica_groups=mesh['row'=8,'col'=16] {'col'}, dimensions={2}, use_global_device_ids=true | all-gather | bytes 69632 | tf_op jit(solution)/shard_map/all_gather | solution.py:79
  1459.1 1.1 fusion.115
  1460.2 1.1 fusion.117
  1461.4 1.1 fusion.42
  1462.5 1.1 fusion.43
  1464.3 12.7 psum.185
  1477.0 23.1 %all_gather.29 = f32[2,64,128]{1,2,0:T(8,128)S(1)} all-gather(f32[2,64,8]{1,2,0:T(8,128)S(1)} %psum.185), channel_id=1, replica_groups=mesh['row'=8,'col'=16] {'col'}, dimensions={2}, use_global_device_ids=true | all-gather | bytes 69632 | tf_op jit(solution)/shard_map/all_gather | solution.py:79
  1500.1 1.1 fusion.125
  1501.2 1.1 fusion.127
  1502.3 1.1 fusion.40
  1503.5 1.1 fusion.41
  1505.3 12.7 psum.186
  1518.0 21.8 %all_gather.30 = f32[2,64,128]{1,2,0:T(8,128)S(1)} all-gather(f32[2,64,8]{1,2,0:T(8,128)S(1)} %psum.186), channel_id=1, replica_groups=mesh['row'=8,'col'=16] {'col'}, dimensions={2}, use_global_device_ids=true | all-gather | bytes 69632 | tf_op jit(solution)/shard_map/all_gather | solution.py:79
  1541.6 12.7 psum.187
  1554.3 23.1 %all_gather.31 = f32[2,64,128]{1,2,0:T(8,128)S(1)} all-gather(f32[2,64,8]{1,2,0:T(8,128)S(1)} %psum.187), channel_id=1, replica_groups=mesh['row'=8,'col'=16] {'col'}, dimensions={2}, use_global_device_ids=true | all-gather | bytes 69632 | tf_op jit(solution)/shard_map/all_gather | solution.py:79
  1579.2 12.7 psum.188
  1591.9 21.5 %all_gather.32 = f32[2,64,128]{1,2,0:T(8,128)S(1)} all-gather(f32[2,64,8]{1,2,0:T(8,128)S(1)} %psum.188), channel_id=1, replica_groups=mesh['row'=8,'col'=16] {'col'}, dimensions={2}, use_global_device_ids=true | all-gather | bytes 69632 | tf_op jit(solution)/shard_map/all_gather | solution.py:79
  1615.2 12.7 psum.189
  1627.9 23.1 %all_gather.33 = f32[2,64,128]{1,2,0:T(8,128)S(1)} all-gather(f32[2,64,8]{1,2,0:T(8,128)S(1)} %psum.189), channel_id=1, replica_groups=mesh['row'=8,'col'=16] {'col'}, dimensions={2}, use_global_device_ids=true | all-gather | bytes 69632 | tf_op jit(solution)/shard_map/all_gather | solution.py:79
  1652.8 12.7 psum.190
  1665.5 21.5 %all_gather.34 = f32[2,64,128]{1,2,0:T(8,128)S(1)} all-gather(f32[2,64,8]{1,2,0:T(8,128)S(1)} %psum.190), channel_id=1, replica_groups=mesh['row'=8,'col'=16] {'col'}, dimensions={2}, use_global_device_ids=true | all-gather | bytes 69632 | tf_op jit(solution)/shard_map/all_gather | solution.py:79
  1688.9 12.7 psum.191
  1701.5 23.1 %all_gather.35 = f32[2,64,128]{1,2,0:T(8,128)S(1)} all-gather(f32[2,64,8]{1,2,0:T(8,128)S(1)} %psum.191), channel_id=1, replica_groups=mesh['row'=8,'col'=16] {'col'}, dimensions={2}, use_global_device_ids=true | all-gather | bytes 69632 | tf_op jit(solution)/shard_map/all_gather | solution.py:79
  (296 shorter events, 90.5 us)
Async XLA Ops:
  7.2 87.3 %all-reduce.19.cloned.1.call-start = ((), (), s32[]{:S(2)}) async-start(), calls=%async_computation | async-start | bytes 131072 | tf_op jit(solution)/shard_map/psum | solution.py:62
  7.9 0.6 copy-start.5
  8.6 149.4 %all-reduce.21.cloned.1.call-start = ((), (), s32[]{:S(2)}) async-start(), calls=%async_computation.1 | async-start | bytes 131072 | tf_op jit(solution)/shard_map/psum | solution.py:13
  8.6 85.8 %copy-start.3 = (f32[2,8,128,128]{3,2,1,0:T(8,128)S(1)}, f32[2,8,128,128]{3,2,1,0:T(8,128)}, u32[]{:S(2)}) copy-start(f32[2,8,128,128]{3,2,1,0:T(8,128)} %param.7) | copy-start | bytes 3145732
  8.7 153.4 %copy-start.6 = (f32[2,64,128]{2,1,0:T(8,128)S(1)}, f32[2,64,128]{2,1,0:T(8,128)}, u32[]{:S(2)}) copy-start(f32[2,64,128]{2,1,0:T(8,128)} %copy-done.5) | copy-start | bytes 196612
  99.2 142.9 %all-reduce.23.cloned.1.call-start = ((), (), s32[]{:S(2)}) async-start(), calls=%async_computation.2 | async-start | bytes 131072 | tf_op jit(solution)/shard_map/psum | solution.py:62
  158.0 531.6 %copy-start.7 = (f32[2,64,128]{2,1,0:T(8,128)S(1)}, f32[2,64,128]{2,1,0:T(8,128)}, u32[]{:S(2)}) copy-start(f32[2,64,128]{2,1,0:T(8,128)} %all-reduce.21.cloned.1.call-done) | copy-start | bytes 196612
  162.7 142.9 %all-reduce.25.cloned.1.call-start = ((), (), s32[]{:S(2)}) async-start(), calls=%async_computation.3 | async-start | bytes 131072 | tf_op jit(solution)/shard_map/psum | solution.py:13
  246.8 142.9 %all-reduce.27.cloned.1.call-start = ((), (), s32[]{:S(2)}) async-start(), calls=%async_computation.4 | async-start | bytes 131072 | tf_op jit(solution)/shard_map/psum | solution.py:62
  305.6 447.6 %copy-start.8 = (f32[2,64,128]{2,1,0:T(8,128)S(1)}, f32[2,64,128]{2,1,0:T(8,128)}, u32[]{:S(2)}) copy-start(f32[2,64,128]{2,1,0:T(8,128)} %all-reduce.25.cloned.1.call-done) | copy-start | bytes 196612
  310.3 142.9 %all-reduce.29.cloned.1.call-start = ((), (), s32[]{:S(2)}) async-start(), calls=%async_computation.5 | async-start | bytes 131072 | tf_op jit(solution)/shard_map/psum | solution.py:13
  394.3 142.9 %all-reduce.31.cloned.1.call-start = ((), (), s32[]{:S(2)}) async-start(), calls=%async_computation.6 | async-start | bytes 131072 | tf_op jit(solution)/shard_map/psum | solution.py:62
  453.2 384.1 %copy-start.9 = (f32[2,64,128]{2,1,0:T(8,128)S(1)}, f32[2,64,128]{2,1,0:T(8,128)}, u32[]{:S(2)}) copy-start(f32[2,64,128]{2,1,0:T(8,128)} %all-reduce.29.cloned.1.call-done) | copy-start | bytes 196612
  457.9 142.9 %all-reduce.33.cloned.1.call-start = ((), (), s32[]{:S(2)}) async-start(), calls=%async_computation.7 | async-start | bytes 131072 | tf_op jit(solution)/shard_map/psum | solution.py:13
  541.9 142.9 %all-reduce.35.cloned.1.call-start = ((), (), s32[]{:S(2)}) async-start(), calls=%async_computation.8 | async-start | bytes 131072 | tf_op jit(solution)/shard_map/psum | solution.py:62
  600.8 300.0 %copy-start.10 = (f32[2,64,128]{2,1,0:T(8,128)S(1)}, f32[2,64,128]{2,1,0:T(8,128)}, u32[]{:S(2)}) copy-start(f32[2,64,128]{2,1,0:T(8,128)} %all-reduce.33.cloned.1.call-done) | copy-start | bytes 196612
  605.5 142.9 %all-reduce.37.cloned.1.call-start = ((), (), s32[]{:S(2)}) async-start(), calls=%async_computation.9 | async-start | bytes 131072 | tf_op jit(solution)/shard_map/psum | solution.py:13
  689.5 143.0 %all-reduce.39.cloned.1.call-start = ((), (), s32[]{:S(2)}) async-start(), calls=%async_computation.10 | async-start | bytes 131072 | tf_op jit(solution)/shard_map/psum | solution.py:62
  748.4 236.5 %copy-start.11 = (f32[2,64,128]{2,1,0:T(8,128)S(1)}, f32[2,64,128]{2,1,0:T(8,128)}, u32[]{:S(2)}) copy-start(f32[2,64,128]{2,1,0:T(8,128)} %all-reduce.37.cloned.1.call-done) | copy-start | bytes 196612
  753.1 142.9 %all-reduce.41.cloned.1.call-start = ((), (), s32[]{:S(2)}) async-start(), calls=%async_computation.11 | async-start | bytes 131072 | tf_op jit(solution)/shard_map/psum | solution.py:13
  837.2 143.0 %all-reduce.43.cloned.1.call-start = ((), (), s32[]{:S(2)}) async-start(), calls=%async_computation.12 | async-start | bytes 131072 | tf_op jit(solution)/shard_map/psum | solution.py:62
  896.0 152.4 %copy-start.12 = (f32[2,64,128]{2,1,0:T(8,128)S(1)}, f32[2,64,128]{2,1,0:T(8,128)}, u32[]{:S(2)}) copy-start(f32[2,64,128]{2,1,0:T(8,128)} %all-reduce.41.cloned.1.call-done) | copy-start | bytes 196612
  900.8 142.9 %all-reduce.45.cloned.1.call-start = ((), (), s32[]{:S(2)}) async-start(), calls=%async_computation.13 | async-start | bytes 131072 | tf_op jit(solution)/shard_map/psum | solution.py:13
  984.8 142.9 %all-reduce.47.cloned.1.call-start = ((), (), s32[]{:S(2)}) async-start(), calls=%async_computation.14 | async-start | bytes 131072 | tf_op jit(solution)/shard_map/psum | solution.py:62
  1048.3 142.9 %all-reduce.49.cloned.1.call-start = ((), (), s32[]{:S(2)}) async-start(), calls=%async_computation.15 | async-start | bytes 131072 | tf_op jit(solution)/shard_map/psum | solution.py:13
  1132.4 199.0 %all-reduce.51.cloned.1.call-start = ((), (), s32[]{:S(2)}) async-start(), calls=%async_computation.17 | async-start | bytes 12451840
  1191.2 10.9 slice-start
  1192.5 9.6 slice-start.1
  1211.1 1.0 copy-start.23
  1211.1 2.0 copy-start.22
  1211.1 8.1 copy-start.29
  1211.1 183.1 %all-gather.2.cloned.1.call-start = ((), (), s32[]{:S(2)}) async-start(), calls=%async_computation.16 | async-start | bytes 6615040 | tf_op jit(solution)/shard_map/all_gather | solution.py:44
  1221.3 5.1 copy-start.13
  1221.3 5.1 copy-start.24
  1406.9 5.3 copy-start
  1406.9 5.3 copy-start.2
  1412.2 3.5 copy-start.1
  1418.9 3.4 copy-start.27
  1419.0 3.4 copy-start.28
  1419.0 40.1 %copy-start.21 = (f32[2,64,128]{1,2,0:T(8,128)S(1)}, f32[2,64,128]{1,2,0:T(8,128)}, u32[]{:S(2)}) copy-start(f32[2,64,128]{1,2,0:T(8,128)} %copy.113) | copy-start | bytes 196612
  1419.0 45.0 %copy-start.26 = (f32[1,1,8,128]{3,1,2,0:T(1,128)S(1)}, f32[1,1,8,128]{3,1,2,0:T(1,128)}, u32[]{:S(2)}) copy-start(f32[1,1,8,128]{3,1,2,0:T(1,128)} %get-tuple-element.15) | copy-start | bytes 12292
  1419.0 81.1 %copy-start.20 = (f32[2,64,128]{1,2,0:T(8,128)S(1)}, f32[2,64,128]{1,2,0:T(8,128)}, u32[]{:S(2)}) copy-start(f32[2,64,128]{1,2,0:T(8,128)} %copy.112) | copy-start | bytes 196612
  1422.2 82.7 %copy-start.25 = (f32[1,1,8,128]{3,1,2,0:T(1,128)S(1)}, f32[1,1,8,128]{3,1,2,0:T(1,128)}, u32[]{:S(2)}) copy-start(f32[1,1,8,128]{3,1,2,0:T(1,128)} %get-tuple-element.14) | copy-start | bytes 12292
  1422.3 117.5 %copy-start.19 = (f32[2,64,128]{1,2,0:T(8,128)S(1)}, f32[2,64,128]{1,2,0:T(8,128)}, u32[]{:S(2)}) copy-start(f32[2,64,128]{1,2,0:T(8,128)} %copy.111) | copy-start | bytes 196612
  1422.3 117.5 %copy-start.4 = (f32[2,8,128,128]{3,2,1,0:T(8,128)S(1)}, f32[2,8,128,128]{3,2,1,0:T(8,128)}, u32[]{:S(2)}) copy-start(f32[2,8,128,128]{3,2,1,0:T(8,128)} %param.7) | copy-start | bytes 3145732
  1422.3 155.1 %copy-start.18 = (f32[2,64,128]{1,2,0:T(8,128)S(1)}, f32[2,64,128]{1,2,0:T(8,128)}, u32[]{:S(2)}) copy-start(f32[2,64,128]{1,2,0:T(8,128)} %copy.110) | copy-start | bytes 196612
  1461.3 152.1 %copy-start.17 = (f32[2,64,128]{1,2,0:T(8,128)S(1)}, f32[2,64,128]{1,2,0:T(8,128)}, u32[]{:S(2)}) copy-start(f32[2,64,128]{1,2,0:T(8,128)} %copy.109) | copy-start | bytes 196612
  1503.4 147.6 %copy-start.16 = (f32[2,64,128]{1,2,0:T(8,128)S(1)}, f32[2,64,128]{1,2,0:T(8,128)}, u32[]{:S(2)}) copy-start(f32[2,64,128]{1,2,0:T(8,128)} %copy.108) | copy-start | bytes 196612
  1540.6 146.4 %copy-start.15 = (f32[2,64,128]{1,2,0:T(8,128)S(1)}, f32[2,64,128]{1,2,0:T(8,128)}, u32[]{:S(2)}) copy-start(f32[2,64,128]{1,2,0:T(8,128)} %copy.107) | copy-start | bytes 196612
  1578.2 146.4 %copy-start.14 = (f32[2,64,128]{1,2,0:T(8,128)S(1)}, f32[2,64,128]{1,2,0:T(8,128)}, u32[]{:S(2)}) copy-start(f32[2,64,128]{1,2,0:T(8,128)} %copy.104) | copy-start | bytes 196612
Sparse Core Ops, SparseCore 0:
  11.8 82.6 all-reduce.18
  99.3 58.6 all-reduce.20
  162.8 79.1 all-reduce.22
  246.9 58.6 all-reduce.24
  310.4 79.1 all-reduce.26
  394.5 58.6 all-reduce.28
  458.0 79.1 all-reduce.30
  542.1 58.6 all-reduce.32
  605.6 79.1 all-reduce.34
  689.7 58.6 all-reduce.36
  753.2 79.2 all-reduce.38
  837.3 58.6 all-reduce.40
  900.9 79.2 all-reduce.42
  984.9 58.6 all-reduce.44
  1048.5 79.2 all-reduce.46
  1132.5 58.6 all-reduce.48
  1211.2 120.0 all-reduce.50
  1333.4 60.8 all-gather.1
where the time goes:
time: 1750 us; the launch traced here: 1730 us
  waiting for transfers between devices  1260 us (72%)
  blocking collectives  283 us (16%)
  matrix products  111 us (6%)
  local copies, waits for them, and re-layouts  37.2 us (2%)
  other arithmetic  22.3 us (1%)
    psum x8, waiting for transfers between devices, body(): summed = lax.psum(residual_block, 'col')  631 us
    psum x8, waiting for transfers between devices, from_root(): return lax.psum(jnp.where(mine, array, jnp.zeros_like(array)), axis)  465 us
    all_gather x8, blocking collectives, body(): gathered = lax.all_gather(reduced, 'col', axis=2, tiled=True)  179 us
    unnamed x19, waiting for transfers between devices  105 us
    psum x8, blocking collectives, body(): reduced = lax.psum(partial_sum, 'row')  104 us
    all_gather x1, waiting for transfers between devices, body(): lax.all_gather(trail_adjoint, 'col', axis=1, tiled=True)  60.8 us
  transfers between devices with their start and end apart: 18, of which 18 were waited for; matrix products, arithmetic and copies ran while one was open for 2% of the time, Pallas kernels for 0%

commit v1 on v0

v1 whole, which is shorter than its diff:
```python
import jax
import jax.numpy as jnp
from jax import lax
from jax.experimental import pallas as pl
from jax.experimental.pallas import tpu as pltpu
from jax.sharding import PartitionSpec as P

NB = 128
STEPS = 8
ROWS_AXIS = 8
COLS_AXIS = 16
PER_COL = 4
WIDTH = 8
LOCAL = 12288
TRAIL_LOCAL = 12160
TILE = 2432
F32 = jnp.float32
BF16 = jnp.bfloat16


def times_i(x):
    rows = x.shape[0]
    rolled = pltpu.roll(x.reshape(rows // 8, 8, x.shape[1]), 4, 1).reshape(x.shape)
    part = lax.broadcasted_iota(jnp.int32, x.shape, 0) % 8
    return jnp.where(part < 4, -rolled, rolled)


def dot_nn(a, b, precision=lax.Precision.HIGHEST):
    return lax.dot_general(a, b, (((1,), (0,)), ((), ())), precision=precision, preferred_element_type=F32)


def dot_nt(a, b, precision=lax.Precision.HIGHEST):
    return lax.dot_general(a, b, (((1,), (1,)), ((), ())), precision=precision, preferred_element_type=F32)


def split(x):
    high = x.astype(BF16)
    return high, (x - high.astype(F32)).astype(BF16)


def dot_split(dot, a, b):
    a_high, a_low = a
    b_high, b_low = b
    native = lax.Precision.DEFAULT
    return dot(a_high, b_high, native) + (dot(a_high, b_low, native) + dot(a_low, b_high, native))


def block_of(g_ref, row, step, part):
    first = part * (STEPS * WIDTH) + step * WIDTH
    return g_ref[row, :, first : first + WIDTH, :].reshape(NB, NB)


def forward_kernel(col_ref, g_ref, d_ref, own_ref, sol_ref, acc, xs):
    col = col_ref[0]
    loads = 2 * STEPS * WIDTH
    for row in range(STEPS):
        acc[row] = g_ref[row, :, loads : loads + 2 * PER_COL, :].reshape(NB, NB)
    lane = lax.broadcasted_iota(jnp.int32, (NB, NB), 1)
    own = jnp.zeros((NB, NB), F32)
    for step in range(STEPS):
        a = acc[step]
        left = jnp.concatenate([a, times_i(a)], axis=1)
        inverse = jnp.concatenate([d_ref[0, step], d_ref[1, step]], axis=1)
        x = dot_nt(left, inverse)
        ix = times_i(x)
        xs[step] = x
        left = jnp.concatenate([x, ix], axis=1)
        for row in range(step + 1, STEPS):
            right = jnp.concatenate([block_of(g_ref, row, step, 0), block_of(g_ref, row, step, 1)], axis=0)
            acc[row] -= dot_nn(left, right)
        mine = pltpu.roll(x, (step * WIDTH - col * WIDTH + NB) % NB, 1)
        mine_i = pltpu.roll(ix, (64 + step * WIDTH - col * WIDTH + NB) % NB, 1)
        own = jnp.where(lane // WIDTH == step, mine, own)
        own = jnp.where(lane // WIDTH == step + STEPS, mine_i, own)
        sol_ref[:, step * NB : (step + 1) * NB] = xs[step, pl.ds(pl.multiple_of(col * 8, 8), 8), :]
    own_ref[...] = own


def backward_kernel(v_ref, g_ref, d_ref, out_ref, acc):
    acc[...] = v_ref[...]
    for step in reversed(range(STEPS)):
        v = acc[step]
        right = jnp.concatenate([d_ref[0, step], -d_ref[1, step]], axis=0)
        y = dot_nn(jnp.concatenate([v, times_i(v)], axis=1), right)
        out_ref[:, step * NB : (step + 1) * NB] = y
        left = jnp.concatenate([y, times_i(y)], axis=1)
        for other in range(step):
            right = jnp.concatenate([block_of(g_ref, step, other, 0), -block_of(g_ref, step, other, 1)], axis=1)
            acc[other] -= dot_nt(left, right)


def trail_kernel(x_ref, l_ref, out_ref):
    out_ref[...] = -dot_split(dot_nn, split(x_ref[...]), split(l_ref[...]))


def zsum_kernel(ta_ref, l_ref, out_ref):
    @pl.when(pl.program_id(0) == 0)
    def _():
        out_ref[...] = jnp.zeros_like(out_ref)

    out_ref[...] += dot_split(dot_nt, split(ta_ref[...]), split(l_ref[...]))

    @pl.when(pl.program_id(0) == pl.num_programs(0) - 1)
    def _():
        q = out_ref[...]
        out_ref[...] = q - times_i(pltpu.roll(q, 64, 1))


FACTOR_SPEC = pl.BlockSpec((pl.Element(NB), pl.Element(TILE)), lambda i: (0, (i * (TILE // NB) + 1) * NB))
VMEM = pl.BlockSpec(memory_space=pltpu.VMEM)
SMEM = pl.BlockSpec(memory_space=pltpu.SMEM)


def body(load_vectors, panel_factor, diag_inverse, trail_adjoint, adjoint_loads):
    col = lax.axis_index("col")
    factor = panel_factor.reshape(NB, LOCAL)
    loads = load_vectors.reshape(2 * PER_COL, LOCAL)
    packed = jnp.concatenate([factor[:, :NB], loads[:, :NB]], axis=0)
    window = lax.all_gather(packed, ("row", "col")).reshape(ROWS_AXIS, COLS_AXIS, 136, NB)
    own, sol = pl.pallas_call(
        forward_kernel,
        out_shape=[jax.ShapeDtypeStruct((NB, NB), F32), jax.ShapeDtypeStruct((8, STEPS * NB), F32)],
        in_specs=[SMEM, VMEM, VMEM],
        out_specs=[VMEM, VMEM],
        scratch_shapes=[pltpu.VMEM((STEPS, NB, NB), F32), pltpu.VMEM((STEPS, NB, NB), F32)],
        compiler_params=pltpu.CompilerParams(vmem_limit_bytes=32 * 2**20),
        name="forward",
    )(col.reshape(1), window, diag_inverse)
    trail = pl.pallas_call(
        trail_kernel,
        out_shape=jax.ShapeDtypeStruct((NB, TRAIL_LOCAL), F32),
        grid=(TRAIL_LOCAL // TILE,),
        in_specs=[pl.BlockSpec((NB, NB), lambda i: (0, 0)), FACTOR_SPEC],
        out_specs=pl.BlockSpec((NB, TILE), lambda i: (0, i)),
        compiler_params=pltpu.CompilerParams(vmem_limit_bytes=32 * 2**20),
        name="trail",
    )(own, factor)
    gathered = lax.all_gather(trail_adjoint.reshape(8, TRAIL_LOCAL), "col", axis=0, tiled=True)
    zpart = pl.pallas_call(
        zsum_kernel,
        out_shape=jax.ShapeDtypeStruct((NB, NB), F32),
        grid=(TRAIL_LOCAL // TILE,),
        in_specs=[pl.BlockSpec((NB, TILE), lambda i: (0, i)), FACTOR_SPEC],
        out_specs=pl.BlockSpec((NB, NB), lambda i: (0, 0)),
        compiler_params=pltpu.CompilerParams(vmem_limit_bytes=32 * 2**20),
        name="zsum",
    )(gathered, factor)
    spread = jnp.broadcast_to(zpart[:, :64].reshape(1, COLS_AXIS, 8, 64), (ROWS_AXIS, COLS_AXIS, 8, 64))
    met = lax.all_to_all(spread.reshape(128, 8, 64), ("row", "col"), 0, 0)
    zsum = met.reshape(ROWS_AXIS, COLS_AXIS, 8, STEPS, WIDTH).sum(0).transpose(2, 1, 0, 3).reshape(STEPS, 8, NB)
    mine = lax.dynamic_slice_in_dim(adjoint_loads, col * PER_COL, PER_COL, 1)
    vector = mine.reshape(8, STEPS, NB).transpose(1, 0, 2) - zsum
    adj = pl.pallas_call(
        backward_kernel,
        out_shape=jax.ShapeDtypeStruct((8, STEPS * NB), F32),
        in_specs=[VMEM, VMEM, VMEM],
        out_specs=VMEM,
        scratch_shapes=[pltpu.VMEM((STEPS, 8, NB), F32)],
        compiler_params=pltpu.CompilerParams(vmem_limit_bytes=32 * 2**20),
        name="backward",
    )(vector, window, diag_inverse)
    mine_trail = lax.psum_scatter(trail.reshape(COLS_AXIS, 8, TRAIL_LOCAL), "col", scatter_dimension=0, tiled=False)
    residual = mine_trail.reshape(2, PER_COL, TRAIL_LOCAL) + load_vectors[:, :, NB:]
    return sol.reshape(2, PER_COL, STEPS * NB), residual, adj.reshape(2, PER_COL, STEPS * NB)


def solution(mesh):
    in_specs = (
        P(None, "col", "row"),
        P(None, "col", None, None, "row"),
        P(),
        P(None, "col", "row"),
        P(),
    )
    out_specs = (P(None, "col", None), P(None, "col", "row"), P(None, "col", None))
    return jax.shard_map(body, mesh=mesh, in_specs=in_specs, out_specs=out_specs, check_vma=False)
```

time: 1750 us -> 246 us (0.14)
  waiting for transfers between devices: 1260 us -> 175 us
  blocking collectives: 283 us -> 0 us
  matrix products: 111 us -> 0 us
  Pallas kernels: 0 us -> 19.6 us
  other arithmetic: 22.3 us -> 2.79 us
    psum x16 -> x0, waiting for transfers between devices: 1100 us -> none  [the longest x8 631 us: body(): summed = lax.psum(residual_block, 'col')]
    all_gather x8 -> x0, blocking collectives: 179 us -> none  [body(): gathered = lax.all_gather(reduced, 'col', axis=2, tiled=True)]
    dot_general x130 -> x0, matrix products: 111 us -> none  [the longest x33 28.8 us: complex_product(): jnp.einsum(pattern, former_re, latter[0], precision=highest)]
    psum x8 -> x0, blocking collectives: 104 us -> none  [body(): reduced = lax.psum(partial_sum, 'row')]
    unnamed x19 -> x4, waiting for transfers between devices: 105 us -> 47.1 us
    all_gather x1 -> x2, waiting for transfers between devices: 60.8 us -> 116 us  [the longest x1 70.5 us: body(): lax.all_gather(packed, ('row', 'col'))]
    pallas_call x0 -> x4, Pallas kernels: none -> 19.6 us  [the longest x1 5.54 us: body(): pl.pallas_call(forward_kernel, out_shape=[jax.ShapeDtypeStruct((NB, NB),...]
  transfers between devices with their start and end apart: 18 -> 4, of which waited for: 18 -> 4; matrix products, arithmetic and copies ran while one was open for 2% -> 3% of each run, Pallas kernels for 0% -> 8%
where the time goes in v1:
time: 246 us; the launch traced here: 245 us
  waiting for transfers between devices  175 us (71%)
  local copies, waits for them, and re-layouts  25.2 us (10%)
  Pallas kernels  19.6 us (8%)
  between operations  13.9 us (6%)
  starting transfers between devices  8.06 us (3%)
  other arithmetic  2.79 us (1%)
    all_gather x1, waiting for transfers between devices, body(): lax.all_gather(packed, ('row', 'col'))  70.5 us
    unnamed x4, waiting for transfers between devices  47.1 us
    all_gather x1, waiting for transfers between devices, body(): lax.all_gather(trail_adjoint.reshape(8, TRAIL_LOCAL), 'col', axis=0, tile...  45.3 us
    unnamed x23, local copies, waits for them, and re-layouts  17.8 us
    all_to_all x1, waiting for transfers between devices, body(): met = lax.all_to_all(spread.reshape(128, 8, 64), ('row', 'col'), 0, 0)  12.1 us
    all_to_all x1, starting transfers between devices, body(): met = lax.all_to_all(spread.reshape(128, 8, 64), ('row', 'col'), 0, 0)  7.94 us
    pallas_call x1, Pallas kernels, body(): pl.pallas_call(forward_kernel, out_shape=[jax.ShapeDtypeStruct((NB, NB),...  5.54 us
    pallas_call x1, Pallas kernels, body(): pl.pallas_call(backward_kernel, out_shape=jax.ShapeDtypeStruct((8, STEPS...  5.44 us
  transfers between devices with their start and end apart: 4, of which 4 were waited for; matrix products, arithmetic and copies ran while one was open for 3% of the time, Pallas kernels for 8%

profile of v1, /device:TPU:8, one launch (start us, length us, event | category | flops | bytes accessed | tf_op | source)
XLA Modules:
  0.0 244.5 jit_solution(16367772995604736252)
XLA Ops:
  7.2 0.0 copy-start
  7.2 0.0 all-gather.6.cloned.1.call-start
  7.2 0.9 slice.16
  8.1 1.1 reshape.46
  9.3 0.6 pad_maximum_fusion
  9.9 0.0 all-gather.6.cloned.1.call-update
  9.9 0.0 all-gather.4.cloned.1.call-start
  10.0 1.9 reshape.51
  11.8 0.0 all-gather.4.cloned.1.call-update
  11.9 0.0 reduce-scatter.4.cloned.1.call-start
  11.9 70.5 %all-gather.6.cloned.1.call-done = f32[17408,128]{1,0:T(8,128)} async-done(((f32[136,128]{1,0:T(8,128)}), f32[17408,128]{1,0:T(8,128)}) %all-gather.6.cloned.1.call-update) | async-done | bytes 8912912 | tf_op jit(solution)/shard_map/all_gather | solution.py:119
  82.4 0.0 copy-start.1
  82.4 3.5 %copy-done.1 = f32[17408,128]{1,0:T(8,128)S(1)} copy-done((f32[17408,128]{1,0:T(8,128)S(1)}, f32[17408,128]{1,0:T(8,128)}, u32[]{:S(2)}) %copy-start.1) | copy-done | bytes 8912920
  86.0 0.0 copy-start.7
  86.0 1.2 copy-done.7
  87.2 0.0 copy-start.3
  87.2 5.5 %forward.1 = (f32[128,128]{1,0:T(8,128)S(1)}, f32[8,1024]{1,0:T(8,128)S(1)}) custom-call(s32[1]{0:T(128)} %bitcast.col_ref, f32[8,16,136,128]{3,2,1,0:T(8,128)S(1)} %bitcast.16, f32[2,8,128,128]{3,2,1,0:T(8,128)S(1)} %copy-done.7), custom_call_target="tpu_custom_call" | custom-call | tf_op jit(solution)/shard_map/forward/pallas_call | solution.py:120
  92.7 0.0 copy-done.3
  92.8 4.1 %trail.1 = f32[128,12160]{1,0:T(8,128)S(1)} custom-call(f32[128,128]{1,0:T(8,128)S(1)} %get-tuple-element.6.x_ref, f32[128,12288]{1,0:T(8,128)S(1)} %bitcast.19), custom_call_target="tpu_custom_call" | custom-call | tf_op jit(solution)/shard_map/trail/pallas_call | solution.py:129
  96.9 0.0 copy-start.5
  96.9 2.6 %copy-done.5 = f32[128,12160]{1,0:T(8,128)} copy-done((f32[128,12160]{1,0:T(8,128)}, f32[128,12160]{1,0:T(8,128)S(1)}, u32[]{:S(2)}) %copy-start.5) | copy-done | bytes 6225944
  99.4 0.0 reduce-scatter.4.cloned.1.call-update
  99.5 45.3 %all-gather.4.cloned.1.call-done.ta_ref = f32[128,12160]{1,0:T(8,128)} async-done(((f32[8,12160]{1,0:T(8,128)}), f32[128,12160]{1,0:T(8,128)}) %all-gather.4.cloned.1.call-update) | async-done | bytes 6225936 | tf_op jit(solution)/shard_map/all_gather | solution.py:138
  144.7 0.0 copy-start.4
  144.7 2.8 %copy-done.4 = f32[2,1,8,8,12288]{4,3,2,1,0:T(8,128)S(1)} copy-done((f32[2,1,8,8,12288]{4,3,2,1,0:T(8,128)S(1)}, f32[2,1,8,8,12288]{4,3,2,1,0:T(8,128)}, u32[]{:S(2)}) %copy-start.4) | copy-done | bytes 6291480
  147.5 0.0 copy-start.6
  147.5 2.8 %copy-done.6 = f32[128,12160]{1,0:T(8,128)S(1)} copy-done((f32[128,12160]{1,0:T(8,128)S(1)}, f32[128,12160]{1,0:T(8,128)}, u32[]{:S(2)}) %copy-start.6) | copy-done | bytes 6225944
  150.3 0.0 copy-start.8
  150.3 4.5 %zsum.1 = f32[128,128]{1,0:T(8,128)S(1)} custom-call(f32[128,12160]{1,0:T(8,128)S(1)} %copy-done.6, f32[128,12288]{1,0:T(8,128)S(1)} %bitcast.20), custom_call_target="tpu_custom_call" | custom-call | tf_op jit(solution)/shard_map/zsum/pallas_call | solution.py:139
  154.9 1.0 reshape.59
  155.9 7.9 %all-to-all-start = ((f32[128,1,512]{2,1,0:T(1,128)}), f32[128,1,512]{2,1,0:T(1,128)S(1)}, u32[]{:S(2)}, u32[]{:S(2)}) async-start(f32[128,1,512]{2,1,0:T(1,128)} %reshape.59), calls=%async_computation | async-start | bytes 524288 | tf_op jit(solution)/shard_map/all_to_all | solution.py:149
  163.9 0.0 copy-done
  163.9 12.1 %all-to-all-done = f32[128,1,512]{2,1,0:T(1,128)S(1)} async-done(((f32[128,1,512]{2,1,0:T(1,128)}), f32[128,1,512]{2,1,0:T(1,128)S(1)}, u32[]{:S(2)}, u32[]{:S(2)}) %all-to-all-start) | async-done | bytes 262176 | tf_op jit(solution)/shard_map/all_to_all | solution.py:149
  176.0 0.5 broadcast
  176.5 1.3 reduce.1
  177.8 0.1 reshape.60
  177.9 0.0 copy-start.9
  178.0 0.1 copy.15
  178.1 0.2 copy.14
  178.3 0.3 reshape.54
  178.6 0.0 copy-done.8
  178.6 0.0 copy-start.2
  178.6 3.6 %copy-done.2 = f32[17408,128]{1,0:T(8,128)S(1)} copy-done((f32[17408,128]{1,0:T(8,128)S(1)}, f32[17408,128]{1,0:T(8,128)}, u32[]{:S(2)}) %copy-start.2) | copy-done | bytes 8912920
  182.3 5.4 %backward.1 = f32[8,1024]{1,0:T(8,128)S(1)} custom-call(f32[8,8,128]{2,1,0:T(8,128)S(1)} %bitcast_subtract_fusion.v_ref, f32[8,16,136,128]{3,2,1,0:T(8,128)S(1)} %bitcast.17, f32[2,8,128,128]{3,2,1,0:T(8,128)S(1)} %copy-done.8), custom_call_target="tpu_custom_call" | custom-call | tf_op jit(solution)/shard_map/backward/pallas_call | solution.py:153
  187.7 0.7 reshape.55
  188.4 0.6 reshape.48
  189.0 47.1 %reduce-scatter.4.cloned.1.call-done = f32[1,8,12160]{2,1,0:T(8,128)} async-done(((f32[16,8,12160]{2,1,0:T(8,128)}), f32[1,8,12160]{2,1,0:T(8,128)}) %reduce-scatter.4.cloned.1.call-update) | async-done | bytes 389136
  236.0 1.1 reshape_reduce_scatter.3
  237.2 0.0 copy-done.9
  237.2 0.8 slice_add_fusion
  (7 shorter events, 0.1 us)
Async XLA Ops:
  7.2 156.7 %copy-start = (f32[2,64,1024]{2,1,0:T(8,128)S(1)}, f32[2,64,1024]{2,1,0:T(8,128)}, u32[]{:S(2)}) copy-start(f32[2,64,1024]{2,1,0:T(8,128)} %param.9) | copy-start | bytes 1572868
  7.2 75.3 %all-gather.6.cloned.1.call-start = ((), (), s32[]{:S(2)}) async-start(), calls=%async_computation.3 | async-start | bytes 8982528 | tf_op jit(solution)/shard_map/all_gather | solution.py:119
  9.9 134.8 %all-gather.4.cloned.1.call-start = ((), (), s32[]{:S(2)}) async-start(), calls=%async_computation.2 | async-start | bytes 6615040 | tf_op jit(solution)/shard_map/all_gather | solution.py:138
  11.9 224.2 %reduce-scatter.4.cloned.1.call-start = ((), (), s32[]{:S(2)}) async-start(), calls=%async_computation.4 | async-start | bytes 6615040
  82.4 3.5 %copy-start.1 = (f32[17408,128]{1,0:T(8,128)S(1)}, f32[17408,128]{1,0:T(8,128)}, u32[]{:S(2)}) copy-start(f32[17408,128]{1,0:T(8,128)} %all-gather.6.cloned.1.call-done) | copy-start | bytes 26738692
  86.0 1.2 copy-start.7
  87.2 5.5 %copy-start.3 = (f32[2,1,8,8,12288]{4,3,2,1,0:T(8,128)S(1)}, f32[2,1,8,8,12288]{4,3,2,1,0:T(8,128)}, u32[]{:S(2)}) copy-start(f32[2,1,8,8,12288]{4,3,2,1,0:T(8,128)} %param.6) | copy-start | bytes 18874372
  96.9 2.6 %copy-start.5 = (f32[128,12160]{1,0:T(8,128)}, f32[128,12160]{1,0:T(8,128)S(1)}, u32[]{:S(2)}) copy-start(f32[128,12160]{1,0:T(8,128)S(1)} %trail.1) | copy-start | bytes 18677764
  144.7 2.8 %copy-start.4 = (f32[2,1,8,8,12288]{4,3,2,1,0:T(8,128)S(1)}, f32[2,1,8,8,12288]{4,3,2,1,0:T(8,128)}, u32[]{:S(2)}) copy-start(f32[2,1,8,8,12288]{4,3,2,1,0:T(8,128)} %param.6) | copy-start | bytes 18874372
  147.5 2.8 %copy-start.6 = (f32[128,12160]{1,0:T(8,128)S(1)}, f32[128,12160]{1,0:T(8,128)}, u32[]{:S(2)}) copy-start(f32[128,12160]{1,0:T(8,128)} %all-gather.4.cloned.1.call-done.ta_ref) | copy-start | bytes 18677764
  150.3 28.3 %copy-start.8 = (f32[2,8,128,128]{3,2,1,0:T(8,128)S(1)}, f32[2,8,128,128]{3,2,1,0:T(8,128)}, u32[]{:S(2)}) copy-start(f32[2,8,128,128]{3,2,1,0:T(8,128)} %d_ref.3) | copy-start | bytes 3145732
  155.9 20.1 %all-to-all-start = ((f32[128,1,512]{2,1,0:T(1,128)}), f32[128,1,512]{2,1,0:T(1,128)S(1)}, u32[]{:S(2)}, u32[]{:S(2)}) async-start(f32[128,1,512]{2,1,0:T(1,128)} %reshape.59), calls=%async_computation | async-start | bytes 524288 | tf_op jit(solution)/shard_map/all_to_all | solution.py:149
  177.9 59.2 %copy-start.9 = (f32[2,4,12288]{2,1,0:T(4,128)S(1)}, f32[2,4,12288]{2,1,0:T(4,128)}, u32[]{:S(2)}) copy-start(f32[2,4,12288]{2,1,0:T(4,128)} %param.5) | copy-start | bytes 1179652
  178.6 3.7 %copy-start.2 = (f32[17408,128]{1,0:T(8,128)S(1)}, f32[17408,128]{1,0:T(8,128)}, u32[]{:S(2)}) copy-start(f32[17408,128]{1,0:T(8,128)} %all-gather.6.cloned.1.call-done) | copy-start | bytes 26738692
Sparse Core Ops, SparseCore 0:
  11.0 71.4 all-gather.5
  85.2 59.5 all-gather.3
  148.2 87.7 reduce-scatter.3

commit v2 on v1

v2 whole, which is shorter than its diff:
```python
import functools

import jax
import jax.numpy as jnp
from jax import lax
from jax.experimental import pallas as pl
from jax.experimental.pallas import tpu as pltpu
from jax.sharding import PartitionSpec as P

NB = 128
STEPS = 8
ROWS_AXIS = 8
COLS_AXIS = 16
PER_COL = 4
WIDTH = 8
LOCAL = 12288
TRAIL_LOCAL = 12160
SIDE = 4
TILES = 32
QUARTER = 1536
QTILES = QUARTER // NB
FIRST = (0, TRAIL_LOCAL - SIDE * QUARTER)
LIMIT = 8 * 2**20
MESSAGE = TILES // 2 + QTILES
F32 = jnp.float32
BF16 = jnp.bfloat16


def times_i(x):
    rows = x.shape[0]
    rolled = pltpu.roll(x.reshape(rows // 8, 8, x.shape[1]), 4, 1).reshape(x.shape)
    part = lax.broadcasted_iota(jnp.int32, x.shape, 0) % 8
    return jnp.where(part < 4, -rolled, rolled)


def dot_nn(a, b, precision=lax.Precision.HIGHEST):
    return lax.dot_general(a, b, (((1,), (0,)), ((), ())), precision=precision, preferred_element_type=F32)


def dot_nt(a, b, precision=lax.Precision.HIGHEST):
    return lax.dot_general(a, b, (((1,), (1,)), ((), ())), precision=precision, preferred_element_type=F32)


def split(x):
    high = x.astype(BF16)
    return high, (x - high.astype(F32)).astype(BF16)


def dot_split(dot, a, b):
    a_high, a_low = a
    b_high, b_low = b
    native = lax.Precision.DEFAULT
    return dot(a_high, b_high, native) + (dot(a_high, b_low, native) + dot(a_low, b_high, native))


def aligned(index, by):
    return pl.multiple_of(index, by)


def cut_kernel(distances, place_ref, f_ref, *refs):
    outs, sems = refs[-2 * len(distances) - 1 : -1], refs[-1]
    copies = []
    for half in range(2):
        for by in distances:
            i = len(copies)
            quarter = (place_ref[2 + half] + by) % SIDE
            first = aligned(NB + FIRST[half] + quarter * QUARTER, NB)
            copies.append(pltpu.make_async_copy(f_ref.at[:, pl.ds(first, QUARTER)], outs[i], sems.at[i]))
    for copy in copies:
        copy.start()
    for copy in copies:
        copy.wait()


def pack_kernel(place_ref, own_ref, one_ref, two_ref, three_ref, ta_ref, *refs):
    outs = refs[-2 * SIDE :]
    z, core = place_ref[0], place_ref[1]
    slabs = (own_ref, one_ref, two_ref, three_ref)

    def pick(chip, first):
        back = (z - chip + SIDE) % SIDE
        value = slabs[0][pl.ds(first, 8), :]
        for s in range(1, SIDE):
            value = jnp.where(back == s, slabs[s][pl.ds(first, 8), :], value)
        return value

    tiles = []
    for row in range(STEPS):
        other = jnp.where(core == row % 2, 0, 1)
        for step in range(row):
            tiles.append(pick(row // 2, aligned(other * (STEPS * WIDTH) + step * WIDTH, 8)))
    for chip in range(SIDE):
        tiles.append(pick(chip, 2 * STEPS * WIDTH))
    for half in range(2):
        for by in range(SIDE):
            out = outs[half * SIDE + by]
            for tile in range(TILES // 2):
                out[tile] = tiles[half * (TILES // 2) + tile]
            quarter = (place_ref[2 + half] + by) % SIDE
            for tile in range(QTILES):
                first = aligned(FIRST[half] + quarter * QUARTER + tile * NB, NB)
                value = ta_ref[:, pl.ds(first, NB)]
                if half == 1 and tile == 0:
                    value = jnp.where(quarter == 0, 0.0, value)
                out[TILES // 2 + tile] = value


def line_kernel(*refs):
    for half in range(2):
        for by in range(SIDE):
            refs[-2 + half][by] = refs[half * SIDE + by][...]


def repack_kernel(*refs):
    first, second, (blocks, ta_first, ta_second) = refs[:4], refs[4:8], refs[-3:]
    for dy in range(SIDE):
        for dx in range(SIDE):
            at = dy * SIDE + dx
            for half, (source, ta) in enumerate(((first[dx].at[dy], ta_first), (second[dy].at[dx], ta_second))):
                for tile in range(TILES // 2):
                    blocks[half * (TILES // 2) + tile, at] = source[tile]
                for tile in range(QTILES):
                    ta[at * 8 : at * 8 + 8, tile * NB : (tile + 1) * NB] = source[TILES // 2 + tile]


def either(core, which, mine_ref, other_ref, tile):
    return jnp.where(core == which, mine_ref[tile], other_ref[tile]).reshape(NB, NB)


def block_of(core, mine_ref, other_ref, row, step, part):
    return either(core, part, mine_ref, other_ref, row * (row - 1) // 2 + step)


def near_inverse(place_ref, d_ref, part, step):
    y, x = place_ref[2], place_ref[3]
    rows = []
    for dy in range(SIDE):
        for dx in range(SIDE):
            col = ((y - dy + SIDE) % SIDE) * SIDE + (x - dx + SIDE) % SIDE
            rows.append(d_ref[part, step, pl.ds(aligned(col * 8, 8), 8), :])
    return jnp.concatenate(rows, axis=0)


def store_parts(ref, step, value):
    for part in range(2):
        ref[part, :, step * NB : (step + 1) * NB] = value[part * PER_COL : (part + 1) * PER_COL]


def forward_kernel(place_ref, mine_ref, other_ref, d_ref, *refs):
    first_ref, second_ref, sol_ref, acc, own = refs[-5:]
    core = place_ref[1]
    for row in range(STEPS):
        acc[row] = either(core, row % 2, mine_ref, other_ref, 28 + row // 2)
    lane = lax.broadcasted_iota(jnp.int32, (NB, NB), 1)
    for step in range(STEPS):
        a = acc[step]
        left = jnp.concatenate([a, times_i(a)], axis=1)
        near = jnp.concatenate([near_inverse(place_ref, d_ref, part, step) for part in range(2)], axis=1)
        x = dot_nt(left, near)
        ix = times_i(x)
        natural = jnp.concatenate([d_ref[0, step], d_ref[1, step]], axis=1)
        store_parts(sol_ref, step, dot_nt(left[:8], natural))
        left = jnp.concatenate([x, ix], axis=1)
        for row in range(step + 1, STEPS):
            right = jnp.concatenate([block_of(core, mine_ref, other_ref, row, step, part) for part in range(2)], axis=0)
            acc[row] -= dot_nn(left, right)
        for half, apart in enumerate((SIDE * WIDTH, WIDTH)):
            for by in range(SIDE):
                at = half * SIDE + by
                mine = own[at] if step else jnp.zeros((NB, NB), F32)
                for part, value in enumerate((x, ix)):
                    to = part * STEPS + step
                    moved = pltpu.roll(value, (to * WIDTH - by * apart) % NB, 1)
                    mine = jnp.where(lane // WIDTH == to, moved, mine)
                own[at] = mine
    for by in range(SIDE):
        second_ref[:, by * NB : (by + 1) * NB] = own[SIDE + by]
        for dy in range(SIDE):
            for dx in range(SIDE):
                from_row, to_row = (dy * SIDE + dx) * 8, (dx * SIDE + dy) * 8
                first_ref[to_row : to_row + 8, by * NB : (by + 1) * NB] = own[by, from_row : from_row + 8]


def backward_kernel(place_ref, loads_ref, *refs):
    sums, (mine_ref, other_ref, d_ref, out_ref, acc) = refs[:4], refs[4:]
    core = place_ref[1]
    acc[...] = jnp.zeros_like(acc)
    for step in reversed(range(STEPS)):
        v = loads_ref[:, step * NB : (step + 1) * NB]
        v -= (sums[0][step] + sums[1][step]) + (sums[2][step] + sums[3][step])
        right = jnp.concatenate([d_ref[0, step], -d_ref[1, step]], axis=0)
        y = dot_nn(jnp.concatenate([v, times_i(v)], axis=1), right)
        if step < STEPS - 1:
            u = acc[step]
            near = [near_inverse(place_ref, d_ref, part, step) for part in range(2)]
            y -= dot_nn(jnp.concatenate([u, times_i(u)], axis=1), jnp.concatenate([near[0], -near[1]], axis=0))
        store_parts(out_ref, step, y)
        left = jnp.concatenate([y, times_i(y)], axis=1)
        for other in range(step):
            right = [block_of(core, mine_ref, other_ref, step, other, part) for part in range(2)]
            acc[other] += dot_nt(left, jnp.concatenate([right[0], -right[1]], axis=1))


def trail_kernel(*refs):
    outs = refs[-2 * SIDE :]
    for half in range(2):
        x_ref = refs[half]
        total = None
        for by in range(SIDE):
            piece = refs[2 + half * SIDE + by]
            term = dot_split(dot_nn, split(x_ref[:, by * NB : (by + 1) * NB]), split(piece[...]))
            total = term if total is None else total + term
        for by in range(SIDE):
            outs[half * SIDE + by][...] = -total[by * 32 : by * 32 + 32]


def zsum_kernel(place_ref, ta_first, ta_second, *refs):
    pieces, outs = refs[: 2 * SIDE], refs[-SIDE:]
    for half, ta_ref in enumerate((ta_first, ta_second)):
        ta = split(ta_ref[...])
        for by in range(SIDE):
            q = dot_split(dot_nt, ta, split(pieces[half * SIDE + by][...]))
            q = q - times_i(pltpu.roll(q, 64, 1))
            index = (place_ref[2 + half] - by + SIDE) % SIDE
            for dy in range(SIDE):
                part = q[dy * 32 : dy * 32 + 32, :64]
                outs[dy][index, :, half * 64 : half * 64 + 64] = part


def middle_kernel(place_ref, *refs):
    got, outs = refs[:SIDE], refs[-SIDE:]
    for dx in range(SIDE):
        rows = slice(dx * 8, dx * 8 + 8)
        for col in range(SIDE):
            values = [got[dy][col, rows, :] for dy in range(SIDE)]
            outs[dx][16 + col] = (values[0] + values[1]) + (values[2] + values[3])
            for dy in range(SIDE):
                outs[dx][((place_ref[2] + dy) % SIDE) * SIDE + col] = values[dy]


def last_kernel(place_ref, *refs):
    got, (out_ref, held) = refs[:SIDE], refs[SIDE:]
    for col in range(COLS_AXIS):
        value = (got[0][col] + got[1][col]) + (got[2][col] + got[3][col])
        held[col] = pltpu.roll(value, 64, 1)
    for dx in range(SIDE):
        for y in range(SIDE):
            held[y * SIDE + (place_ref[3] + dx) % SIDE] += got[dx][16 + y]
    lane = lax.broadcasted_iota(jnp.int32, (8, NB), 1)
    for step in range(STEPS):
        value = jnp.zeros((8, NB), F32)
        for col in range(COLS_AXIS):
            moved = pltpu.roll(held[col], ((col - step) * WIDTH) % NB, 1)
            value = jnp.where(lane // WIDTH == col, moved, value)
        out_ref[step] = value


def finish_kernel(place_ref, loads_ref, *refs):
    pieces, out_ref = refs[:-1], refs[-1]
    for half in range(2):
        for by in range(SIDE):
            quarter = (place_ref[2 + half] + by) % SIDE
            to = aligned(FIRST[half] + quarter * QUARTER, NB)
            value = pieces[half * SIDE + by][...]
            for part in range(2):
                rows = value[part * PER_COL : (part + 1) * PER_COL]
                loads = loads_ref[part, :, pl.ds(aligned(to + NB, NB), QUARTER)]
                out_ref[part, :, pl.ds(to, QUARTER)] = rows + loads


VMEM = pl.BlockSpec(memory_space=pltpu.VMEM)
SMEM = pl.BlockSpec(memory_space=pltpu.SMEM)
ANY = pl.BlockSpec(memory_space=pl.ANY)
HBM = pl.BlockSpec(memory_space=pltpu.HBM)


def call(kernel, name, shapes, args, scratch=(), after=(), far=(), us=1):
    specs = [SMEM if arg.dtype == jnp.int32 else VMEM for arg in args]
    specs = [HBM if i in far else spec for i, spec in enumerate(specs)] + [ANY] * len(after)
    args = [*args, *after]
    return pl.pallas_call(
        kernel,
        out_shape=[jax.ShapeDtypeStruct(shape, F32) for shape in shapes],
        in_specs=specs,
        out_specs=[VMEM] * len(shapes),
        scratch_shapes=list(scratch),
        compiler_params=pltpu.CompilerParams(vmem_limit_bytes=LIMIT),
        cost_estimate=pl.CostEstimate(flops=0, bytes_accessed=3_500_000 * us, transcendentals=0),
        name=name,
    )(*args)


def to_other_core(array):
    return lax.ppermute(array, "row", [(r, r ^ 1) for r in range(ROWS_AXIS)])


def up_z(array, by):
    return lax.ppermute(array, "row", [(r, (r + 2 * by) % ROWS_AXIS) for r in range(ROWS_AXIS)])


def up(array, axis, by):
    def moved(c):
        y, x = c // SIDE, c % SIDE
        return ((y + by) % SIDE) * SIDE + x if axis == "y" else y * SIDE + (x + by) % SIDE

    return lax.ppermute(array, "col", [(c, moved(c)) for c in range(COLS_AXIS)])


def to_all(pieces, axis, sign=1):
    return [pieces[0]] + [up(pieces[by], axis, sign * by) for by in (1, 2, 3)]


AXES = (("y", "x"), ("x", "y"))


def cut(place, factor, distances, after=()):
    return call(
        functools.partial(cut_kernel, distances),
        "cut",
        [(NB, QUARTER)] * 2 * len(distances),
        [place, factor],
        [pltpu.SemaphoreType.DMA((2 * len(distances),))],
        after,
        (1,),
    )


def body(load_vectors, panel_factor, diag_inverse, trail_adjoint, adjoint_loads):
    col, row = lax.axis_index("col"), lax.axis_index("row")
    place = jnp.stack([row // 2, row % 2, col // SIDE, col % SIDE]).astype(jnp.int32)
    core = row % 2
    factor = panel_factor.reshape(NB, LOCAL)
    parts = factor[:, :NB].reshape(2, STEPS * WIDTH, NB)
    keep = lax.dynamic_index_in_dim(parts, core, 0, False)
    got = to_other_core(lax.dynamic_index_in_dim(parts, 1 - core, 0, False))
    slab = jnp.concatenate([keep, got, load_vectors[:, :, :NB].reshape(8, NB)], axis=0)
    slabs = [slab] + [up_z(slab, by) for by in (1, 2, 3)]
    early = cut(place, factor, (1, 3))
    one = [up(early[2 * half], AXES[half][0], 1) for half in range(2)]
    three = [up(early[2 * half + 1], AXES[half][0], 3) for half in range(2)]
    messages = call(
        pack_kernel,
        "pack",
        [(MESSAGE, 8, NB)] * 8,
        [place, *slabs, trail_adjoint.reshape(8, TRAIL_LOCAL)],
        after=one + three,
    )
    heard = [to_all(messages[half * SIDE : half * SIDE + SIDE], AXES[half][0]) for half in range(2)]
    first_lines = call(line_kernel, "line", [(SIDE, MESSAGE, 8, NB)] * 2, heard[0] + heard[1])
    late = cut(place, factor, (0, 2), first_lines)
    two = [up(late[2 * half + 1], AXES[half][0], 2) for half in range(2)]
    pieces = [[late[2 * half], one[half], two[half], three[half]] for half in range(2)]
    lines = to_all([first_lines[0]] * SIDE, AXES[0][1]) + to_all([first_lines[1]] * SIDE, AXES[1][1])
    blocks, ta_first, ta_second = call(
        repack_kernel, "repack", [(TILES, COLS_AXIS, 8, NB)] + [(NB, QUARTER)] * 2, lines, after=two
    )
    window = (blocks, to_other_core(blocks))
    zparts = call(
        zsum_kernel,
        "zsum",
        [(SIDE, 32, NB)] * SIDE,
        [place, ta_first, ta_second, *pieces[0], *pieces[1]],
        us=3,
    )
    *trail_x, sol = call(
        forward_kernel,
        "forward",
        [(NB, SIDE * NB)] * 2 + [(2, PER_COL, STEPS * NB)],
        [place, *window, diag_inverse],
        [pltpu.VMEM((STEPS, NB, NB), F32)] * 2,
        after=[zparts[0]],
        us=6,
    )
    trail = call(trail_kernel, "trail", [(32, QUARTER)] * 2 * SIDE, [*trail_x, *pieces[0], *pieces[1]], us=3)
    zparts = call(middle_kernel, "middle", [(20, 8, NB)] * SIDE, [place, *to_all(zparts, "y", -1)], after=[trail[0]])
    (zown,) = call(
        last_kernel,
        "last",
        [(STEPS, 8, NB)],
        [place, *to_all(zparts, "x", -1)],
        [pltpu.VMEM((COLS_AXIS, 8, NB), F32)],
    )
    zchip = zown + to_other_core(zown)
    zsums = [zchip] + [up_z(zchip, by) for by in (1, 2, 3)]
    mine = lax.dynamic_slice_in_dim(adjoint_loads, col * PER_COL, PER_COL, 1).reshape(8, STEPS * NB)
    (adj,) = call(
        backward_kernel,
        "backward",
        [(2, PER_COL, STEPS * NB)],
        [place, mine, *zsums, *window, diag_inverse],
        [pltpu.VMEM((STEPS, 8, NB), F32)],
        us=6,
    )
    back = []
    for half in range(2):
        met = to_all(trail[half * SIDE : half * SIDE + SIDE], AXES[half][1], -1)
        total = (met[0] + met[1]) + (met[2] + met[3])
        back += to_all([total[by * 8 : by * 8 + 8] for by in range(SIDE)], AXES[half][0], -1)
    (residual,) = call(finish_kernel, "finish", [(2, PER_COL, TRAIL_LOCAL)], [place, load_vectors, *back])
    return sol, residual, adj


def solution(mesh):
    in_specs = (
        P(None, "col", "row"),
        P(None, "col", None, None, "row"),
        P(),
        P(None, "col", "row"),
        P(),
    )
    out_specs = (P(None, "col", None), P(None, "col", "row"), P(None, "col", None))
    return jax.shard_map(body, mesh=mesh, in_specs=in_specs, out_specs=out_specs, check_vma=False)
```

time: 246 us -> 171 us (0.70)
  waiting for transfers between devices: 175 us -> 54.9 us
  starting transfers between devices: 8.06 us -> 68.6 us
  between operations: 13.9 us -> 0.96 us
  local copies, waits for them, and re-layouts: 25.2 us -> 13.2 us
  Pallas kernels: 19.6 us -> 29.5 us
    all_gather x2 -> x0, waiting for transfers between devices: 116 us -> none  [the longest x1 70.5 us: body(): lax.all_gather(packed, ('row', 'col'))]
    ppermute x0 -> x45, starting transfers between devices: none -> 68.6 us  [the longest x36 54.8 us: up(): return lax.ppermute(array, 'col', [(c, moved(c)) for c in range(COLS_AXIS)])]
    ppermute x0 -> x45, waiting for transfers between devices: none -> 54.9 us  [the longest x36 43.5 us: up(): return lax.ppermute(array, 'col', [(c, moved(c)) for c in range(COLS_AXIS)])]
    unnamed x4 -> x0, waiting for transfers between devices: 47.1 us -> none
    all_to_all x1 -> x0, waiting for transfers between devices: 12.1 us -> none  [body(): met = lax.all_to_all(spread.reshape(128, 8, 64), ('row', 'col'), 0, 0)]
    pallas_call x4 -> x12, Pallas kernels: 19.6 us -> 29.5 us  [call(): pl.pallas_call(kernel, out_shape=[jax.ShapeDtypeStruct(shape, F32) for sh...]
    all_to_all x1 -> x0, starting transfers between devices: 7.94 us -> none  [body(): met = lax.all_to_all(spread.reshape(128, 8, 64), ('row', 'col'), 0, 0)]
    unnamed x23 -> x34, local copies, waits for them, and re-layouts: 17.8 us -> 10.5 us
  transfers between devices with their start and end apart: 4 -> 45, of which waited for: 4 -> 14; matrix products, arithmetic and copies ran while one was open for 3% -> 3% of each run, Pallas kernels for 8% -> 14%
where the time goes in v2:
time: 171 us; the launch traced here: 170 us
  starting transfers between devices  68.6 us (40%)
  waiting for transfers between devices  54.9 us (32%)
  Pallas kernels  29.5 us (17%)
  local copies, waits for them, and re-layouts  13.2 us (8%)
  other arithmetic  2.33 us (1%)
    ppermute x36, starting transfers between devices, up(): return lax.ppermute(array, 'col', [(c, moved(c)) for c in range(COLS_AXIS)])  54.8 us
    ppermute x36, waiting for transfers between devices, up(): return lax.ppermute(array, 'col', [(c, moved(c)) for c in range(COLS_AXIS)])  43.5 us
    pallas_call x12, Pallas kernels, call(): pl.pallas_call(kernel, out_shape=[jax.ShapeDtypeStruct(shape, F32) for sh...  29.5 us
    ppermute x6, starting transfers between devices, up_z(): lax.ppermute(array, 'row', [(r, (r + 2 * by) % ROWS_AXIS) for r in range(...  13.6 us
    unnamed x34, local copies, waits for them, and re-layouts  10.5 us
    ppermute x6, waiting for transfers between devices, up_z(): lax.ppermute(array, 'row', [(r, (r + 2 * by) % ROWS_AXIS) for r in range(...  10.3 us
  transfers between devices with their start and end apart: 45, of which 14 were waited for; matrix products, arithmetic and copies ran while one was open for 3% of the time, Pallas kernels for 14%

profile of v2, /device:TPU:8, one launch (start us, length us, event | category | flops | bytes accessed | tf_op | source)
XLA Modules:
  0.0 169.5 jit_solution(18238504890703952173)
XLA Ops:
  0.8 2.8 %copy-done.1 = f32[2,1,8,8,12288]{4,3,2,1,0:T(8,128)S(1)} copy-done((f32[2,1,8,8,12288]{4,3,2,1,0:T(8,128)S(1)}, f32[2,1,8,8,12288]{4,3,2,1,0:T(8,128)}, u32[]{:S(2)}) %copy-start.1) | copy-done | bytes 6291480
  3.6 2.5 %cut.2 = (f32[128,1536]{1,0:T(8,128)}, f32[128,1536]{1,0:T(8,128)}, f32[128,1536]{1,0:T(8,128)}, f32[128,1536]{1,0:T(8,128)}) custom-call(s32[4]{0:T(128)S(1)} %pad_add_fusion.place_ref, f32[128,12288]{1,0:T(8,128)S(1)} %bitcast.12), custom_call_target="tpu_custom_call" | custom-call | bytes 3500000 | tf_op jit(solution)/shard_map/cut/pallas_call | solution.py:281
  6.1 1.6 collective-permute-start.4
  7.7 1.5 collective-permute-start.5
  9.7 1.7 %collective-permute-start.7 = (f32[128,1536]{1,0:T(8,128)}, f32[128,1536]{1,0:T(8,128)}, u32[]{:S(2)}, u32[]{:S(2)}) collective-permute-start(f32[128,1536]{1,0:T(8,128)} %get-tuple-element.46), channel_id=1, source_target_pairs={{0,3},{1,0},{2,1},{3,2},{4,7},{5,4},{6,5},{7,6},{8,11},{9,8},{10,9... | collective-permute-start | bytes 2359304 | tf_op jit(solution)/shard_map/ppermute | solution.py:306
  11.4 0.8 slice.40
  12.3 1.2 collective-permute-done
  13.6 2.0 %collective-permute-start.1 = (f32[136,128]{1,0:T(8,128)S(1)}, f32[136,128]{1,0:T(8,128)S(1)}, u32[]{:S(2)}, u32[]{:S(2)}) collective-permute-start(f32[136,128]{1,0:T(8,128)S(1)} %pad_maximum_fusion.own_ref), channel_id=1, source_target_pairs={{0,32},{16,48},{32,64},{48,80},{64,96},{80,112},{96,0},{112,16},{1... | collective-permute-start | bytes 208904 | tf_op jit(solution)/shard_map/ppermute | solution.py:298
  15.5 4.6 %collective-permute-done.1.one_ref = f32[136,128]{1,0:T(8,128)S(1)} collective-permute-done((f32[136,128]{1,0:T(8,128)S(1)}, f32[136,128]{1,0:T(8,128)S(1)}, u32[]{:S(2)}, u32[]{:S(2)}) %collective-permute-start.1) | collective-permute-done | bytes 69664 | tf_op jit(solution)/shard_map/ppermute | solution.py:298
  20.2 1.6 collective-permute-start.2
  21.8 4.2 %collective-permute-done.2.two_ref = f32[136,128]{1,0:T(8,128)S(1)} collective-permute-done((f32[136,128]{1,0:T(8,128)S(1)}, f32[136,128]{1,0:T(8,128)S(1)}, u32[]{:S(2)}, u32[]{:S(2)}) %collective-permute-start.2) | collective-permute-done | bytes 69664 | tf_op jit(solution)/shard_map/ppermute | solution.py:298
  26.0 1.8 %collective-permute-start.3 = (f32[136,128]{1,0:T(8,128)S(1)}, f32[136,128]{1,0:T(8,128)}, u32[]{:S(2)}, u32[]{:S(2)}) collective-permute-start(f32[136,128]{1,0:T(8,128)S(1)} %pad_maximum_fusion.own_ref), channel_id=1, source_target_pairs={{0,96},{16,112},{32,0},{48,16},{64,32},{80,48},{96,64},{112,80},{1... | collective-permute-start | bytes 208904 | tf_op jit(solution)/shard_map/ppermute | solution.py:298
  27.8 1.1 reshape.24.ta_ref
  28.9 1.5 collective-permute-done.3.three_ref
  30.4 1.2 pack.1
  31.6 1.7 %collective-permute-start.10 = (f32[28,8,128]{2,1,0:T(8,128)S(1)}, f32[28,8,128]{2,1,0:T(8,128)S(1)}, u32[]{:S(2)}, u32[]{:S(2)}) collective-permute-start(f32[28,8,128]{2,1,0:T(8,128)S(1)} %get-tuple-element.50), channel_id=1, source_target_pairs={{0,12},{1,13},{2,14},{3,15},{4,0},{5,1},{6,2},{7,3},{8,4},{9,5},{1... | collective-permute-start | bytes 344072 | tf_op jit(solution)/shard_map/ppermute | solution.py:306
  33.6 2.7 %collective-permute-start.12 = (f32[28,8,128]{2,1,0:T(8,128)S(1)}, f32[28,8,128]{2,1,0:T(8,128)S(1)}, u32[]{:S(2)}, u32[]{:S(2)}) collective-permute-start(f32[28,8,128]{2,1,0:T(8,128)S(1)} %get-tuple-element.53), channel_id=1, source_target_pairs={{0,2},{1,3},{2,0},{3,1},{4,6},{5,7},{6,4},{7,5},{8,10},{9,11},{10,... | collective-permute-start | bytes 344072 | tf_op jit(solution)/shard_map/ppermute | solution.py:306
  36.3 1.4 collective-permute-start.13
  38.1 3.5 %collective-permute-start.9 = (f32[28,8,128]{2,1,0:T(8,128)S(1)}, f32[28,8,128]{2,1,0:T(8,128)S(1)}, u32[]{:S(2)}, u32[]{:S(2)}) collective-permute-start(f32[28,8,128]{2,1,0:T(8,128)S(1)} %get-tuple-element.49), channel_id=1, source_target_pairs={{0,8},{1,9},{2,10},{3,11},{4,12},{5,13},{6,14},{7,15},{8,0},{9,1},... | collective-permute-start | bytes 344072 | tf_op jit(solution)/shard_map/ppermute | solution.py:306
  41.7 0.9 collective-permute-done.8.refs_1_
  42.6 1.9 %collective-permute-done.9.refs_2_ = f32[28,8,128]{2,1,0:T(8,128)S(1)} collective-permute-done((f32[28,8,128]{2,1,0:T(8,128)S(1)}, f32[28,8,128]{2,1,0:T(8,128)S(1)}, u32[]{:S(2)}, u32[]{:S(2)}) %collective-permute-start.9) | collective-permute-done | bytes 114720 | tf_op jit(solution)/shard_map/ppermute | solution.py:306
  45.2 1.2 collective-permute-start.15
  46.4 2.5 %collective-permute-start.16 = (f32[4,28,8,128]{3,2,1,0:T(8,128)S(1)}, f32[4,28,8,128]{3,2,1,0:T(8,128)S(1)}, u32[]{:S(2)}, u32[]{:S(2)}) collective-permute-start(f32[4,28,8,128]{3,2,1,0:T(8,128)S(1)} %get-tuple-element.55.refs_0_), channel_id=1, source_target_pairs={{0,3},{1,0},{2,1},{3,2},{4,7},{5,4},{6,5},{7,6},{8,11},{9,8},{10,9... | collective-permute-start | bytes 1376264 | tf_op jit(solution)/shard_map/ppermute | solution.py:306
  48.9 2.8 %copy-done.2 = f32[2,1,8,8,12288]{4,3,2,1,0:T(8,128)S(1)} copy-done((f32[2,1,8,8,12288]{4,3,2,1,0:T(8,128)S(1)}, f32[2,1,8,8,12288]{4,3,2,1,0:T(8,128)}, u32[]{:S(2)}) %copy-start.2) | copy-done | bytes 6291480
  51.7 0.8 cut.3
  52.6 3.6 %collective-permute-start.20 = (f32[128,1536]{1,0:T(8,128)S(1)}, f32[128,1536]{1,0:T(8,128)S(1)}, u32[]{:S(2)}, u32[]{:S(2)}) collective-permute-start(f32[128,1536]{1,0:T(8,128)S(1)} %get-tuple-element.57), channel_id=1, source_target_pairs={{0,8},{1,9},{2,10},{3,11},{4,12},{5,13},{6,14},{7,15},{8,0},{9,1},... | collective-permute-start | bytes 2359304 | tf_op jit(solution)/shard_map/ppermute | solution.py:306
  56.1 1.8 %collective-permute-start.21 = (f32[128,1536]{1,0:T(8,128)S(1)}, f32[128,1536]{1,0:T(8,128)S(1)}, u32[]{:S(2)}, u32[]{:S(2)}) collective-permute-start(f32[128,1536]{1,0:T(8,128)S(1)} %get-tuple-element.58), channel_id=1, source_target_pairs={{0,2},{1,3},{2,0},{3,1},{4,6},{5,7},{6,4},{7,5},{8,10},{9,11},{10,... | collective-permute-start | bytes 2359304 | tf_op jit(solution)/shard_map/ppermute | solution.py:306
  58.0 22.6 %collective-permute-done.14.refs_1_ = f32[4,28,8,128]{3,2,1,0:T(8,128)S(1)} collective-permute-done((f32[4,28,8,128]{3,2,1,0:T(8,128)S(1)}, f32[4,28,8,128]{3,2,1,0:T(8,128)S(1)}, u32[]{:S(2)}, u32[]{:S(2)}) %collective-permute-start.14) | collective-permute-done | bytes 458784 | tf_op jit(solution)/shard_map/ppermute | solution.py:306
  80.6 1.0 collective-permute-start.17
  81.6 3.4 %collective-permute-start.18 = (f32[4,28,8,128]{3,2,1,0:T(8,128)S(1)}, f32[4,28,8,128]{3,2,1,0:T(8,128)S(1)}, u32[]{:S(2)}, u32[]{:S(2)}) collective-permute-start(f32[4,28,8,128]{3,2,1,0:T(8,128)S(1)} %get-tuple-element.56.refs_1_.refs_4_), channel_id=1, source_target_pairs={{0,8},{1,9},{2,10},{3,11},{4,12},{5,13},{6,14},{7,15},{8,0},{9,1},... | collective-permute-start | bytes 1376264 | tf_op jit(solution)/shard_map/ppermute | solution.py:306
  85.0 1.1 collective-permute-start.19
  86.2 3.3 %collective-permute-done.17.refs_5_ = f32[4,28,8,128]{3,2,1,0:T(8,128)S(1)} collective-permute-done((f32[4,28,8,128]{3,2,1,0:T(8,128)S(1)}, f32[4,28,8,128]{3,2,1,0:T(8,128)S(1)}, u32[]{:S(2)}, u32[]{:S(2)}) %collective-permute-start.17) | collective-permute-done | bytes 458784 | tf_op jit(solution)/shard_map/ppermute | solution.py:306
  89.4 2.3 %collective-permute-done.18.refs_6_ = f32[4,28,8,128]{3,2,1,0:T(8,128)S(1)} collective-permute-done((f32[4,28,8,128]{3,2,1,0:T(8,128)S(1)}, f32[4,28,8,128]{3,2,1,0:T(8,128)S(1)}, u32[]{:S(2)}, u32[]{:S(2)}) %collective-permute-start.18) | collective-permute-done | bytes 458784 | tf_op jit(solution)/shard_map/ppermute | solution.py:306
  91.7 4.8 %collective-permute-done.19.refs_7_ = f32[4,28,8,128]{3,2,1,0:T(8,128)S(1)} collective-permute-done((f32[4,28,8,128]{3,2,1,0:T(8,128)S(1)}, f32[4,28,8,128]{3,2,1,0:T(8,128)S(1)}, u32[]{:S(2)}, u32[]{:S(2)}) %collective-permute-start.19) | collective-permute-done | bytes 458784 | tf_op jit(solution)/shard_map/ppermute | solution.py:306
  97.0 4.0 %zsum.1 = (f32[4,32,128]{2,1,0:T(8,128)S(1)}, f32[4,32,128]{2,1,0:T(8,128)S(1)}, f32[4,32,128]{2,1,0:T(8,128)S(1)}, f32[4,32,128]{2,1,0:T(8,128)S(1)}) custom-call(s32[4]{0:T(128)S(1)} %pad_add_fusion.place_ref, f32[128,1536]{1,0:T(8,128)S(1)} %get-tuple-element.60.ta_first, f32[128,1536]{1,0:T(8,128)S(1)} %get-tuple-element.61.ta_second, ...), custom_call_target="tpu_custom_call" | custom-call | bytes 10500000 | tf_op jit(solution)/shard_map/zsum/pallas_call | solution.py:281
  101.0 2.1 %collective-permute-start.35 = (f32[4,32,128]{2,1,0:T(8,128)S(1)}, f32[4,32,128]{2,1,0:T(8,128)S(1)}, u32[]{:S(2)}, u32[]{:S(2)}) collective-permute-start(f32[4,32,128]{2,1,0:T(8,128)S(1)} %get-tuple-element.76), channel_id=1, source_target_pairs={{0,12},{1,13},{2,14},{3,15},{4,0},{5,1},{6,2},{7,3},{8,4},{9,5},{1... | collective-permute-start | bytes 196616 | tf_op jit(solution)/shard_map/ppermute | solution.py:306
  103.1 1.5 collective-permute-start.36
  104.6 2.4 %collective-permute-start.37 = (f32[4,32,128]{2,1,0:T(8,128)S(1)}, f32[4,32,128]{2,1,0:T(8,128)S(1)}, u32[]{:S(2)}, u32[]{:S(2)}) collective-permute-start(f32[4,32,128]{2,1,0:T(8,128)S(1)} %get-tuple-element.78), channel_id=1, source_target_pairs={{0,4},{1,5},{2,6},{3,7},{4,8},{5,9},{6,10},{7,11},{8,12},{9,13},{1... | collective-permute-start | bytes 196616 | tf_op jit(solution)/shard_map/ppermute | solution.py:306
  107.0 6.8 %forward.1 = (f32[128,512]{1,0:T(8,128)S(1)}, f32[128,512]{1,0:T(8,128)S(1)}, f32[2,4,1024]{2,1,0:T(4,128)}) custom-call(s32[4]{0:T(128)S(1)} %pad_add_fusion.place_ref, f32[32,16,8,128]{3,2,1,0:T(8,128)S(1)} %get-tuple-element.59.mine_ref.refs_4_, f32[32,16,8,128]{3,2,1,0:T(8,128)S(1)} %collective-permute-done.22.other_ref.refs_5_, ...), custom_call_target="tpu_custom_call" | custom-call | bytes 21000000 | tf_op jit(solution)/shard_map/forward/pallas_call | solution.py:281
  113.8 4.5 %trail.1 = (f32[32,1536]{1,0:T(8,128)S(1)}, f32[32,1536]{1,0:T(8,128)S(1)}, f32[32,1536]{1,0:T(8,128)S(1)}, f32[32,1536]{1,0:T(8,128)S(1)}, f32[32,1536]{1,0:T(8...) custom-call(f32[128,512]{1,0:T(8,128)S(1)} %get-tuple-element.66.refs_0_, ...), custom_call_target="tpu_custom_call" | custom-call | bytes 10500000 | tf_op jit(solution)/shard_map/trail/pallas_call | solution.py:281
  121.0 1.7 collective-permute-start.30
  122.7 1.6 collective-permute-start.31
  124.2 1.2 collective-permute-done.38.refs_1_
  125.4 0.8 collective-permute-start.40
  126.3 4.6 %collective-permute-done.39.refs_2_ = f32[20,8,128]{2,1,0:T(8,128)S(1)} collective-permute-done((f32[20,8,128]{2,1,0:T(8,128)S(1)}, f32[20,8,128]{2,1,0:T(8,128)S(1)}, u32[]{:S(2)}, u32[]{:S(2)}) %collective-permute-start.39) | collective-permute-done | bytes 81952 | tf_op jit(solution)/shard_map/ppermute | solution.py:306
  131.6 0.8 last.1
  132.5 1.9 %collective-permute-start.23 = (f32[32,1536]{1,0:T(8,128)}, f32[32,1536]{1,0:T(8,128)S(1)}, u32[]{:S(2)}, u32[]{:S(2)}) collective-permute-start(f32[32,1536]{1,0:T(8,128)} %copy-done.16), channel_id=1, source_target_pairs={{0,3},{1,0},{2,1},{3,2},{4,7},{5,4},{6,5},{7,6},{8,11},{9,8},{10,9... | collective-permute-start | bytes 589832 | tf_op jit(solution)/shard_map/ppermute | solution.py:306
  134.4 0.9 collective-permute-start.24
  135.3 1.2 collective-permute-start.25
  136.5 1.2 collective-permute-start.42
  137.7 3.6 %collective-permute-start.43 = (f32[8,8,128]{2,1,0:T(8,128)S(1)}, f32[8,8,128]{2,1,0:T(8,128)S(1)}, u32[]{:S(2)}, u32[]{:S(2)}) collective-permute-start(f32[8,8,128]{2,1,0:T(8,128)S(1)} %add.53.refs_0_), channel_id=1, source_target_pairs={{0,64},{16,80},{32,96},{48,112},{64,0},{80,16},{96,32},{112,48},{1... | collective-permute-start | bytes 98312 | tf_op jit(solution)/shard_map/ppermute | solution.py:298
  141.3 1.3 add_add_fusion
  142.5 1.2 collective-permute-done.23
  143.7 3.3 %collective-permute-start.44 = (f32[8,8,128]{2,1,0:T(8,128)S(1)}, f32[8,8,128]{2,1,0:T(8,128)S(1)}, u32[]{:S(2)}, u32[]{:S(2)}) collective-permute-start(f32[8,8,128]{2,1,0:T(8,128)S(1)} %add.53.refs_0_), channel_id=1, source_target_pairs={{0,96},{16,112},{32,0},{48,16},{64,32},{80,48},{96,64},{112,80},{1... | collective-permute-start | bytes 98312 | tf_op jit(solution)/shard_map/ppermute | solution.py:298
  147.1 3.6 %collective-permute-start.32 = (f32[8,1536]{1,0:T(8,128)S(1)}, f32[8,1536]{1,0:T(8,128)S(1)}, u32[]{:S(2)}, u32[]{:S(2)}) collective-permute-start(f32[8,1536]{1,0:T(8,128)S(1)} %get-tuple-element.85), channel_id=1, source_target_pairs={{0,3},{1,0},{2,1},{3,2},{4,7},{5,4},{6,5},{7,6},{8,11},{9,8},{10,9... | collective-permute-start | bytes 147464 | tf_op jit(solution)/shard_map/ppermute | solution.py:306
  150.6 1.0 add_add_fusion.1
  152.2 0.9 collective-permute-start.34
  153.2 0.9 collective-permute-start.26
  154.1 2.1 %collective-permute-start.27 = (f32[8,1536]{1,0:T(8,128)}, f32[8,1536]{1,0:T(8,128)S(1)}, u32[]{:S(2)}, u32[]{:S(2)}) collective-permute-start(f32[8,1536]{1,0:T(8,128)} %get-tuple-element.88), channel_id=1, source_target_pairs={{0,8},{1,9},{2,10},{3,11},{4,12},{5,13},{6,14},{7,15},{8,0},{9,1},... | collective-permute-start | bytes 147464 | tf_op jit(solution)/shard_map/ppermute | solution.py:306
  156.2 2.5 %collective-permute-start.28 = (f32[8,1536]{1,0:T(8,128)}, f32[8,1536]{1,0:T(8,128)S(1)}, u32[]{:S(2)}, u32[]{:S(2)}) collective-permute-start(f32[8,1536]{1,0:T(8,128)} %get-tuple-element.87), channel_id=1, source_target_pairs={{0,4},{1,5},{2,6},{3,7},{4,8},{5,9},{6,10},{7,11},{8,12},{9,13},{1... | collective-permute-start | bytes 147464 | tf_op jit(solution)/shard_map/ppermute | solution.py:306
  158.8 1.6 copy-done.4
  160.4 1.2 copy-done.10
  161.6 6.5 %backward.1 = f32[2,4,1024]{2,1,0:T(4,128)} custom-call(s32[4]{0:T(128)S(1)} %pad_add_fusion.place_ref, f32[8,1024]{1,0:T(8,128)S(1)} %reshape.25.loads_ref, f32[8,8,128]{2,1,0:T(8,128)S(1)} %add.53.refs_0_, f32[8,8,128]{2,1,0:T(8,128)S(1)} %collective-permute-done.42.refs_1_, f32[8,8,128]{2,1,0:T(8,128)S(1)} %collective-permute-done.43.refs_2_, ...), custom_call_target="tpu_custom_call" | custom-call | bytes 21000000 | tf_op jit(solution)/shard_map/backward/pallas_call | solution.py:281
  168.2 1.4 finish.1
  (86 shorter events, 6.7 us)
Async XLA Ops:
  0.6 158.1 %copy-start = (f32[2,64,1024]{2,1,0:T(8,128)S(1)}, f32[2,64,1024]{2,1,0:T(8,128)}, u32[]{:S(2)}) copy-start(f32[2,64,1024]{2,1,0:T(8,128)} %param.9) | copy-start | bytes 1572868
  0.8 2.8 %copy-start.1 = (f32[2,1,8,8,12288]{4,3,2,1,0:T(8,128)S(1)}, f32[2,1,8,8,12288]{4,3,2,1,0:T(8,128)}, u32[]{:S(2)}) copy-start(f32[2,1,8,8,12288]{4,3,2,1,0:T(8,128)} %param.6) | copy-start | bytes 18874372
  3.6 10.0 %slice-start = ((f32[2,4,12288]{2,1,0:T(4,128)}), f32[2,4,128]{2,1,0:T(4,128)S(1)}, s32[]{:S(2)}) async-start(f32[2,4,12288]{2,1,0:T(4,128)} %loads_ref.1), calls=%async_computation | async-start | bytes 8192 | tf_op jit(solution)/shard_map/slice | solution.py:336
  6.1 24.3 %collective-permute-start.4 = (f32[128,1536]{1,0:T(8,128)}, f32[128,1536]{1,0:T(8,128)S(1)}, u32[]{:S(2)}, u32[]{:S(2)}) collective-permute-start(f32[128,1536]{1,0:T(8,128)} %get-tuple-element.43), channel_id=1, source_target_pairs={{0,4},{1,5},{2,6},{3,7},{4,8},{5,9},{6,10},{7,11},{8,12},{9,13},{1... | collective-permute-start | bytes 2359304 | tf_op jit(solution)/shard_map/ppermute | solution.py:306
  7.7 22.7 %collective-permute-start.5 = (f32[128,1536]{1,0:T(8,128)}, f32[128,1536]{1,0:T(8,128)S(1)}, u32[]{:S(2)}, u32[]{:S(2)}) collective-permute-start(f32[128,1536]{1,0:T(8,128)} %get-tuple-element.44), channel_id=1, source_target_pairs={{0,1},{1,2},{2,3},{3,0},{4,5},{5,6},{6,7},{7,4},{8,9},{9,10},{10,1... | collective-permute-start | bytes 2359304 | tf_op jit(solution)/shard_map/ppermute | solution.py:306
  9.2 21.2 %collective-permute-start.6 = (f32[128,1536]{1,0:T(8,128)}, f32[128,1536]{1,0:T(8,128)S(1)}, u32[]{:S(2)}, u32[]{:S(2)}) collective-permute-start(f32[128,1536]{1,0:T(8,128)} %get-tuple-element.45), channel_id=1, source_target_pairs={{0,12},{1,13},{2,14},{3,15},{4,0},{5,1},{6,2},{7,3},{8,4},{9,5},{1... | collective-permute-start | bytes 2359304 | tf_op jit(solution)/shard_map/ppermute | solution.py:306
  9.7 20.8 %collective-permute-start.7 = (f32[128,1536]{1,0:T(8,128)}, f32[128,1536]{1,0:T(8,128)}, u32[]{:S(2)}, u32[]{:S(2)}) collective-permute-start(f32[128,1536]{1,0:T(8,128)} %get-tuple-element.46), channel_id=1, source_target_pairs={{0,3},{1,0},{2,1},{3,2},{4,7},{5,4},{6,5},{7,6},{8,11},{9,8},{10,9... | collective-permute-start | bytes 2359304 | tf_op jit(solution)/shard_map/ppermute | solution.py:306
  12.2 1.3 collective-permute-start
  13.6 6.6 %collective-permute-start.1 = (f32[136,128]{1,0:T(8,128)S(1)}, f32[136,128]{1,0:T(8,128)S(1)}, u32[]{:S(2)}, u32[]{:S(2)}) collective-permute-start(f32[136,128]{1,0:T(8,128)S(1)} %pad_maximum_fusion.own_ref), channel_id=1, source_target_pairs={{0,32},{16,48},{32,64},{48,80},{64,96},{80,112},{96,0},{112,16},{1... | collective-permute-start | bytes 208904 | tf_op jit(solution)/shard_map/ppermute | solution.py:298
  20.2 5.8 %collective-permute-start.2 = (f32[136,128]{1,0:T(8,128)S(1)}, f32[136,128]{1,0:T(8,128)S(1)}, u32[]{:S(2)}, u32[]{:S(2)}) collective-permute-start(f32[136,128]{1,0:T(8,128)S(1)} %pad_maximum_fusion.own_ref), channel_id=1, source_target_pairs={{0,64},{16,80},{32,96},{48,112},{64,0},{80,16},{96,32},{112,48},{1... | collective-permute-start | bytes 208904 | tf_op jit(solution)/shard_map/ppermute | solution.py:298
  26.0 4.4 %collective-permute-start.3 = (f32[136,128]{1,0:T(8,128)S(1)}, f32[136,128]{1,0:T(8,128)}, u32[]{:S(2)}, u32[]{:S(2)}) collective-permute-start(f32[136,128]{1,0:T(8,128)S(1)} %pad_maximum_fusion.own_ref), channel_id=1, source_target_pairs={{0,96},{16,112},{32,0},{48,16},{64,32},{80,48},{96,64},{112,80},{1... | collective-permute-start | bytes 208904 | tf_op jit(solution)/shard_map/ppermute | solution.py:298
  30.4 14.1 %copy-start.5 = (f32[128,1536]{1,0:T(8,128)}, f32[128,1536]{1,0:T(8,128)S(1)}, u32[]{:S(2)}) copy-start(f32[128,1536]{1,0:T(8,128)S(1)} %collective-permute-done.5.refs_1_.refs_5_.refs_7_) | copy-start | bytes 2359300
  30.4 14.1 %copy-start.7 = (f32[128,1536]{1,0:T(8,128)}, f32[128,1536]{1,0:T(8,128)S(1)}, u32[]{:S(2)}) copy-start(f32[128,1536]{1,0:T(8,128)S(1)} %collective-permute-done.6.refs_2_.refs_3_.refs_5_) | copy-start | bytes 2359300
  31.6 6.5 %collective-permute-start.10 = (f32[28,8,128]{2,1,0:T(8,128)S(1)}, f32[28,8,128]{2,1,0:T(8,128)S(1)}, u32[]{:S(2)}, u32[]{:S(2)}) collective-permute-start(f32[28,8,128]{2,1,0:T(8,128)S(1)} %get-tuple-element.50), channel_id=1, source_target_pairs={{0,12},{1,13},{2,14},{3,15},{4,0},{5,1},{6,2},{7,3},{8,4},{9,5},{1... | collective-permute-start | bytes 344072 | tf_op jit(solution)/shard_map/ppermute | solution.py:306
  33.3 8.3 %collective-permute-start.11 = (f32[28,8,128]{2,1,0:T(8,128)S(1)}, f32[28,8,128]{2,1,0:T(8,128)S(1)}, u32[]{:S(2)}, u32[]{:S(2)}) collective-permute-start(f32[28,8,128]{2,1,0:T(8,128)S(1)} %get-tuple-element.52), channel_id=1, source_target_pairs={{0,1},{1,2},{2,3},{3,0},{4,5},{5,6},{6,7},{7,4},{8,9},{9,10},{10,1... | collective-permute-start | bytes 344072 | tf_op jit(solution)/shard_map/ppermute | solution.py:306
  33.6 8.0 %collective-permute-start.12 = (f32[28,8,128]{2,1,0:T(8,128)S(1)}, f32[28,8,128]{2,1,0:T(8,128)S(1)}, u32[]{:S(2)}, u32[]{:S(2)}) collective-permute-start(f32[28,8,128]{2,1,0:T(8,128)S(1)} %get-tuple-element.53), channel_id=1, source_target_pairs={{0,2},{1,3},{2,0},{3,1},{4,6},{5,7},{6,4},{7,5},{8,10},{9,11},{10,... | collective-permute-start | bytes 344072 | tf_op jit(solution)/shard_map/ppermute | solution.py:306
  36.3 5.3 %collective-permute-start.13 = (f32[28,8,128]{2,1,0:T(8,128)S(1)}, f32[28,8,128]{2,1,0:T(8,128)S(1)}, u32[]{:S(2)}, u32[]{:S(2)}) collective-permute-start(f32[28,8,128]{2,1,0:T(8,128)S(1)} %get-tuple-element.54), channel_id=1, source_target_pairs={{0,3},{1,0},{2,1},{3,2},{4,7},{5,4},{6,5},{7,6},{8,11},{9,8},{10,9... | collective-permute-start | bytes 344072 | tf_op jit(solution)/shard_map/ppermute | solution.py:306
  37.8 4.8 %collective-permute-start.8 = (f32[28,8,128]{2,1,0:T(8,128)S(1)}, f32[28,8,128]{2,1,0:T(8,128)S(1)}, u32[]{:S(2)}, u32[]{:S(2)}) collective-permute-start(f32[28,8,128]{2,1,0:T(8,128)S(1)} %get-tuple-element.48), channel_id=1, source_target_pairs={{0,4},{1,5},{2,6},{3,7},{4,8},{5,9},{6,10},{7,11},{8,12},{9,13},{1... | collective-permute-start | bytes 344072 | tf_op jit(solution)/shard_map/ppermute | solution.py:306
  38.1 6.3 %collective-permute-start.9 = (f32[28,8,128]{2,1,0:T(8,128)S(1)}, f32[28,8,128]{2,1,0:T(8,128)S(1)}, u32[]{:S(2)}, u32[]{:S(2)}) collective-permute-start(f32[28,8,128]{2,1,0:T(8,128)S(1)} %get-tuple-element.49), channel_id=1, source_target_pairs={{0,8},{1,9},{2,10},{3,11},{4,12},{5,13},{6,14},{7,15},{8,0},{9,1},... | collective-permute-start | bytes 344072 | tf_op jit(solution)/shard_map/ppermute | solution.py:306
  44.5 36.0 %collective-permute-start.14 = (f32[4,28,8,128]{3,2,1,0:T(8,128)S(1)}, f32[4,28,8,128]{3,2,1,0:T(8,128)S(1)}, u32[]{:S(2)}, u32[]{:S(2)}) collective-permute-start(f32[4,28,8,128]{3,2,1,0:T(8,128)S(1)} %get-tuple-element.55.refs_0_), channel_id=1, source_target_pairs={{0,1},{1,2},{2,3},{3,0},{4,5},{5,6},{6,7},{7,4},{8,9},{9,10},{10,1... | collective-permute-start | bytes 1376264 | tf_op jit(solution)/shard_map/ppermute | solution.py:306
  45.2 36.4 %collective-permute-start.15 = (f32[4,28,8,128]{3,2,1,0:T(8,128)S(1)}, f32[4,28,8,128]{3,2,1,0:T(8,128)S(1)}, u32[]{:S(2)}, u32[]{:S(2)}) collective-permute-start(f32[4,28,8,128]{3,2,1,0:T(8,128)S(1)} %get-tuple-element.55.refs_0_), channel_id=1, source_target_pairs={{0,2},{1,3},{2,0},{3,1},{4,6},{5,7},{6,4},{7,5},{8,10},{9,11},{10,... | collective-permute-start | bytes 1376264 | tf_op jit(solution)/shard_map/ppermute | solution.py:306
  46.4 38.6 %collective-permute-start.16 = (f32[4,28,8,128]{3,2,1,0:T(8,128)S(1)}, f32[4,28,8,128]{3,2,1,0:T(8,128)S(1)}, u32[]{:S(2)}, u32[]{:S(2)}) collective-permute-start(f32[4,28,8,128]{3,2,1,0:T(8,128)S(1)} %get-tuple-element.55.refs_0_), channel_id=1, source_target_pairs={{0,3},{1,0},{2,1},{3,2},{4,7},{5,4},{6,5},{7,6},{8,11},{9,8},{10,9... | collective-permute-start | bytes 1376264 | tf_op jit(solution)/shard_map/ppermute | solution.py:306
  48.9 2.8 %copy-start.2 = (f32[2,1,8,8,12288]{4,3,2,1,0:T(8,128)S(1)}, f32[2,1,8,8,12288]{4,3,2,1,0:T(8,128)}, u32[]{:S(2)}) copy-start(f32[2,1,8,8,12288]{4,3,2,1,0:T(8,128)} %param.6) | copy-start | bytes 18874372
  52.6 43.9 %collective-permute-start.20 = (f32[128,1536]{1,0:T(8,128)S(1)}, f32[128,1536]{1,0:T(8,128)S(1)}, u32[]{:S(2)}, u32[]{:S(2)}) collective-permute-start(f32[128,1536]{1,0:T(8,128)S(1)} %get-tuple-element.57), channel_id=1, source_target_pairs={{0,8},{1,9},{2,10},{3,11},{4,12},{5,13},{6,14},{7,15},{8,0},{9,1},... | collective-permute-start | bytes 2359304 | tf_op jit(solution)/shard_map/ppermute | solution.py:306
  56.1 40.8 %copy-start.6 = (f32[128,1536]{1,0:T(8,128)S(1)}, f32[128,1536]{1,0:T(8,128)}, u32[]{:S(2)}) copy-start(f32[128,1536]{1,0:T(8,128)} %copy-done.5) | copy-start | bytes 2359300
  56.1 40.8 %copy-start.8 = (f32[128,1536]{1,0:T(8,128)S(1)}, f32[128,1536]{1,0:T(8,128)}, u32[]{:S(2)}) copy-start(f32[128,1536]{1,0:T(8,128)} %copy-done.7) | copy-start | bytes 2359300
  56.1 40.4 %collective-permute-start.21 = (f32[128,1536]{1,0:T(8,128)S(1)}, f32[128,1536]{1,0:T(8,128)S(1)}, u32[]{:S(2)}, u32[]{:S(2)}) collective-permute-start(f32[128,1536]{1,0:T(8,128)S(1)} %get-tuple-element.58), channel_id=1, source_target_pairs={{0,2},{1,3},{2,0},{3,1},{4,6},{5,7},{6,4},{7,5},{8,10},{9,11},{10,... | collective-permute-start | bytes 2359304 | tf_op jit(solution)/shard_map/ppermute | solution.py:306
  80.6 8.8 %collective-permute-start.17 = (f32[4,28,8,128]{3,2,1,0:T(8,128)S(1)}, f32[4,28,8,128]{3,2,1,0:T(8,128)S(1)}, u32[]{:S(2)}, u32[]{:S(2)}) collective-permute-start(f32[4,28,8,128]{3,2,1,0:T(8,128)S(1)} %get-tuple-element.56.refs_1_.refs_4_), channel_id=1, source_target_pairs={{0,4},{1,5},{2,6},{3,7},{4,8},{5,9},{6,10},{7,11},{8,12},{9,13},{1... | collective-permute-start | bytes 1376264 | tf_op jit(solution)/shard_map/ppermute | solution.py:306
  81.6 10.1 %collective-permute-start.18 = (f32[4,28,8,128]{3,2,1,0:T(8,128)S(1)}, f32[4,28,8,128]{3,2,1,0:T(8,128)S(1)}, u32[]{:S(2)}, u32[]{:S(2)}) collective-permute-start(f32[4,28,8,128]{3,2,1,0:T(8,128)S(1)} %get-tuple-element.56.refs_1_.refs_4_), channel_id=1, source_target_pairs={{0,8},{1,9},{2,10},{3,11},{4,12},{5,13},{6,14},{7,15},{8,0},{9,1},... | collective-permute-start | bytes 1376264 | tf_op jit(solution)/shard_map/ppermute | solution.py:306
  85.0 11.5 %collective-permute-start.19 = (f32[4,28,8,128]{3,2,1,0:T(8,128)S(1)}, f32[4,28,8,128]{3,2,1,0:T(8,128)S(1)}, u32[]{:S(2)}, u32[]{:S(2)}) collective-permute-start(f32[4,28,8,128]{3,2,1,0:T(8,128)S(1)} %get-tuple-element.56.refs_1_.refs_4_), channel_id=1, source_target_pairs={{0,12},{1,13},{2,14},{3,15},{4,0},{5,1},{6,2},{7,3},{8,4},{9,5},{1... | collective-permute-start | bytes 1376264 | tf_op jit(solution)/shard_map/ppermute | solution.py:306
  96.9 10.1 %collective-permute-start.22 = (f32[32,16,8,128]{3,2,1,0:T(8,128)S(1)}, f32[32,16,8,128]{3,2,1,0:T(8,128)S(1)}, u32[]{:S(2)}, u32[]{:S(2)}) collective-permute-start(f32[32,16,8,128]{3,2,1,0:T(8,128)S(1)} %get-tuple-element.59.mine_ref.refs_4_), channel_id=1, source_target_pairs={{0,16},{16,0},{32,48},{48,32},{64,80},{80,64},{96,112},{112,96},{1... | collective-permute-start | bytes 6291464 | tf_op jit(solution)/shard_map/ppermute | solution.py:294
  97.0 10.0 %copy-start.9 = (f32[2,8,128,128]{3,2,1,0:T(8,128)S(1)}, f32[2,8,128,128]{3,2,1,0:T(8,128)}, u32[]{:S(2)}) copy-start(f32[2,8,128,128]{3,2,1,0:T(8,128)} %refs_6_.1) | copy-start | bytes 3145732
  101.0 18.6 %collective-permute-start.35 = (f32[4,32,128]{2,1,0:T(8,128)S(1)}, f32[4,32,128]{2,1,0:T(8,128)S(1)}, u32[]{:S(2)}, u32[]{:S(2)}) collective-permute-start(f32[4,32,128]{2,1,0:T(8,128)S(1)} %get-tuple-element.76), channel_id=1, source_target_pairs={{0,12},{1,13},{2,14},{3,15},{4,0},{5,1},{6,2},{7,3},{8,4},{9,5},{1... | collective-permute-start | bytes 196616 | tf_op jit(solution)/shard_map/ppermute | solution.py:306
  103.1 16.6 %collective-permute-start.36 = (f32[4,32,128]{2,1,0:T(8,128)S(1)}, f32[4,32,128]{2,1,0:T(8,128)S(1)}, u32[]{:S(2)}, u32[]{:S(2)}) collective-permute-start(f32[4,32,128]{2,1,0:T(8,128)S(1)} %get-tuple-element.77), channel_id=1, source_target_pairs={{0,8},{1,9},{2,10},{3,11},{4,12},{5,13},{6,14},{7,15},{8,0},{9,1},... | collective-permute-start | bytes 196616 | tf_op jit(solution)/shard_map/ppermute | solution.py:306
  104.6 15.1 %collective-permute-start.37 = (f32[4,32,128]{2,1,0:T(8,128)S(1)}, f32[4,32,128]{2,1,0:T(8,128)S(1)}, u32[]{:S(2)}, u32[]{:S(2)}) collective-permute-start(f32[4,32,128]{2,1,0:T(8,128)S(1)} %get-tuple-element.78), channel_id=1, source_target_pairs={{0,4},{1,5},{2,6},{3,7},{4,8},{5,9},{6,10},{7,11},{8,12},{9,13},{1... | collective-permute-start | bytes 196616 | tf_op jit(solution)/shard_map/ppermute | solution.py:306
  107.0 6.8 %copy-start.3 = (f32[32,16,8,128]{3,2,1,0:T(8,128)}, f32[32,16,8,128]{3,2,1,0:T(8,128)S(1)}, u32[]{:S(2)}) copy-start(f32[32,16,8,128]{3,2,1,0:T(8,128)S(1)} %collective-permute-done.22.other_ref.refs_5_) | copy-start | bytes 6291460
  118.3 0.7 copy-start.15
  119.0 0.7 copy-start.16
  119.6 0.7 copy-start.13
  119.6 12.8 %copy-start.14 = (f32[32,1536]{1,0:T(8,128)}, f32[32,1536]{1,0:T(8,128)S(1)}, u32[]{:S(2)}) copy-start(f32[32,1536]{1,0:T(8,128)S(1)} %get-tuple-element.71) | copy-start | bytes 589828
  120.3 0.7 copy-start.11
  121.0 4.4 %collective-permute-start.38 = (f32[20,8,128]{2,1,0:T(8,128)S(1)}, f32[20,8,128]{2,1,0:T(8,128)S(1)}, u32[]{:S(2)}, u32[]{:S(2)}) collective-permute-start(f32[20,8,128]{2,1,0:T(8,128)S(1)} %get-tuple-element.80), channel_id=1, source_target_pairs={{0,3},{1,0},{2,1},{3,2},{4,7},{5,4},{6,5},{7,6},{8,11},{9,8},{10,9... | collective-permute-start | bytes 245768 | tf_op jit(solution)/shard_map/ppermute | solution.py:306
  121.0 14.3 %collective-permute-start.29 = (f32[32,1536]{1,0:T(8,128)}, f32[32,1536]{1,0:T(8,128)}, u32[]{:S(2)}, u32[]{:S(2)}) collective-permute-start(f32[32,1536]{1,0:T(8,128)} %get-tuple-element.73), channel_id=1, source_target_pairs={{0,12},{1,13},{2,14},{3,15},{4,0},{5,1},{6,2},{7,3},{8,4},{9,5},{1... | collective-permute-start | bytes 589832 | tf_op jit(solution)/shard_map/ppermute | solution.py:306
  121.0 15.5 %collective-permute-start.30 = (f32[32,1536]{1,0:T(8,128)}, f32[32,1536]{1,0:T(8,128)}, u32[]{:S(2)}, u32[]{:S(2)}) collective-permute-start(f32[32,1536]{1,0:T(8,128)} %get-tuple-element.74), channel_id=1, source_target_pairs={{0,8},{1,9},{2,10},{3,11},{4,12},{5,13},{6,14},{7,15},{8,0},{9,1},... | collective-permute-start | bytes 589832 | tf_op jit(solution)/shard_map/ppermute | solution.py:306
  122.7 15.0 %collective-permute-start.31 = (f32[32,1536]{1,0:T(8,128)}, f32[32,1536]{1,0:T(8,128)}, u32[]{:S(2)}, u32[]{:S(2)}) collective-permute-start(f32[32,1536]{1,0:T(8,128)} %get-tuple-element.75), channel_id=1, source_target_pairs={{0,4},{1,5},{2,6},{3,7},{4,8},{5,9},{6,10},{7,11},{8,12},{9,13},{1... | collective-permute-start | bytes 589832 | tf_op jit(solution)/shard_map/ppermute | solution.py:306
  124.2 6.7 %collective-permute-start.39 = (f32[20,8,128]{2,1,0:T(8,128)S(1)}, f32[20,8,128]{2,1,0:T(8,128)S(1)}, u32[]{:S(2)}, u32[]{:S(2)}) collective-permute-start(f32[20,8,128]{2,1,0:T(8,128)S(1)} %get-tuple-element.81), channel_id=1, source_target_pairs={{0,2},{1,3},{2,0},{3,1},{4,6},{5,7},{6,4},{7,5},{8,10},{9,11},{10,... | collective-permute-start | bytes 245768 | tf_op jit(solution)/shard_map/ppermute | solution.py:306
  125.4 6.1 %collective-permute-start.40 = (f32[20,8,128]{2,1,0:T(8,128)S(1)}, f32[20,8,128]{2,1,0:T(8,128)S(1)}, u32[]{:S(2)}, u32[]{:S(2)}) collective-permute-start(f32[20,8,128]{2,1,0:T(8,128)S(1)} %get-tuple-element.82), channel_id=1, source_target_pairs={{0,1},{1,2},{2,3},{3,0},{4,5},{5,6},{6,7},{7,4},{8,9},{9,10},{10,1... | collective-permute-start | bytes 245768 | tf_op jit(solution)/shard_map/ppermute | solution.py:306
  132.4 2.0 %collective-permute-start.41 = (f32[8,8,128]{2,1,0:T(8,128)S(1)}, f32[8,8,128]{2,1,0:T(8,128)S(1)}, u32[]{:S(2)}, u32[]{:S(2)}) collective-permute-start(f32[8,8,128]{2,1,0:T(8,128)S(1)} %last.1), channel_id=1, source_target_pairs={{0,16},{16,0},{32,48},{48,32},{64,80},{80,64},{96,112},{112,96},{1... | collective-permute-start | bytes 98312 | tf_op jit(solution)/shard_map/ppermute | solution.py:294
  132.5 11.2 %collective-permute-start.23 = (f32[32,1536]{1,0:T(8,128)}, f32[32,1536]{1,0:T(8,128)S(1)}, u32[]{:S(2)}, u32[]{:S(2)}) collective-permute-start(f32[32,1536]{1,0:T(8,128)} %copy-done.16), channel_id=1, source_target_pairs={{0,3},{1,0},{2,1},{3,2},{4,7},{5,4},{6,5},{7,6},{8,11},{9,8},{10,9... | collective-permute-start | bytes 589832 | tf_op jit(solution)/shard_map/ppermute | solution.py:306
  134.4 12.7 %collective-permute-start.24 = (f32[32,1536]{1,0:T(8,128)}, f32[32,1536]{1,0:T(8,128)S(1)}, u32[]{:S(2)}, u32[]{:S(2)}) collective-permute-start(f32[32,1536]{1,0:T(8,128)} %copy-done.15), channel_id=1, source_target_pairs={{0,2},{1,3},{2,0},{3,1},{4,6},{5,7},{6,4},{7,5},{8,10},{9,11},{10,... | collective-permute-start | bytes 589832 | tf_op jit(solution)/shard_map/ppermute | solution.py:306
  135.3 15.3 %collective-permute-start.25 = (f32[32,1536]{1,0:T(8,128)}, f32[32,1536]{1,0:T(8,128)S(1)}, u32[]{:S(2)}, u32[]{:S(2)}) collective-permute-start(f32[32,1536]{1,0:T(8,128)} %copy-done.14), channel_id=1, source_target_pairs={{0,1},{1,2},{2,3},{3,0},{4,5},{5,6},{6,7},{7,4},{8,9},{9,10},{10,1... | collective-permute-start | bytes 589832 | tf_op jit(solution)/shard_map/ppermute | solution.py:306
  136.5 15.8 %collective-permute-start.42 = (f32[8,8,128]{2,1,0:T(8,128)S(1)}, f32[8,8,128]{2,1,0:T(8,128)S(1)}, u32[]{:S(2)}, u32[]{:S(2)}) collective-permute-start(f32[8,8,128]{2,1,0:T(8,128)S(1)} %add.53.refs_0_), channel_id=1, source_target_pairs={{0,32},{16,48},{32,64},{48,80},{64,96},{80,112},{96,0},{112,16},{1... | collective-permute-start | bytes 98312 | tf_op jit(solution)/shard_map/ppermute | solution.py:298
  137.7 15.5 %collective-permute-start.43 = (f32[8,8,128]{2,1,0:T(8,128)S(1)}, f32[8,8,128]{2,1,0:T(8,128)S(1)}, u32[]{:S(2)}, u32[]{:S(2)}) collective-permute-start(f32[8,8,128]{2,1,0:T(8,128)S(1)} %add.53.refs_0_), channel_id=1, source_target_pairs={{0,64},{16,80},{32,96},{48,112},{64,0},{80,16},{96,32},{112,48},{1... | collective-permute-start | bytes 98312 | tf_op jit(solution)/shard_map/ppermute | solution.py:298
  143.7 10.3 %collective-permute-start.44 = (f32[8,8,128]{2,1,0:T(8,128)S(1)}, f32[8,8,128]{2,1,0:T(8,128)S(1)}, u32[]{:S(2)}, u32[]{:S(2)}) collective-permute-start(f32[8,8,128]{2,1,0:T(8,128)S(1)} %add.53.refs_0_), channel_id=1, source_target_pairs={{0,96},{16,112},{32,0},{48,16},{64,32},{80,48},{96,64},{112,80},{1... | collective-permute-start | bytes 98312 | tf_op jit(solution)/shard_map/ppermute | solution.py:298
  147.1 9.2 %collective-permute-start.32 = (f32[8,1536]{1,0:T(8,128)S(1)}, f32[8,1536]{1,0:T(8,128)S(1)}, u32[]{:S(2)}, u32[]{:S(2)}) collective-permute-start(f32[8,1536]{1,0:T(8,128)S(1)} %get-tuple-element.85), channel_id=1, source_target_pairs={{0,3},{1,0},{2,1},{3,2},{4,7},{5,4},{6,5},{7,6},{8,11},{9,8},{10,9... | collective-permute-start | bytes 147464 | tf_op jit(solution)/shard_map/ppermute | solution.py:306
  150.6 17.5 %collective-permute-start.33 = (f32[8,1536]{1,0:T(8,128)S(1)}, f32[8,1536]{1,0:T(8,128)S(1)}, u32[]{:S(2)}, u32[]{:S(2)}) collective-permute-start(f32[8,1536]{1,0:T(8,128)S(1)} %get-tuple-element.84), channel_id=1, source_target_pairs={{0,2},{1,3},{2,0},{3,1},{4,6},{5,7},{6,4},{7,5},{8,10},{9,11},{10,... | collective-permute-start | bytes 147464 | tf_op jit(solution)/shard_map/ppermute | solution.py:306
  152.2 15.9 %collective-permute-start.34 = (f32[8,1536]{1,0:T(8,128)S(1)}, f32[8,1536]{1,0:T(8,128)S(1)}, u32[]{:S(2)}, u32[]{:S(2)}) collective-permute-start(f32[8,1536]{1,0:T(8,128)S(1)} %get-tuple-element.83), channel_id=1, source_target_pairs={{0,1},{1,2},{2,3},{3,0},{4,5},{5,6},{6,7},{7,4},{8,9},{9,10},{10,1... | collective-permute-start | bytes 147464 | tf_op jit(solution)/shard_map/ppermute | solution.py:306
  153.2 14.9 %collective-permute-start.26 = (f32[8,1536]{1,0:T(8,128)}, f32[8,1536]{1,0:T(8,128)S(1)}, u32[]{:S(2)}, u32[]{:S(2)}) collective-permute-start(f32[8,1536]{1,0:T(8,128)} %get-tuple-element.89), channel_id=1, source_target_pairs={{0,12},{1,13},{2,14},{3,15},{4,0},{5,1},{6,2},{7,3},{8,4},{9,5},{1... | collective-permute-start | bytes 147464 | tf_op jit(solution)/shard_map/ppermute | solution.py:306
  154.1 14.1 %collective-permute-start.27 = (f32[8,1536]{1,0:T(8,128)}, f32[8,1536]{1,0:T(8,128)S(1)}, u32[]{:S(2)}, u32[]{:S(2)}) collective-permute-start(f32[8,1536]{1,0:T(8,128)} %get-tuple-element.88), channel_id=1, source_target_pairs={{0,8},{1,9},{2,10},{3,11},{4,12},{5,13},{6,14},{7,15},{8,0},{9,1},... | collective-permute-start | bytes 147464 | tf_op jit(solution)/shard_map/ppermute | solution.py:306
  156.2 11.9 %collective-permute-start.28 = (f32[8,1536]{1,0:T(8,128)}, f32[8,1536]{1,0:T(8,128)S(1)}, u32[]{:S(2)}, u32[]{:S(2)}) collective-permute-start(f32[8,1536]{1,0:T(8,128)} %get-tuple-element.87), channel_id=1, source_target_pairs={{0,4},{1,5},{2,6},{3,7},{4,8},{5,9},{6,10},{7,11},{8,12},{9,13},{1... | collective-permute-start | bytes 147464 | tf_op jit(solution)/shard_map/ppermute | solution.py:306
  158.8 1.6 copy-start.4
  160.4 1.2 copy-start.10
  161.6 6.6 %copy-start.12 = (f32[2,4,12288]{2,1,0:T(4,128)S(1)}, f32[2,4,12288]{2,1,0:T(4,128)}, u32[]{:S(2)}) copy-start(f32[2,4,12288]{2,1,0:T(4,128)} %loads_ref.1) | copy-start | bytes 1179652

commit v3 on v2

--- a/solution.py
+++ b/solution.py
@@ -33,11 +33,11 @@
     return jnp.where(part < 4, -rolled, rolled)
 
 
-def dot_nn(a, b, precision=lax.Precision.HIGHEST):
+def dot_nn(a, b, precision):
     return lax.dot_general(a, b, (((1,), (0,)), ((), ())), precision=precision, preferred_element_type=F32)
 
 
-def dot_nt(a, b, precision=lax.Precision.HIGHEST):
+def dot_nt(a, b, precision):
     return lax.dot_general(a, b, (((1,), (1,)), ((), ())), precision=precision, preferred_element_type=F32)
 
 
@@ -154,16 +154,17 @@
     lane = lax.broadcasted_iota(jnp.int32, (NB, NB), 1)
     for step in range(STEPS):
         a = acc[step]
-        left = jnp.concatenate([a, times_i(a)], axis=1)
+        left = split(jnp.concatenate([a, times_i(a)], axis=1))
         near = jnp.concatenate([near_inverse(place_ref, d_ref, part, step) for part in range(2)], axis=1)
-        x = dot_nt(left, near)
+        x = dot_split(dot_nt, left, split(near))
         ix = times_i(x)
         natural = jnp.concatenate([d_ref[0, step], d_ref[1, step]], axis=1)
-        store_parts(sol_ref, step, dot_nt(left[:8], natural))
-        left = jnp.concatenate([x, ix], axis=1)
+        own_left = split(jnp.concatenate([a[:8], times_i(a[:8])], axis=1))
+        store_parts(sol_ref, step, dot_split(dot_nt, own_left, split(natural)))
+        left = split(jnp.concatenate([x, ix], axis=1))
         for row in range(step + 1, STEPS):
             right = jnp.concatenate([block_of(core, mine_ref, other_ref, row, step, part) for part in range(2)], axis=0)
-            acc[row] -= dot_nn(left, right)
+            acc[row] -= dot_split(dot_nn, left, split(right))
         for half, apart in enumerate((SIDE * WIDTH, WIDTH)):
             for by in range(SIDE):
                 at = half * SIDE + by
@@ -189,63 +190,85 @@
         v = loads_ref[:, step * NB : (step + 1) * NB]
         v -= (sums[0][step] + sums[1][step]) + (sums[2][step] + sums[3][step])
         right = jnp.concatenate([d_ref[0, step], -d_ref[1, step]], axis=0)
-        y = dot_nn(jnp.concatenate([v, times_i(v)], axis=1), right)
+        y = dot_split(dot_nn, split(jnp.concatenate([v, times_i(v)], axis=1)), split(right))
         if step < STEPS - 1:
             u = acc[step]
             near = [near_inverse(place_ref, d_ref, part, step) for part in range(2)]
-            y -= dot_nn(jnp.concatenate([u, times_i(u)], axis=1), jnp.concatenate([near[0], -near[1]], axis=0))
+            right = split(jnp.concatenate([near[0], -near[1]], axis=0))
+            y -= dot_split(dot_nn, split(jnp.concatenate([u, times_i(u)], axis=1)), right)
         store_parts(out_ref, step, y)
-        left = jnp.concatenate([y, times_i(y)], axis=1)
+        left = split(jnp.concatenate([y, times_i(y)], axis=1))
         for other in range(step):
             right = [block_of(core, mine_ref, other_ref, step, other, part) for part in range(2)]
-            acc[other] += dot_nt(left, jnp.concatenate([right[0], -right[1]], axis=1))
-
-
-def trail_kernel(*refs):
-    outs = refs[-2 * SIDE :]
-    for half in range(2):
-        x_ref = refs[half]
+            acc[other] += dot_split(dot_nt, left, split(jnp.concatenate([right[0], -right[1]], axis=1)))
+
+
+def trail_term(x_ref, by, piece_ref):
+    return dot_split(dot_nn, split(x_ref[:, by * NB : (by + 1) * NB]), split(piece_ref[...]))
+
+
+def zsum_term(place_ref, ta, half, by, piece_ref, out):
+    q = dot_split(dot_nt, ta, split(piece_ref[...]))
+    q = q - times_i(pltpu.roll(q, 64, 1))
+    index = (place_ref[2 + half] - by + SIDE) % SIDE
+    for dy in range(SIDE):
+        out[dy, index, :, half * 64 : half * 64 + 64] = q[dy * 32 : dy * 32 + 32, :64]
+
+
+def early_kernel(place_ref, *refs):
+    zout, touts = refs[-3], refs[-2:]
+    for half in range(2):
+        ta = split(refs[2 + half][...])
         total = None
+        for i, by in enumerate((0, 1, 3)):
+            piece = refs[4 + half * 3 + i]
+            zsum_term(place_ref, ta, half, by, piece, zout)
+            term = trail_term(refs[half], by, piece)
+            total = term if total is None else total + term
+        touts[half][...] = total
+
+
+def late_kernel(place_ref, *refs):
+    zin, tins, pieces, outs = refs[4], refs[5:7], refs[7:9], refs[-2 * SIDE - 1 : -1]
+    zsums = refs[-1]
+    zsums[...] = zin[...]
+    for half in range(2):
+        zsum_term(place_ref, split(refs[2 + half][...]), half, 2, pieces[half], zsums)
+        total = tins[half][...] + trail_term(refs[half], 2, pieces[half])
         for by in range(SIDE):
-            piece = refs[2 + half * SIDE + by]
-            term = dot_split(dot_nn, split(x_ref[:, by * NB : (by + 1) * NB]), split(piece[...]))
-            total = term if total is None else total + term
-        for by in range(SIDE):
-            outs[half * SIDE + by][...] = -total[by * 32 : by * 32 + 32]
-
-
-def zsum_kernel(place_ref, ta_first, ta_second, *refs):
-    pieces, outs = refs[: 2 * SIDE], refs[-SIDE:]
-    for half, ta_ref in enumerate((ta_first, ta_second)):
-        ta = split(ta_ref[...])
-        for by in range(SIDE):
-            q = dot_split(dot_nt, ta, split(pieces[half * SIDE + by][...]))
-            q = q - times_i(pltpu.roll(q, 64, 1))
-            index = (place_ref[2 + half] - by + SIDE) % SIDE
-            for dy in range(SIDE):
-                part = q[dy * 32 : dy * 32 + 32, :64]
-                outs[dy][index, :, half * 64 : half * 64 + 64] = part
-
-
-def middle_kernel(place_ref, *refs):
-    got, outs = refs[:SIDE], refs[-SIDE:]
-    for dx in range(SIDE):
-        rows = slice(dx * 8, dx * 8 + 8)
+            outs[half * SIDE + by][:, :QUARTER] = -total[by * 32 : by * 32 + 32]
+    for dy in range(SIDE):
+        for index in range(SIDE):
+            outs[SIDE + dy][:, QUARTER + index * NB : QUARTER + (index + 1) * NB] = zsums[dy, index]
+
+
+def middle_kernel(*refs):
+    got, outs = (refs[:SIDE], refs[SIDE : 2 * SIDE]), refs[-2 * SIDE :]
+    for by in range(SIDE):
+        rows = slice(by * 8, by * 8 + 8)
+        for half in range(2):
+            values = [ref[rows, :QUARTER] for ref in got[half]]
+            outs[half * SIDE + by][:, :QUARTER] = (values[0] + values[1]) + (values[2] + values[3])
         for col in range(SIDE):
-            values = [got[dy][col, rows, :] for dy in range(SIDE)]
-            outs[dx][16 + col] = (values[0] + values[1]) + (values[2] + values[3])
-            for dy in range(SIDE):
-                outs[dx][((place_ref[2] + dy) % SIDE) * SIDE + col] = values[dy]
+            values = [ref[rows, QUARTER + col * NB : QUARTER + (col + 1) * NB] for ref in got[1]]
+            values.append((values[0] + values[1]) + (values[2] + values[3]))
+            for dy in range(SIDE + 1):
+                to = QUARTER + (dy * SIDE + col) * NB
+                outs[SIDE + by][:, to : to + NB] = values[dy]
 
 
 def last_kernel(place_ref, *refs):
-    got, (out_ref, held) = refs[:SIDE], refs[SIDE:]
-    for col in range(COLS_AXIS):
-        value = (got[0][col] + got[1][col]) + (got[2][col] + got[3][col])
-        held[col] = pltpu.roll(value, 64, 1)
+    got, (out_ref, held) = refs[:SIDE], refs[-2:]
+    for dy in range(SIDE):
+        for col in range(SIDE):
+            at = QUARTER + (dy * SIDE + col) * NB
+            values = [ref[:, at : at + NB] for ref in got]
+            value = (values[0] + values[1]) + (values[2] + values[3])
+            held[(place_ref[2] + dy) % SIDE * SIDE + col] = pltpu.roll(value, 64, 1)
     for dx in range(SIDE):
         for y in range(SIDE):
-            held[y * SIDE + (place_ref[3] + dx) % SIDE] += got[dx][16 + y]
+            at = QUARTER + (SIDE * SIDE + y) * NB
+            held[y * SIDE + (place_ref[3] + dx) % SIDE] += got[dx][:, at : at + NB]
     lane = lax.broadcasted_iota(jnp.int32, (8, NB), 1)
     for step in range(STEPS):
         value = jnp.zeros((8, NB), F32)
@@ -256,12 +279,12 @@
 
 
 def finish_kernel(place_ref, loads_ref, *refs):
-    pieces, out_ref = refs[:-1], refs[-1]
+    pieces, out_ref = refs[: 2 * SIDE], refs[-1]
     for half in range(2):
         for by in range(SIDE):
             quarter = (place_ref[2 + half] + by) % SIDE
             to = aligned(FIRST[half] + quarter * QUARTER, NB)
-            value = pieces[half * SIDE + by][...]
+            value = pieces[half * SIDE + by][:, :QUARTER]
             for part in range(2):
                 rows = value[part * PER_COL : (part + 1) * PER_COL]
                 loads = loads_ref[part, :, pl.ds(aligned(to + NB, NB), QUARTER)]
@@ -325,6 +348,10 @@
     )
 
 
+def quarter_of(factor, place, half, by):
+    return lax.dynamic_slice(factor, (0, NB + FIRST[half] + (place[2 + half] + by) % SIDE * QUARTER), (NB, QUARTER))
+
+
 def body(load_vectors, panel_factor, diag_inverse, trail_adjoint, adjoint_loads):
     col, row = lax.axis_index("col"), lax.axis_index("row")
     place = jnp.stack([row // 2, row % 2, col // SIDE, col % SIDE]).astype(jnp.int32)
@@ -335,7 +362,7 @@
     got = to_other_core(lax.dynamic_index_in_dim(parts, 1 - core, 0, False))
     slab = jnp.concatenate([keep, got, load_vectors[:, :, :NB].reshape(8, NB)], axis=0)
     slabs = [slab] + [up_z(slab, by) for by in (1, 2, 3)]
-    early = cut(place, factor, (1, 3))
+    early = [quarter_of(factor, place, half, by) for half in range(2) for by in (1, 3)]
     one = [up(early[2 * half], AXES[half][0], 1) for half in range(2)]
     three = [up(early[2 * half + 1], AXES[half][0], 3) for half in range(2)]
     messages = call(
@@ -347,38 +374,47 @@
     )
     heard = [to_all(messages[half * SIDE : half * SIDE + SIDE], AXES[half][0]) for half in range(2)]
     first_lines = call(line_kernel, "line", [(SIDE, MESSAGE, 8, NB)] * 2, heard[0] + heard[1])
-    late = cut(place, factor, (0, 2), first_lines)
+    lines = to_all([first_lines[0]] * SIDE, AXES[0][1]) + to_all([first_lines[1]] * SIDE, AXES[1][1])
+    late = cut(place, factor, (0, 2), [lines[1], lines[5]])
     two = [up(late[2 * half + 1], AXES[half][0], 2) for half in range(2)]
     pieces = [[late[2 * half], one[half], two[half], three[half]] for half in range(2)]
-    lines = to_all([first_lines[0]] * SIDE, AXES[0][1]) + to_all([first_lines[1]] * SIDE, AXES[1][1])
     blocks, ta_first, ta_second = call(
-        repack_kernel, "repack", [(TILES, COLS_AXIS, 8, NB)] + [(NB, QUARTER)] * 2, lines, after=two
+        repack_kernel, "repack", [(TILES, COLS_AXIS, 8, NB)] + [(NB, QUARTER)] * 2, lines
     )
     window = (blocks, to_other_core(blocks))
-    zparts = call(
-        zsum_kernel,
-        "zsum",
-        [(SIDE, 32, NB)] * SIDE,
-        [place, ta_first, ta_second, *pieces[0], *pieces[1]],
-        us=3,
-    )
     *trail_x, sol = call(
         forward_kernel,
         "forward",
         [(NB, SIDE * NB)] * 2 + [(2, PER_COL, STEPS * NB)],
         [place, *window, diag_inverse],
         [pltpu.VMEM((STEPS, NB, NB), F32)] * 2,
-        after=[zparts[0]],
         us=6,
     )
-    trail = call(trail_kernel, "trail", [(32, QUARTER)] * 2 * SIDE, [*trail_x, *pieces[0], *pieces[1]], us=3)
-    zparts = call(middle_kernel, "middle", [(20, 8, NB)] * SIDE, [place, *to_all(zparts, "y", -1)], after=[trail[0]])
+    zpart, *tparts = call(
+        early_kernel,
+        "early",
+        [(SIDE, SIDE, 32, NB)] + [(NB, QUARTER)] * 2,
+        [place, *trail_x, ta_first, ta_second] + [pieces[half][by] for half in range(2) for by in (0, 1, 3)],
+        us=6,
+    )
+    sent = call(
+        late_kernel,
+        "late",
+        [(32, QUARTER)] * SIDE + [(32, QUARTER + SIDE * NB)] * SIDE,
+        [place, *trail_x, ta_first, ta_second, zpart, *tparts, pieces[0][2], pieces[1][2]],
+        [pltpu.VMEM((SIDE, SIDE, 32, NB), F32)],
+        us=3,
+    )
+    met = [to_all(sent[half * SIDE : half * SIDE + SIDE], AXES[half][1], -1) for half in range(2)]
+    sent = call(
+        middle_kernel,
+        "middle",
+        [(8, QUARTER)] * SIDE + [(8, QUARTER + 20 * NB)] * SIDE,
+        met[0] + met[1],
+    )
+    met = [to_all(sent[half * SIDE : half * SIDE + SIDE], AXES[half][0], -1) for half in range(2)]
     (zown,) = call(
-        last_kernel,
-        "last",
-        [(STEPS, 8, NB)],
-        [place, *to_all(zparts, "x", -1)],
-        [pltpu.VMEM((COLS_AXIS, 8, NB), F32)],
+        last_kernel, "last", [(STEPS, 8, NB)], [place, *met[1]], [pltpu.VMEM((COLS_AXIS, 8, NB), F32)]
     )
     zchip = zown + to_other_core(zown)
     zsums = [zchip] + [up_z(zchip, by) for by in (1, 2, 3)]
@@ -391,12 +427,13 @@
         [pltpu.VMEM((STEPS, 8, NB), F32)],
         us=6,
     )
-    back = []
-    for half in range(2):
-        met = to_all(trail[half * SIDE : half * SIDE + SIDE], AXES[half][1], -1)
-        total = (met[0] + met[1]) + (met[2] + met[3])
-        back += to_all([total[by * 8 : by * 8 + 8] for by in range(SIDE)], AXES[half][0], -1)
-    (residual,) = call(finish_kernel, "finish", [(2, PER_COL, TRAIL_LOCAL)], [place, load_vectors, *back])
+    (residual,) = call(
+        finish_kernel,
+        "finish",
+        [(2, PER_COL, TRAIL_LOCAL)],
+        [place, load_vectors, *met[0], *met[1]],
+        after=[zown],
+    )
     return sol, residual, adj
 
 

time: 171 us -> 150 us (0.88)
  starting transfers between devices: 68.6 us -> 56.9 us
  Pallas kernels: 29.5 us -> 23.3 us
  waiting for transfers between devices: 54.9 us -> 48.9 us
  local copies, waits for them, and re-layouts: 13.2 us -> 17 us
    ppermute x36 -> x30, starting transfers between devices: 54.8 us -> 45.7 us  [up(): return lax.ppermute(array, 'col', [(c, moved(c)) for c in range(COLS_AXIS)])]
    pallas_call x12 -> x11, Pallas kernels: 29.5 us -> 23.3 us  [call(): pl.pallas_call(kernel, out_shape=[jax.ShapeDtypeStruct(shape, F32) for sh...]
    ppermute x36 -> x30, waiting for transfers between devices: 43.5 us -> 38.2 us  [up(): return lax.ppermute(array, 'col', [(c, moved(c)) for c in range(COLS_AXIS)])]
    dynamic_slice x0 -> x1, local copies, waits for them, and re-layouts: none -> 3.67 us  [quarter_of(): lax.dynamic_slice(factor, (0, NB + FIRST[half] + (place[2 + half] + by) %...]
    ppermute x6, starting transfers between devices: 13.6 us -> 11 us  [up_z(): lax.ppermute(array, 'row', [(r, (r + 2 * by) % ROWS_AXIS) for r in range(...]
    add x2 -> x0, other arithmetic: 2.24 us -> none  [body(): total = met[0] + met[1] + (met[2] + met[3])]
    unnamed x34 -> x32, local copies, waits for them, and re-layouts: 10.5 us -> 8.57 us
  transfers between devices with their start and end apart: 45 -> 39, of which waited for: 14 -> 17; matrix products, arithmetic and copies ran while one was open for 3% -> 4% of each run, Pallas kernels for 14% -> 10%
where the time goes in v3:
time: 150 us; the launch traced here: 149 us
  starting transfers between devices  56.9 us (38%)
  waiting for transfers between devices  48.9 us (33%)
  Pallas kernels  23.3 us (16%)
  local copies, waits for them, and re-layouts  17 us (11%)
    ppermute x30, starting transfers between devices, up(): return lax.ppermute(array, 'col', [(c, moved(c)) for c in range(COLS_AXIS)])  45.7 us
    ppermute x30, waiting for transfers between devices, up(): return lax.ppermute(array, 'col', [(c, moved(c)) for c in range(COLS_AXIS)])  38.2 us
    pallas_call x11, Pallas kernels, call(): pl.pallas_call(kernel, out_shape=[jax.ShapeDtypeStruct(shape, F32) for sh...  23.3 us
    ppermute x6, starting transfers between devices, up_z(): lax.ppermute(array, 'row', [(r, (r + 2 * by) % ROWS_AXIS) for r in range(...  11 us
    ppermute x6, waiting for transfers between devices, up_z(): lax.ppermute(array, 'row', [(r, (r + 2 * by) % ROWS_AXIS) for r in range(...  9.47 us
    unnamed x32, local copies, waits for them, and re-layouts  8.57 us
    dynamic_slice x1, local copies, waits for them, and re-layouts, quarter_of(): lax.dynamic_slice(factor, (0, NB + FIRST[half] + (place[2 + half] + by) %...  3.67 us
  transfers between devices with their start and end apart: 39, of which 17 were waited for; matrix products, arithmetic and copies ran while one was open for 4% of the time, Pallas kernels for 10%

profile of v3, /device:TPU:8, one launch (start us, length us, event | category | flops | bytes accessed | tf_op | source)
XLA Modules:
  0.0 148.5 jit_solution(11919432073316728950)
XLA Ops:
  0.8 3.7 %constant_dynamic-slice_fusion.1 = (f32[128,1536]{1,0:T(8,128)}, f32[128,1536]{1,0:T(8,128)}, f32[128,1536]{1,0:T(8,128)}, f32[128,1536]{1,0:T(8,128)}) fusion(f32[128,12288]{1,0:T(8,128)} %bitcast.11, s32[]{:T(128)S(6)} %select_n.71, s32[]{:T(128)S(6)} %select_n.69, s32[]{:T(128)S(6)} %select_n.67, s32[]{:T(128)S(6)} %select_n.65), kind=kLoop, calls=%fused_computation.4 | loop fusion | bytes 6291472 | tf_op jit(solution)/shard_map/dynamic_slice | solution.py:352
  4.4 1.6 %collective-permute-start.4 = (f32[128,1536]{1,0:T(8,128)}, f32[128,1536]{1,0:T(8,128)S(1)}, u32[]{:S(2)}, u32[]{:S(2)}) collective-permute-start(f32[128,1536]{1,0:T(8,128)} %get-tuple-element.84), channel_id=1, source_target_pairs={{0,4},{1,5},{2,6},{3,7},{4,8},{5,9},{6,10},{7,11},{8,12},{9,13},{1... | collective-permute-start | bytes 2359304 | tf_op jit(solution)/shard_map/ppermute | solution.py:329
  6.0 1.5 %collective-permute-start.5 = (f32[128,1536]{1,0:T(8,128)}, f32[128,1536]{1,0:T(8,128)}, u32[]{:S(2)}, u32[]{:S(2)}) collective-permute-start(f32[128,1536]{1,0:T(8,128)} %get-tuple-element.83), channel_id=1, source_target_pairs={{0,1},{1,2},{2,3},{3,0},{4,5},{5,6},{6,7},{7,4},{8,9},{9,10},{10,1... | collective-permute-start | bytes 2359304 | tf_op jit(solution)/shard_map/ppermute | solution.py:329
  8.0 1.7 %collective-permute-start.7 = (f32[128,1536]{1,0:T(8,128)}, f32[128,1536]{1,0:T(8,128)}, u32[]{:S(2)}, u32[]{:S(2)}) collective-permute-start(f32[128,1536]{1,0:T(8,128)} %get-tuple-element.81), channel_id=1, source_target_pairs={{0,3},{1,0},{2,1},{3,2},{4,7},{5,4},{6,5},{7,6},{8,11},{9,8},{10,9... | collective-permute-start | bytes 2359304 | tf_op jit(solution)/shard_map/ppermute | solution.py:329
  9.7 0.8 slice.8
  10.6 1.2 collective-permute-done
  11.9 2.0 %collective-permute-start.1 = (f32[136,128]{1,0:T(8,128)S(1)}, f32[136,128]{1,0:T(8,128)S(1)}, u32[]{:S(2)}, u32[]{:S(2)}) collective-permute-start(f32[136,128]{1,0:T(8,128)S(1)} %pad_maximum_fusion.own_ref), channel_id=1, source_target_pairs={{0,32},{16,48},{32,64},{48,80},{64,96},{80,112},{96,0},{112,16},{1... | collective-permute-start | bytes 208904 | tf_op jit(solution)/shard_map/ppermute | solution.py:321
  13.8 4.6 %collective-permute-done.1.one_ref = f32[136,128]{1,0:T(8,128)S(1)} collective-permute-done((f32[136,128]{1,0:T(8,128)S(1)}, f32[136,128]{1,0:T(8,128)S(1)}, u32[]{:S(2)}, u32[]{:S(2)}) %collective-permute-start.1) | collective-permute-done | bytes 69664 | tf_op jit(solution)/shard_map/ppermute | solution.py:321
  18.5 1.6 %collective-permute-start.2 = (f32[136,128]{1,0:T(8,128)S(1)}, f32[136,128]{1,0:T(8,128)}, u32[]{:S(2)}, u32[]{:S(2)}) collective-permute-start(f32[136,128]{1,0:T(8,128)S(1)} %pad_maximum_fusion.own_ref), channel_id=1, source_target_pairs={{0,64},{16,80},{32,96},{48,112},{64,0},{80,16},{96,32},{112,48},{1... | collective-permute-start | bytes 208904 | tf_op jit(solution)/shard_map/ppermute | solution.py:321
  20.1 1.9 %reshape.24.ta_ref = f32[8,12160]{1,0:T(8,128)} reshape(f32[2,4,12160]{2,1,0:T(4,128)} %param.8) | data formatting | bytes 778240 | tf_op jit(solution)/shard_map/reshape | solution.py:372
  22.0 2.4 %collective-permute-done.2.two_ref = f32[136,128]{1,0:T(8,128)} collective-permute-done((f32[136,128]{1,0:T(8,128)S(1)}, f32[136,128]{1,0:T(8,128)}, u32[]{:S(2)}, u32[]{:S(2)}) %collective-permute-start.2) | collective-permute-done | bytes 69664 | tf_op jit(solution)/shard_map/ppermute | solution.py:321
  24.4 1.8 %collective-permute-start.3 = (f32[136,128]{1,0:T(8,128)S(1)}, f32[136,128]{1,0:T(8,128)S(1)}, u32[]{:S(2)}, u32[]{:S(2)}) collective-permute-start(f32[136,128]{1,0:T(8,128)S(1)} %pad_maximum_fusion.own_ref), channel_id=1, source_target_pairs={{0,96},{16,112},{32,0},{48,16},{64,32},{80,48},{96,64},{112,80},{1... | collective-permute-start | bytes 208904 | tf_op jit(solution)/shard_map/ppermute | solution.py:321
  26.3 2.4 %collective-permute-done.3.three_ref = f32[136,128]{1,0:T(8,128)S(1)} collective-permute-done((f32[136,128]{1,0:T(8,128)S(1)}, f32[136,128]{1,0:T(8,128)S(1)}, u32[]{:S(2)}, u32[]{:S(2)}) %collective-permute-start.3) | collective-permute-done | bytes 69664 | tf_op jit(solution)/shard_map/ppermute | solution.py:321
  28.7 1.0 copy-done.7
  29.7 1.1 pack.1
  30.8 1.6 %collective-permute-start.8 = (f32[28,8,128]{2,1,0:T(8,128)S(1)}, f32[28,8,128]{2,1,0:T(8,128)S(1)}, u32[]{:S(2)}, u32[]{:S(2)}) collective-permute-start(f32[28,8,128]{2,1,0:T(8,128)S(1)} %get-tuple-element.43), channel_id=1, source_target_pairs={{0,4},{1,5},{2,6},{3,7},{4,8},{5,9},{6,10},{7,11},{8,12},{9,13},{1... | collective-permute-start | bytes 344072 | tf_op jit(solution)/shard_map/ppermute | solution.py:329
  32.4 2.2 %collective-permute-start.9 = (f32[28,8,128]{2,1,0:T(8,128)S(1)}, f32[28,8,128]{2,1,0:T(8,128)S(1)}, u32[]{:S(2)}, u32[]{:S(2)}) collective-permute-start(f32[28,8,128]{2,1,0:T(8,128)S(1)} %get-tuple-element.44), channel_id=1, source_target_pairs={{0,8},{1,9},{2,10},{3,11},{4,12},{5,13},{6,14},{7,15},{8,0},{9,1},... | collective-permute-start | bytes 344072 | tf_op jit(solution)/shard_map/ppermute | solution.py:329
  34.6 1.2 collective-permute-start.10
  36.1 2.7 %collective-permute-start.12 = (f32[28,8,128]{2,1,0:T(8,128)S(1)}, f32[28,8,128]{2,1,0:T(8,128)S(1)}, u32[]{:S(2)}, u32[]{:S(2)}) collective-permute-start(f32[28,8,128]{2,1,0:T(8,128)S(1)} %get-tuple-element.48), channel_id=1, source_target_pairs={{0,2},{1,3},{2,0},{3,1},{4,6},{5,7},{6,4},{7,5},{8,10},{9,11},{10,... | collective-permute-start | bytes 344072 | tf_op jit(solution)/shard_map/ppermute | solution.py:329
  38.8 1.4 collective-permute-start.13
  40.2 2.8 %collective-permute-done.11.refs_5_ = f32[28,8,128]{2,1,0:T(8,128)S(1)} collective-permute-done((f32[28,8,128]{2,1,0:T(8,128)S(1)}, f32[28,8,128]{2,1,0:T(8,128)S(1)}, u32[]{:S(2)}, u32[]{:S(2)}) %collective-permute-start.11) | collective-permute-done | bytes 114720 | tf_op jit(solution)/shard_map/ppermute | solution.py:329
  43.0 0.9 collective-permute-done.13.refs_7_
  43.9 1.3 collective-permute-start.14
  45.2 2.9 %collective-permute-start.15 = (f32[4,28,8,128]{3,2,1,0:T(8,128)S(1)}, f32[4,28,8,128]{3,2,1,0:T(8,128)S(1)}, u32[]{:S(2)}, u32[]{:S(2)}) collective-permute-start(f32[4,28,8,128]{3,2,1,0:T(8,128)S(1)} %get-tuple-element.50.refs_0_), channel_id=1, source_target_pairs={{0,2},{1,3},{2,0},{3,1},{4,6},{5,7},{6,4},{7,5},{8,10},{9,11},{10,... | collective-permute-start | bytes 1376264 | tf_op jit(solution)/shard_map/ppermute | solution.py:329
  48.5 0.8 collective-permute-start.17
  49.3 2.6 %collective-permute-start.18 = (f32[4,28,8,128]{3,2,1,0:T(8,128)S(1)}, f32[4,28,8,128]{3,2,1,0:T(8,128)S(1)}, u32[]{:S(2)}, u32[]{:S(2)}) collective-permute-start(f32[4,28,8,128]{3,2,1,0:T(8,128)S(1)} %get-tuple-element.51.refs_4_), channel_id=1, source_target_pairs={{0,8},{1,9},{2,10},{3,11},{4,12},{5,13},{6,14},{7,15},{8,0},{9,1},... | collective-permute-start | bytes 1376264 | tf_op jit(solution)/shard_map/ppermute | solution.py:329
  51.9 6.7 %collective-permute-done.14.refs_1_.refs_0_ = f32[4,28,8,128]{3,2,1,0:T(8,128)S(1)} collective-permute-done((f32[4,28,8,128]{3,2,1,0:T(8,128)S(1)}, f32[4,28,8,128]{3,2,1,0:T(8,128)S(1)}, u32[]{:S(2)}, u32[]{:S(2)}) %collective-permute-start.14) | collective-permute-done | bytes 458784 | tf_op jit(solution)/shard_map/ppermute | solution.py:329
  58.6 1.3 collective-permute-start.19
  60.0 4.0 %collective-permute-done.15.refs_2_ = f32[4,28,8,128]{3,2,1,0:T(8,128)S(1)} collective-permute-done((f32[4,28,8,128]{3,2,1,0:T(8,128)S(1)}, f32[4,28,8,128]{3,2,1,0:T(8,128)S(1)}, u32[]{:S(2)}, u32[]{:S(2)}) %collective-permute-start.15) | collective-permute-done | bytes 458784 | tf_op jit(solution)/shard_map/ppermute | solution.py:329
  64.0 3.8 %collective-permute-done.19.refs_7_ = f32[4,28,8,128]{3,2,1,0:T(8,128)S(1)} collective-permute-done((f32[4,28,8,128]{3,2,1,0:T(8,128)S(1)}, f32[4,28,8,128]{3,2,1,0:T(8,128)S(1)}, u32[]{:S(2)}, u32[]{:S(2)}) %collective-permute-start.19) | collective-permute-done | bytes 458784 | tf_op jit(solution)/shard_map/ppermute | solution.py:329
  68.2 0.8 cut.1
  69.1 2.6 %collective-permute-start.21 = (f32[128,1536]{1,0:T(8,128)S(1)}, f32[128,1536]{1,0:T(8,128)S(1)}, u32[]{:S(2)}, u32[]{:S(2)}) collective-permute-start(f32[128,1536]{1,0:T(8,128)S(1)} %get-tuple-element.63), channel_id=1, source_target_pairs={{0,8},{1,9},{2,10},{3,11},{4,12},{5,13},{6,14},{7,15},{8,0},{9,1},... | collective-permute-start | bytes 2359304 | tf_op jit(solution)/shard_map/ppermute | solution.py:329
  71.7 1.5 %collective-permute-start.22 = (f32[128,1536]{1,0:T(8,128)S(1)}, f32[128,1536]{1,0:T(8,128)S(1)}, u32[]{:S(2)}, u32[]{:S(2)}) collective-permute-start(f32[128,1536]{1,0:T(8,128)S(1)} %get-tuple-element.64), channel_id=1, source_target_pairs={{0,2},{1,3},{2,0},{3,1},{4,6},{5,7},{6,4},{7,5},{8,10},{9,11},{10,... | collective-permute-start | bytes 2359304 | tf_op jit(solution)/shard_map/ppermute | solution.py:329
  73.2 4.6 %forward.1 = (f32[128,512]{1,0:T(8,128)S(1)}, f32[128,512]{1,0:T(8,128)S(1)}, f32[2,4,1024]{2,1,0:T(4,128)}) custom-call(s32[4]{0:T(128)S(1)} %pad_add_fusion.place_ref, f32[32,16,8,128]{3,2,1,0:T(8,128)S(1)} %get-tuple-element.52.mine_ref.refs_4_, f32[32,16,8,128]{3,2,1,0:T(8,128)S(1)} %collective-permute-done.20.other_ref.refs_5_, ...), custom_call_target="tpu_custom_call" | custom-call | bytes 21000000 | tf_op jit(solution)/shard_map/forward/pallas_call | solution.py:304
  77.8 1.3 copy-done.3
  79.1 5.7 %early.1 = (f32[4,4,32,128]{3,2,1,0:T(8,128)S(1)}, f32[128,1536]{1,0:T(8,128)S(1)}, f32[128,1536]{1,0:T(8,128)S(1)}) custom-call(s32[4]{0:T(128)S(1)} %pad_add_fusion.place_ref, f32[128,512]{1,0:T(8,128)S(1)} %get-tuple-element.54.refs_0_, f32[128,512]{1,0:T(8,128)S(1)} %get-tuple-element.55.refs_1_, f32[128,1536]{1,0:T(8,128)S(1)} %get-tuple-element.56.refs_2_, ...), custom_call_target="tpu_custom_call" | custom-call | bytes 21000000 | tf_op jit(solution)/shard_map/early/pallas_call | solution.py:304
  84.8 5.8 %collective-permute-done.21.refs_7_ = f32[128,1536]{1,0:T(8,128)S(1)} collective-permute-done((f32[128,1536]{1,0:T(8,128)S(1)}, f32[128,1536]{1,0:T(8,128)S(1)}, u32[]{:S(2)}, u32[]{:S(2)}) %collective-permute-start.21) | collective-permute-done | bytes 786464 | tf_op jit(solution)/shard_map/ppermute | solution.py:329
  90.6 2.3 %collective-permute-done.22.refs_8_ = f32[128,1536]{1,0:T(8,128)S(1)} collective-permute-done((f32[128,1536]{1,0:T(8,128)S(1)}, f32[128,1536]{1,0:T(8,128)S(1)}, u32[]{:S(2)}, u32[]{:S(2)}) %collective-permute-start.22) | collective-permute-done | bytes 786464 | tf_op jit(solution)/shard_map/ppermute | solution.py:329
  92.8 2.1 %late.1 = (f32[32,1536]{1,0:T(8,128)S(1)}, f32[32,1536]{1,0:T(8,128)S(1)}, f32[32,1536]{1,0:T(8,128)S(1)}, f32[32,1536]{1,0:T(8,128)S(1)}, f32[32,2048]{1,0:T(8,...) custom-call(s32[4]{0:T(128)S(1)} %pad_add_fusion.place_ref, ...), custom_call_target="tpu_custom_call" | custom-call | bytes 10500000 | tf_op jit(solution)/shard_map/late/pallas_call | solution.py:304
  94.9 1.0 collective-permute-start.23
  96.1 1.4 collective-permute-start.27
  97.5 2.1 %collective-permute-start.28 = (f32[32,2048]{1,0:T(8,128)S(1)}, f32[32,2048]{1,0:T(8,128)S(1)}, u32[]{:S(2)}, u32[]{:S(2)}) collective-permute-start(f32[32,2048]{1,0:T(8,128)S(1)} %get-tuple-element.72), channel_id=1, source_target_pairs={{0,4},{1,5},{2,6},{3,7},{4,8},{5,9},{6,10},{7,11},{8,12},{9,13},{1... | collective-permute-start | bytes 786440 | tf_op jit(solution)/shard_map/ppermute | solution.py:329
  99.5 2.6 %collective-permute-start.24 = (f32[32,1536]{1,0:T(8,128)S(1)}, f32[32,1536]{1,0:T(8,128)S(1)}, u32[]{:S(2)}, u32[]{:S(2)}) collective-permute-start(f32[32,1536]{1,0:T(8,128)S(1)} %get-tuple-element.67), channel_id=1, source_target_pairs={{0,2},{1,3},{2,0},{3,1},{4,6},{5,7},{6,4},{7,5},{8,10},{9,11},{10,... | collective-permute-start | bytes 589832 | tf_op jit(solution)/shard_map/ppermute | solution.py:329
  102.7 5.6 %collective-permute-done.24.refs_2_ = f32[32,1536]{1,0:T(8,128)S(1)} collective-permute-done((f32[32,1536]{1,0:T(8,128)S(1)}, f32[32,1536]{1,0:T(8,128)S(1)}, u32[]{:S(2)}, u32[]{:S(2)}) %collective-permute-start.24) | collective-permute-done | bytes 196640 | tf_op jit(solution)/shard_map/ppermute | solution.py:329
  108.3 2.0 %collective-permute-done.25.refs_3_ = f32[32,1536]{1,0:T(8,128)S(1)} collective-permute-done((f32[32,1536]{1,0:T(8,128)S(1)}, f32[32,1536]{1,0:T(8,128)S(1)}, u32[]{:S(2)}, u32[]{:S(2)}) %collective-permute-start.25) | collective-permute-done | bytes 196640 | tf_op jit(solution)/shard_map/ppermute | solution.py:329
  113.3 1.1 collective-permute-start.32
  114.4 2.0 %collective-permute-start.33 = (f32[8,4096]{1,0:T(8,128)S(1)}, f32[8,4096]{1,0:T(8,128)S(1)}, u32[]{:S(2)}, u32[]{:S(2)}) collective-permute-start(f32[8,4096]{1,0:T(8,128)S(1)} %get-tuple-element.79), channel_id=1, source_target_pairs={{0,2},{1,3},{2,0},{3,1},{4,6},{5,7},{6,4},{7,5},{8,10},{9,11},{10,... | collective-permute-start | bytes 393224 | tf_op jit(solution)/shard_map/ppermute | solution.py:329
  116.4 0.9 collective-permute-start.34
  117.3 1.5 %collective-permute-start.29 = (f32[8,1536]{1,0:T(8,128)}, f32[8,1536]{1,0:T(8,128)}, u32[]{:S(2)}, u32[]{:S(2)}) collective-permute-start(f32[8,1536]{1,0:T(8,128)} %get-tuple-element.74), channel_id=1, source_target_pairs={{0,12},{1,13},{2,14},{3,15},{4,0},{5,1},{6,2},{7,3},{8,4},{9,5},{1... | collective-permute-start | bytes 147464 | tf_op jit(solution)/shard_map/ppermute | solution.py:329
  119.1 2.3 %collective-permute-done.33.refs_2_.refs_6_ = f32[8,4096]{1,0:T(8,128)S(1)} collective-permute-done((f32[8,4096]{1,0:T(8,128)S(1)}, f32[8,4096]{1,0:T(8,128)S(1)}, u32[]{:S(2)}, u32[]{:S(2)}) %collective-permute-start.33) | collective-permute-done | bytes 131104 | tf_op jit(solution)/shard_map/ppermute | solution.py:329
  121.4 1.4 collective-permute-done.34.refs_3_.refs_7_
  122.8 1.5 last.1.refs_8_
  124.2 2.1 %collective-permute-start.30 = (f32[8,1536]{1,0:T(8,128)}, f32[8,1536]{1,0:T(8,128)}, u32[]{:S(2)}, u32[]{:S(2)}) collective-permute-start(f32[8,1536]{1,0:T(8,128)} %copy-done.13), channel_id=1, source_target_pairs={{0,8},{1,9},{2,10},{3,11},{4,12},{5,13},{6,14},{7,15},{8,0},{9,1},... | collective-permute-start | bytes 147464 | tf_op jit(solution)/shard_map/ppermute | solution.py:329
  126.3 2.2 %collective-permute-start.31 = (f32[8,1536]{1,0:T(8,128)}, f32[8,1536]{1,0:T(8,128)}, u32[]{:S(2)}, u32[]{:S(2)}) collective-permute-start(f32[8,1536]{1,0:T(8,128)} %copy-done.12), channel_id=1, source_target_pairs={{0,4},{1,5},{2,6},{3,7},{4,8},{5,9},{6,10},{7,11},{8,12},{9,13},{1... | collective-permute-start | bytes 147464 | tf_op jit(solution)/shard_map/ppermute | solution.py:329
  128.6 1.4 add.101.refs_0_
  130.0 1.0 collective-permute-start.36
  131.0 3.8 %collective-permute-start.37 = (f32[8,8,128]{2,1,0:T(8,128)}, f32[8,8,128]{2,1,0:T(8,128)}, u32[]{:S(2)}, u32[]{:S(2)}) collective-permute-start(f32[8,8,128]{2,1,0:T(8,128)} %add.101.refs_0_), channel_id=1, source_target_pairs={{0,64},{16,80},{32,96},{48,112},{64,0},{80,16},{96,32},{112,48},{1... | collective-permute-start | bytes 98312 | tf_op jit(solution)/shard_map/ppermute | solution.py:321
  134.8 0.8 collective-permute-start.38
  136.2 1.4 reshape.25.loads_ref
  137.6 0.8 copy-done.11
  138.4 1.7 %finish.1 = f32[2,4,12160]{2,1,0:T(4,128)} custom-call(s32[4]{0:T(128)S(1)} %pad_add_fusion.place_ref, f32[2,4,12288]{2,1,0:T(4,128)S(1)} %copy-done.8, f32[8,1536]{1,0:T(8,128)S(1)} %copy-done.11, f32[8,1536]{1,0:T(8,128)} %collective-permute-done.29.refs_1_, f32[8,1536]{1,0:T(8,128)} %collective-permute-done.30.refs_2_, ...), custom_call_target="tpu_custom_call" | custom-call | bytes 3500000 | tf_op jit(solution)/shard_map/finish/pallas_call | solution.py:304
  140.1 1.6 %copy-done.4 = f32[32,16,8,128]{3,2,1,0:T(8,128)S(1)} copy-done((f32[32,16,8,128]{3,2,1,0:T(8,128)S(1)}, f32[32,16,8,128]{3,2,1,0:T(8,128)}, u32[]{:S(2)}) %copy-start.4) | copy-done | bytes 2097176
  141.7 1.2 copy-done.6
  143.7 4.9 %backward.1 = f32[2,4,1024]{2,1,0:T(4,128)} custom-call(s32[4]{0:T(128)S(1)} %pad_add_fusion.place_ref, f32[8,1024]{1,0:T(8,128)S(1)} %copy-done.9, f32[8,8,128]{2,1,0:T(8,128)} %add.101.refs_0_, f32[8,8,128]{2,1,0:T(8,128)} %collective-permute-done.36.refs_1_, f32[8,8,128]{2,1,0:T(8,128)} %collective-permute-done.37.refs_2_, ...), custom_call_target="tpu_custom_call" | custom-call | bytes 21000000 | tf_op jit(solution)/shard_map/backward/pallas_call | solution.py:304
  (69 shorter events, 7.1 us)
Async XLA Ops:
  0.6 134.9 %copy-start = (f32[2,64,1024]{2,1,0:T(8,128)S(1)}, f32[2,64,1024]{2,1,0:T(8,128)}, u32[]{:S(2)}) copy-start(f32[2,64,1024]{2,1,0:T(8,128)} %param.9) | copy-start | bytes 1572868
  0.6 11.2 %slice-start.2 = ((f32[2,4,12288]{2,1,0:T(4,128)}), f32[2,4,128]{2,1,0:T(4,128)S(1)}, s32[]{:S(2)}) async-start(f32[2,4,12288]{2,1,0:T(4,128)} %loads_ref.1), calls=%async_computation.2 | async-start | bytes 8192 | tf_op jit(solution)/shard_map/slice | solution.py:363
  0.8 67.5 %slice-start = ((s8[6291456]{0:T(1024)(128)(4,1)}), s8[2097152]{0:T(1024)(128)(4,1)S(1)}, s32[]{:S(2)}) async-start(s8[6291456]{0:T(1024)(128)(4,1)} %bitcast.13), calls=%async_computation | async-start | bytes 4194304
  4.4 24.3 %collective-permute-start.4 = (f32[128,1536]{1,0:T(8,128)}, f32[128,1536]{1,0:T(8,128)S(1)}, u32[]{:S(2)}, u32[]{:S(2)}) collective-permute-start(f32[128,1536]{1,0:T(8,128)} %get-tuple-element.84), channel_id=1, source_target_pairs={{0,4},{1,5},{2,6},{3,7},{4,8},{5,9},{6,10},{7,11},{8,12},{9,13},{1... | collective-permute-start | bytes 2359304 | tf_op jit(solution)/shard_map/ppermute | solution.py:329
  6.0 22.7 %collective-permute-start.5 = (f32[128,1536]{1,0:T(8,128)}, f32[128,1536]{1,0:T(8,128)}, u32[]{:S(2)}, u32[]{:S(2)}) collective-permute-start(f32[128,1536]{1,0:T(8,128)} %get-tuple-element.83), channel_id=1, source_target_pairs={{0,1},{1,2},{2,3},{3,0},{4,5},{5,6},{6,7},{7,4},{8,9},{9,10},{10,1... | collective-permute-start | bytes 2359304 | tf_op jit(solution)/shard_map/ppermute | solution.py:329
  7.5 21.2 %collective-permute-start.6 = (f32[128,1536]{1,0:T(8,128)}, f32[128,1536]{1,0:T(8,128)}, u32[]{:S(2)}, u32[]{:S(2)}) collective-permute-start(f32[128,1536]{1,0:T(8,128)} %get-tuple-element.82), channel_id=1, source_target_pairs={{0,12},{1,13},{2,14},{3,15},{4,0},{5,1},{6,2},{7,3},{8,4},{9,5},{1... | collective-permute-start | bytes 2359304 | tf_op jit(solution)/shard_map/ppermute | solution.py:329
  8.0 20.8 %collective-permute-start.7 = (f32[128,1536]{1,0:T(8,128)}, f32[128,1536]{1,0:T(8,128)}, u32[]{:S(2)}, u32[]{:S(2)}) collective-permute-start(f32[128,1536]{1,0:T(8,128)} %get-tuple-element.81), channel_id=1, source_target_pairs={{0,3},{1,0},{2,1},{3,2},{4,7},{5,4},{6,5},{7,6},{8,11},{9,8},{10,9... | collective-permute-start | bytes 2359304 | tf_op jit(solution)/shard_map/ppermute | solution.py:329
  10.6 1.3 collective-permute-start
  11.9 6.6 %collective-permute-start.1 = (f32[136,128]{1,0:T(8,128)S(1)}, f32[136,128]{1,0:T(8,128)S(1)}, u32[]{:S(2)}, u32[]{:S(2)}) collective-permute-start(f32[136,128]{1,0:T(8,128)S(1)} %pad_maximum_fusion.own_ref), channel_id=1, source_target_pairs={{0,32},{16,48},{32,64},{48,80},{64,96},{80,112},{96,0},{112,16},{1... | collective-permute-start | bytes 208904 | tf_op jit(solution)/shard_map/ppermute | solution.py:321
  18.5 5.9 %collective-permute-start.2 = (f32[136,128]{1,0:T(8,128)S(1)}, f32[136,128]{1,0:T(8,128)}, u32[]{:S(2)}, u32[]{:S(2)}) collective-permute-start(f32[136,128]{1,0:T(8,128)S(1)} %pad_maximum_fusion.own_ref), channel_id=1, source_target_pairs={{0,64},{16,80},{32,96},{48,112},{64,0},{80,16},{96,32},{112,48},{1... | collective-permute-start | bytes 208904 | tf_op jit(solution)/shard_map/ppermute | solution.py:321
  24.4 4.3 %collective-permute-start.3 = (f32[136,128]{1,0:T(8,128)S(1)}, f32[136,128]{1,0:T(8,128)S(1)}, u32[]{:S(2)}, u32[]{:S(2)}) collective-permute-start(f32[136,128]{1,0:T(8,128)S(1)} %pad_maximum_fusion.own_ref), channel_id=1, source_target_pairs={{0,96},{16,112},{32,0},{48,16},{64,32},{80,48},{96,64},{112,80},{1... | collective-permute-start | bytes 208904 | tf_op jit(solution)/shard_map/ppermute | solution.py:321
  26.3 42.0 %slice-start.1 = ((s8[6291456]{0:T(1024)(128)(4,1)}), s8[4194304]{0:T(1024)(128)(4,1)S(1)}, s32[]{:S(2)}) async-start(s8[6291456]{0:T(1024)(128)(4,1)} %bitcast.13), calls=%async_computation.1 | async-start | bytes 8388608
  28.7 1.0 copy-start.7
  30.8 42.4 %copy-start.5 = (f32[2,8,128,128]{3,2,1,0:T(8,128)S(1)}, f32[2,8,128,128]{3,2,1,0:T(8,128)}, u32[]{:S(2)}) copy-start(f32[2,8,128,128]{3,2,1,0:T(8,128)} %refs_6_.1) | copy-start | bytes 3145732
  30.8 8.0 %collective-permute-start.8 = (f32[28,8,128]{2,1,0:T(8,128)S(1)}, f32[28,8,128]{2,1,0:T(8,128)S(1)}, u32[]{:S(2)}, u32[]{:S(2)}) collective-permute-start(f32[28,8,128]{2,1,0:T(8,128)S(1)} %get-tuple-element.43), channel_id=1, source_target_pairs={{0,4},{1,5},{2,6},{3,7},{4,8},{5,9},{6,10},{7,11},{8,12},{9,13},{1... | collective-permute-start | bytes 344072 | tf_op jit(solution)/shard_map/ppermute | solution.py:329
  32.4 7.8 %collective-permute-start.9 = (f32[28,8,128]{2,1,0:T(8,128)S(1)}, f32[28,8,128]{2,1,0:T(8,128)S(1)}, u32[]{:S(2)}, u32[]{:S(2)}) collective-permute-start(f32[28,8,128]{2,1,0:T(8,128)S(1)} %get-tuple-element.44), channel_id=1, source_target_pairs={{0,8},{1,9},{2,10},{3,11},{4,12},{5,13},{6,14},{7,15},{8,0},{9,1},... | collective-permute-start | bytes 344072 | tf_op jit(solution)/shard_map/ppermute | solution.py:329
  34.6 5.7 %collective-permute-start.10 = (f32[28,8,128]{2,1,0:T(8,128)S(1)}, f32[28,8,128]{2,1,0:T(8,128)S(1)}, u32[]{:S(2)}, u32[]{:S(2)}) collective-permute-start(f32[28,8,128]{2,1,0:T(8,128)S(1)} %get-tuple-element.45), channel_id=1, source_target_pairs={{0,12},{1,13},{2,14},{3,15},{4,0},{5,1},{6,2},{7,3},{8,4},{9,5},{1... | collective-permute-start | bytes 344072 | tf_op jit(solution)/shard_map/ppermute | solution.py:329
  35.8 7.2 %collective-permute-start.11 = (f32[28,8,128]{2,1,0:T(8,128)S(1)}, f32[28,8,128]{2,1,0:T(8,128)S(1)}, u32[]{:S(2)}, u32[]{:S(2)}) collective-permute-start(f32[28,8,128]{2,1,0:T(8,128)S(1)} %get-tuple-element.47), channel_id=1, source_target_pairs={{0,1},{1,2},{2,3},{3,0},{4,5},{5,6},{6,7},{7,4},{8,9},{9,10},{10,1... | collective-permute-start | bytes 344072 | tf_op jit(solution)/shard_map/ppermute | solution.py:329
  36.1 7.0 %collective-permute-start.12 = (f32[28,8,128]{2,1,0:T(8,128)S(1)}, f32[28,8,128]{2,1,0:T(8,128)S(1)}, u32[]{:S(2)}, u32[]{:S(2)}) collective-permute-start(f32[28,8,128]{2,1,0:T(8,128)S(1)} %get-tuple-element.48), channel_id=1, source_target_pairs={{0,2},{1,3},{2,0},{3,1},{4,6},{5,7},{6,4},{7,5},{8,10},{9,11},{10,... | collective-permute-start | bytes 344072 | tf_op jit(solution)/shard_map/ppermute | solution.py:329
  38.8 5.1 %collective-permute-start.13 = (f32[28,8,128]{2,1,0:T(8,128)S(1)}, f32[28,8,128]{2,1,0:T(8,128)S(1)}, u32[]{:S(2)}, u32[]{:S(2)}) collective-permute-start(f32[28,8,128]{2,1,0:T(8,128)S(1)} %get-tuple-element.49), channel_id=1, source_target_pairs={{0,3},{1,0},{2,1},{3,2},{4,7},{5,4},{6,5},{7,6},{8,11},{9,8},{10,9... | collective-permute-start | bytes 344072 | tf_op jit(solution)/shard_map/ppermute | solution.py:329
  43.9 14.7 %collective-permute-start.14 = (f32[4,28,8,128]{3,2,1,0:T(8,128)S(1)}, f32[4,28,8,128]{3,2,1,0:T(8,128)S(1)}, u32[]{:S(2)}, u32[]{:S(2)}) collective-permute-start(f32[4,28,8,128]{3,2,1,0:T(8,128)S(1)} %get-tuple-element.50.refs_0_), channel_id=1, source_target_pairs={{0,1},{1,2},{2,3},{3,0},{4,5},{5,6},{6,7},{7,4},{8,9},{9,10},{10,1... | collective-permute-start | bytes 1376264 | tf_op jit(solution)/shard_map/ppermute | solution.py:329
  45.2 18.7 %collective-permute-start.15 = (f32[4,28,8,128]{3,2,1,0:T(8,128)S(1)}, f32[4,28,8,128]{3,2,1,0:T(8,128)S(1)}, u32[]{:S(2)}, u32[]{:S(2)}) collective-permute-start(f32[4,28,8,128]{3,2,1,0:T(8,128)S(1)} %get-tuple-element.50.refs_0_), channel_id=1, source_target_pairs={{0,2},{1,3},{2,0},{3,1},{4,6},{5,7},{6,4},{7,5},{8,10},{9,11},{10,... | collective-permute-start | bytes 1376264 | tf_op jit(solution)/shard_map/ppermute | solution.py:329
  48.2 15.8 %collective-permute-start.16 = (f32[4,28,8,128]{3,2,1,0:T(8,128)S(1)}, f32[4,28,8,128]{3,2,1,0:T(8,128)S(1)}, u32[]{:S(2)}, u32[]{:S(2)}) collective-permute-start(f32[4,28,8,128]{3,2,1,0:T(8,128)S(1)} %get-tuple-element.50.refs_0_), channel_id=1, source_target_pairs={{0,3},{1,0},{2,1},{3,2},{4,7},{5,4},{6,5},{7,6},{8,11},{9,8},{10,9... | collective-permute-start | bytes 1376264 | tf_op jit(solution)/shard_map/ppermute | solution.py:329
  48.5 15.5 %collective-permute-start.17 = (f32[4,28,8,128]{3,2,1,0:T(8,128)S(1)}, f32[4,28,8,128]{3,2,1,0:T(8,128)S(1)}, u32[]{:S(2)}, u32[]{:S(2)}) collective-permute-start(f32[4,28,8,128]{3,2,1,0:T(8,128)S(1)} %get-tuple-element.51.refs_4_), channel_id=1, source_target_pairs={{0,4},{1,5},{2,6},{3,7},{4,8},{5,9},{6,10},{7,11},{8,12},{9,13},{1... | collective-permute-start | bytes 1376264 | tf_op jit(solution)/shard_map/ppermute | solution.py:329
  49.3 14.7 %collective-permute-start.18 = (f32[4,28,8,128]{3,2,1,0:T(8,128)S(1)}, f32[4,28,8,128]{3,2,1,0:T(8,128)S(1)}, u32[]{:S(2)}, u32[]{:S(2)}) collective-permute-start(f32[4,28,8,128]{3,2,1,0:T(8,128)S(1)} %get-tuple-element.51.refs_4_), channel_id=1, source_target_pairs={{0,8},{1,9},{2,10},{3,11},{4,12},{5,13},{6,14},{7,15},{8,0},{9,1},... | collective-permute-start | bytes 1376264 | tf_op jit(solution)/shard_map/ppermute | solution.py:329
  58.6 9.1 %collective-permute-start.19 = (f32[4,28,8,128]{3,2,1,0:T(8,128)S(1)}, f32[4,28,8,128]{3,2,1,0:T(8,128)S(1)}, u32[]{:S(2)}, u32[]{:S(2)}) collective-permute-start(f32[4,28,8,128]{3,2,1,0:T(8,128)S(1)} %get-tuple-element.51.refs_4_), channel_id=1, source_target_pairs={{0,12},{1,13},{2,14},{3,15},{4,0},{5,1},{6,2},{7,3},{8,4},{9,5},{1... | collective-permute-start | bytes 1376264 | tf_op jit(solution)/shard_map/ppermute | solution.py:329
  68.1 16.7 %copy-start.1 = (f32[32,16,8,128]{3,2,1,0:T(8,128)}, f32[32,16,8,128]{3,2,1,0:T(8,128)S(1)}, u32[]{:S(2)}) copy-start(f32[32,16,8,128]{3,2,1,0:T(8,128)S(1)} %get-tuple-element.52.mine_ref.refs_4_) | copy-start | bytes 6291460
  68.1 5.1 %collective-permute-start.20 = (f32[32,16,8,128]{3,2,1,0:T(8,128)S(1)}, f32[32,16,8,128]{3,2,1,0:T(8,128)S(1)}, u32[]{:S(2)}, u32[]{:S(2)}) collective-permute-start(f32[32,16,8,128]{3,2,1,0:T(8,128)S(1)} %get-tuple-element.52.mine_ref.refs_4_), channel_id=1, source_target_pairs={{0,16},{16,0},{32,48},{48,32},{64,80},{80,64},{96,112},{112,96},{1... | collective-permute-start | bytes 6291464 | tf_op jit(solution)/shard_map/ppermute | solution.py:317
  69.1 21.5 %collective-permute-start.21 = (f32[128,1536]{1,0:T(8,128)S(1)}, f32[128,1536]{1,0:T(8,128)S(1)}, u32[]{:S(2)}, u32[]{:S(2)}) collective-permute-start(f32[128,1536]{1,0:T(8,128)S(1)} %get-tuple-element.63), channel_id=1, source_target_pairs={{0,8},{1,9},{2,10},{3,11},{4,12},{5,13},{6,14},{7,15},{8,0},{9,1},... | collective-permute-start | bytes 2359304 | tf_op jit(solution)/shard_map/ppermute | solution.py:329
  71.7 21.1 %collective-permute-start.22 = (f32[128,1536]{1,0:T(8,128)S(1)}, f32[128,1536]{1,0:T(8,128)S(1)}, u32[]{:S(2)}, u32[]{:S(2)}) collective-permute-start(f32[128,1536]{1,0:T(8,128)S(1)} %get-tuple-element.64), channel_id=1, source_target_pairs={{0,2},{1,3},{2,0},{3,1},{4,6},{5,7},{6,4},{7,5},{8,10},{9,11},{10,... | collective-permute-start | bytes 2359304 | tf_op jit(solution)/shard_map/ppermute | solution.py:329
  77.8 1.3 copy-start.3
  84.8 52.8 %copy-start.8 = (f32[2,4,12288]{2,1,0:T(4,128)S(1)}, f32[2,4,12288]{2,1,0:T(4,128)}, u32[]{:S(2)}) copy-start(f32[2,4,12288]{2,1,0:T(4,128)} %loads_ref.1) | copy-start | bytes 1179652
  90.6 49.5 %copy-start.2 = (f32[32,16,8,128]{3,2,1,0:T(8,128)S(1)}, f32[32,16,8,128]{3,2,1,0:T(8,128)}, u32[]{:S(2)}) copy-start(f32[32,16,8,128]{3,2,1,0:T(8,128)} %copy-done.1) | copy-start | bytes 6291460
  94.9 7.2 %collective-permute-start.23 = (f32[32,1536]{1,0:T(8,128)S(1)}, f32[32,1536]{1,0:T(8,128)S(1)}, u32[]{:S(2)}, u32[]{:S(2)}) collective-permute-start(f32[32,1536]{1,0:T(8,128)S(1)} %get-tuple-element.66), channel_id=1, source_target_pairs={{0,3},{1,0},{2,1},{3,2},{4,7},{5,4},{6,5},{7,6},{8,11},{9,8},{10,9... | collective-permute-start | bytes 589832 | tf_op jit(solution)/shard_map/ppermute | solution.py:329
  96.0 14.4 %collective-permute-start.26 = (f32[32,2048]{1,0:T(8,128)S(1)}, f32[32,2048]{1,0:T(8,128)S(1)}, u32[]{:S(2)}, u32[]{:S(2)}) collective-permute-start(f32[32,2048]{1,0:T(8,128)S(1)} %get-tuple-element.70), channel_id=1, source_target_pairs={{0,12},{1,13},{2,14},{3,15},{4,0},{5,1},{6,2},{7,3},{8,4},{9,5},{1... | collective-permute-start | bytes 786440 | tf_op jit(solution)/shard_map/ppermute | solution.py:329
  96.1 14.3 %collective-permute-start.27 = (f32[32,2048]{1,0:T(8,128)S(1)}, f32[32,2048]{1,0:T(8,128)S(1)}, u32[]{:S(2)}, u32[]{:S(2)}) collective-permute-start(f32[32,2048]{1,0:T(8,128)S(1)} %get-tuple-element.71), channel_id=1, source_target_pairs={{0,8},{1,9},{2,10},{3,11},{4,12},{5,13},{6,14},{7,15},{8,0},{9,1},... | collective-permute-start | bytes 786440 | tf_op jit(solution)/shard_map/ppermute | solution.py:329
  97.5 13.3 %collective-permute-start.28 = (f32[32,2048]{1,0:T(8,128)S(1)}, f32[32,2048]{1,0:T(8,128)S(1)}, u32[]{:S(2)}, u32[]{:S(2)}) collective-permute-start(f32[32,2048]{1,0:T(8,128)S(1)} %get-tuple-element.72), channel_id=1, source_target_pairs={{0,4},{1,5},{2,6},{3,7},{4,8},{5,9},{6,10},{7,11},{8,12},{9,13},{1... | collective-permute-start | bytes 786440 | tf_op jit(solution)/shard_map/ppermute | solution.py:329
  99.5 8.8 %collective-permute-start.24 = (f32[32,1536]{1,0:T(8,128)S(1)}, f32[32,1536]{1,0:T(8,128)S(1)}, u32[]{:S(2)}, u32[]{:S(2)}) collective-permute-start(f32[32,1536]{1,0:T(8,128)S(1)} %get-tuple-element.67), channel_id=1, source_target_pairs={{0,2},{1,3},{2,0},{3,1},{4,6},{5,7},{6,4},{7,5},{8,10},{9,11},{10,... | collective-permute-start | bytes 589832 | tf_op jit(solution)/shard_map/ppermute | solution.py:329
  102.2 8.2 %collective-permute-start.25 = (f32[32,1536]{1,0:T(8,128)S(1)}, f32[32,1536]{1,0:T(8,128)S(1)}, u32[]{:S(2)}, u32[]{:S(2)}) collective-permute-start(f32[32,1536]{1,0:T(8,128)S(1)} %get-tuple-element.68), channel_id=1, source_target_pairs={{0,1},{1,2},{2,3},{3,0},{4,5},{5,6},{6,7},{7,4},{8,9},{9,10},{10,1... | collective-permute-start | bytes 589832 | tf_op jit(solution)/shard_map/ppermute | solution.py:329
  111.5 0.6 copy-start.10
  112.1 0.6 copy-start.12
  112.7 0.6 copy-start.13
  113.3 5.8 %collective-permute-start.32 = (f32[8,4096]{1,0:T(8,128)S(1)}, f32[8,4096]{1,0:T(8,128)S(1)}, u32[]{:S(2)}, u32[]{:S(2)}) collective-permute-start(f32[8,4096]{1,0:T(8,128)S(1)} %get-tuple-element.78), channel_id=1, source_target_pairs={{0,3},{1,0},{2,1},{3,2},{4,7},{5,4},{6,5},{7,6},{8,11},{9,8},{10,9... | collective-permute-start | bytes 393224 | tf_op jit(solution)/shard_map/ppermute | solution.py:329
  114.4 7.0 %collective-permute-start.33 = (f32[8,4096]{1,0:T(8,128)S(1)}, f32[8,4096]{1,0:T(8,128)S(1)}, u32[]{:S(2)}, u32[]{:S(2)}) collective-permute-start(f32[8,4096]{1,0:T(8,128)S(1)} %get-tuple-element.79), channel_id=1, source_target_pairs={{0,2},{1,3},{2,0},{3,1},{4,6},{5,7},{6,4},{7,5},{8,10},{9,11},{10,... | collective-permute-start | bytes 393224 | tf_op jit(solution)/shard_map/ppermute | solution.py:329
  116.4 6.4 %collective-permute-start.34 = (f32[8,4096]{1,0:T(8,128)S(1)}, f32[8,4096]{1,0:T(8,128)S(1)}, u32[]{:S(2)}, u32[]{:S(2)}) collective-permute-start(f32[8,4096]{1,0:T(8,128)S(1)} %get-tuple-element.80), channel_id=1, source_target_pairs={{0,1},{1,2},{2,3},{3,0},{4,5},{5,6},{6,7},{7,4},{8,9},{9,10},{10,1... | collective-permute-start | bytes 393224 | tf_op jit(solution)/shard_map/ppermute | solution.py:329
  117.3 17.5 %collective-permute-start.29 = (f32[8,1536]{1,0:T(8,128)}, f32[8,1536]{1,0:T(8,128)}, u32[]{:S(2)}, u32[]{:S(2)}) collective-permute-start(f32[8,1536]{1,0:T(8,128)} %get-tuple-element.74), channel_id=1, source_target_pairs={{0,12},{1,13},{2,14},{3,15},{4,0},{5,1},{6,2},{7,3},{8,4},{9,5},{1... | collective-permute-start | bytes 147464 | tf_op jit(solution)/shard_map/ppermute | solution.py:329
  124.2 4.3 %collective-permute-start.35 = (f32[8,8,128]{2,1,0:T(8,128)}, f32[8,8,128]{2,1,0:T(8,128)}, u32[]{:S(2)}, u32[]{:S(2)}) collective-permute-start(f32[8,8,128]{2,1,0:T(8,128)} %last.1.refs_8_), channel_id=1, source_target_pairs={{0,16},{16,0},{32,48},{48,32},{64,80},{80,64},{96,112},{112,96},{1... | collective-permute-start | bytes 98312 | tf_op jit(solution)/shard_map/ppermute | solution.py:317
  124.2 13.3 %collective-permute-start.30 = (f32[8,1536]{1,0:T(8,128)}, f32[8,1536]{1,0:T(8,128)}, u32[]{:S(2)}, u32[]{:S(2)}) collective-permute-start(f32[8,1536]{1,0:T(8,128)} %copy-done.13), channel_id=1, source_target_pairs={{0,8},{1,9},{2,10},{3,11},{4,12},{5,13},{6,14},{7,15},{8,0},{9,1},... | collective-permute-start | bytes 147464 | tf_op jit(solution)/shard_map/ppermute | solution.py:329
  126.3 11.2 %collective-permute-start.31 = (f32[8,1536]{1,0:T(8,128)}, f32[8,1536]{1,0:T(8,128)}, u32[]{:S(2)}, u32[]{:S(2)}) collective-permute-start(f32[8,1536]{1,0:T(8,128)} %copy-done.12), channel_id=1, source_target_pairs={{0,4},{1,5},{2,6},{3,7},{4,8},{5,9},{6,10},{7,11},{8,12},{9,13},{1... | collective-permute-start | bytes 147464 | tf_op jit(solution)/shard_map/ppermute | solution.py:329
  130.0 10.1 %collective-permute-start.36 = (f32[8,8,128]{2,1,0:T(8,128)}, f32[8,8,128]{2,1,0:T(8,128)}, u32[]{:S(2)}, u32[]{:S(2)}) collective-permute-start(f32[8,8,128]{2,1,0:T(8,128)} %add.101.refs_0_), channel_id=1, source_target_pairs={{0,32},{16,48},{32,64},{48,80},{64,96},{80,112},{96,0},{112,16},{1... | collective-permute-start | bytes 98312 | tf_op jit(solution)/shard_map/ppermute | solution.py:321
  131.0 9.1 %collective-permute-start.37 = (f32[8,8,128]{2,1,0:T(8,128)}, f32[8,8,128]{2,1,0:T(8,128)}, u32[]{:S(2)}, u32[]{:S(2)}) collective-permute-start(f32[8,8,128]{2,1,0:T(8,128)} %add.101.refs_0_), channel_id=1, source_target_pairs={{0,64},{16,80},{32,96},{48,112},{64,0},{80,16},{96,32},{112,48},{1... | collective-permute-start | bytes 98312 | tf_op jit(solution)/shard_map/ppermute | solution.py:321
  134.8 5.3 %collective-permute-start.38 = (f32[8,8,128]{2,1,0:T(8,128)}, f32[8,8,128]{2,1,0:T(8,128)}, u32[]{:S(2)}, u32[]{:S(2)}) collective-permute-start(f32[8,8,128]{2,1,0:T(8,128)} %add.101.refs_0_), channel_id=1, source_target_pairs={{0,96},{16,112},{32,0},{48,16},{64,32},{80,48},{96,64},{112,80},{1... | collective-permute-start | bytes 98312 | tf_op jit(solution)/shard_map/ppermute | solution.py:321
  137.6 0.8 copy-start.11
  140.1 1.6 %copy-start.4 = (f32[32,16,8,128]{3,2,1,0:T(8,128)S(1)}, f32[32,16,8,128]{3,2,1,0:T(8,128)}, u32[]{:S(2)}) copy-start(f32[32,16,8,128]{3,2,1,0:T(8,128)} %copy-done.3) | copy-start | bytes 6291460
  141.7 1.2 copy-start.6
  142.9 0.8 copy-start.9

commit v4 on v3

--- a/solution.py
+++ b/solution.py
@@ -103,6 +103,15 @@
                 if half == 1 and tile == 0:
                     value = jnp.where(quarter == 0, 0.0, value)
                 out[TILES // 2 + tile] = value
+
+
+def hold_kernel(*refs):
+    ins, outs, sems = refs[:4], refs[-5:-1], refs[-1]
+    copies = [pltpu.make_async_copy(ins[i], outs[i], sems.at[i]) for i in range(4)]
+    for copy in copies:
+        copy.start()
+    for copy in copies:
+        copy.wait()
 
 
 def line_kernel(*refs):
@@ -294,12 +303,11 @@
 VMEM = pl.BlockSpec(memory_space=pltpu.VMEM)
 SMEM = pl.BlockSpec(memory_space=pltpu.SMEM)
 ANY = pl.BlockSpec(memory_space=pl.ANY)
-HBM = pl.BlockSpec(memory_space=pltpu.HBM)
 
 
 def call(kernel, name, shapes, args, scratch=(), after=(), far=(), us=1):
     specs = [SMEM if arg.dtype == jnp.int32 else VMEM for arg in args]
-    specs = [HBM if i in far else spec for i, spec in enumerate(specs)] + [ANY] * len(after)
+    specs = [ANY if i in far else spec for i, spec in enumerate(specs)] + [ANY] * len(after)
     args = [*args, *after]
     return pl.pallas_call(
         kernel,
@@ -405,12 +413,23 @@
         [pltpu.VMEM((SIDE, SIDE, 32, NB), F32)],
         us=3,
     )
+    mine = lax.dynamic_slice_in_dim(adjoint_loads, col * PER_COL, PER_COL, 1).reshape(8, STEPS * NB)
+    held = call(
+        hold_kernel,
+        "hold",
+        [window[0].shape, window[1].shape, diag_inverse.shape, mine.shape],
+        [*window, diag_inverse, mine],
+        [pltpu.SemaphoreType.DMA((4,))],
+        sent[:1],
+        range(4),
+    )
     met = [to_all(sent[half * SIDE : half * SIDE + SIDE], AXES[half][1], -1) for half in range(2)]
     sent = call(
         middle_kernel,
         "middle",
         [(8, QUARTER)] * SIDE + [(8, QUARTER + 20 * NB)] * SIDE,
         met[0] + met[1],
+        after=held[:1],
     )
     met = [to_all(sent[half * SIDE : half * SIDE + SIDE], AXES[half][0], -1) for half in range(2)]
     (zown,) = call(
@@ -418,12 +437,11 @@
     )
     zchip = zown + to_other_core(zown)
     zsums = [zchip] + [up_z(zchip, by) for by in (1, 2, 3)]
-    mine = lax.dynamic_slice_in_dim(adjoint_loads, col * PER_COL, PER_COL, 1).reshape(8, STEPS * NB)
     (adj,) = call(
         backward_kernel,
         "backward",
         [(2, PER_COL, STEPS * NB)],
-        [place, mine, *zsums, *window, diag_inverse],
+        [place, held[3], *zsums, *held[:3]],
         [pltpu.VMEM((STEPS, 8, NB), F32)],
         us=6,
     )

time: 150 us -> 142 us (0.947)
  local copies, waits for them, and re-layouts: 17 us -> 13 us
  waiting for transfers between devices: 48.9 us -> 46.3 us
    ppermute x30, waiting for transfers between devices: 38.2 us -> 33.9 us  [up(): return lax.ppermute(array, 'col', [(c, moved(c)) for c in range(COLS_AXIS)])]
    unnamed x32 -> x24, local copies, waits for them, and re-layouts: 8.57 us -> 4.61 us
    ppermute x6, waiting for transfers between devices: 9.47 us -> 11.2 us  [up_z(): lax.ppermute(array, 'row', [(r, (r + 2 * by) % ROWS_AXIS) for r in range(...]
    pallas_call x11 -> x12, Pallas kernels: 23.3 us -> 24.1 us  [call(): pl.pallas_call(kernel, out_shape=[jax.ShapeDtypeStruct(shape, F32) for sh...]
  transfers between devices with their start and end apart: 39 -> 39, of which waited for: 17 -> 18; matrix products, arithmetic and copies ran while one was open for 4% -> 3% of each run, Pallas kernels for 10% -> 10%
where the time goes in v4:
time: 142 us
  starting transfers between devices  57.1 us (40%)
  waiting for transfers between devices  46.3 us (33%)
  Pallas kernels  24.1 us (17%)
  local copies, waits for them, and re-layouts  13 us (9%)
    ppermute x30, starting transfers between devices, up(): return lax.ppermute(array, 'col', [(c, moved(c)) for c in range(COLS_AXIS)])  45.8 us
    ppermute x30, waiting for transfers between devices, up(): return lax.ppermute(array, 'col', [(c, moved(c)) for c in range(COLS_AXIS)])  33.9 us
    pallas_call x12, Pallas kernels, call(): pl.pallas_call(kernel, out_shape=[jax.ShapeDtypeStruct(shape, F32) for sh...  24.1 us
    ppermute x6, waiting for transfers between devices, up_z(): lax.ppermute(array, 'row', [(r, (r + 2 * by) % ROWS_AXIS) for r in range(...  11.2 us
    ppermute x6, starting transfers between devices, up_z(): lax.ppermute(array, 'row', [(r, (r + 2 * by) % ROWS_AXIS) for r in range(...  11.1 us
    unnamed x24, local copies, waits for them, and re-layouts  4.61 us
    dynamic_slice x1, local copies, waits for them, and re-layouts, quarter_of(): lax.dynamic_slice(factor, (0, NB + FIRST[half] + (place[2 + half] + by) %...  3.68 us
  transfers between devices with their start and end apart: 39, of which 18 were waited for; matrix products, arithmetic and copies ran while one was open for 3% of the time, Pallas kernels for 10%

profile of v4, /device:TPU:8, one launch (start us, length us, event | category | flops | bytes accessed | tf_op | source)
XLA Modules:
  0.0 141.6 jit_solution(16298475698355805427)
XLA Ops:
  0.8 3.7 %constant_dynamic-slice_fusion.1 = (f32[128,1536]{1,0:T(8,128)}, f32[128,1536]{1,0:T(8,128)}, f32[128,1536]{1,0:T(8,128)}, f32[128,1536]{1,0:T(8,128)}) fusion(f32[128,12288]{1,0:T(8,128)} %bitcast.11, s32[]{:T(128)S(6)} %select_n.71, s32[]{:T(128)S(6)} %select_n.69, s32[]{:T(128)S(6)} %select_n.67, s32[]{:T(128)S(6)} %select_n.65), kind=kLoop, calls=%fused_computation.4 | loop fusion | bytes 6291472 | tf_op jit(solution)/shard_map/dynamic_slice | solution.py:360
  4.4 1.6 %collective-permute-start.4 = (f32[128,1536]{1,0:T(8,128)}, f32[128,1536]{1,0:T(8,128)S(1)}, u32[]{:S(2)}, u32[]{:S(2)}) collective-permute-start(f32[128,1536]{1,0:T(8,128)} %get-tuple-element.92), channel_id=1, source_target_pairs={{0,4},{1,5},{2,6},{3,7},{4,8},{5,9},{6,10},{7,11},{8,12},{9,13},{1... | collective-permute-start | bytes 2359304 | tf_op jit(solution)/shard_map/ppermute | solution.py:337
  6.0 1.5 %collective-permute-start.5 = (f32[128,1536]{1,0:T(8,128)}, f32[128,1536]{1,0:T(8,128)}, u32[]{:S(2)}, u32[]{:S(2)}) collective-permute-start(f32[128,1536]{1,0:T(8,128)} %get-tuple-element.91), channel_id=1, source_target_pairs={{0,1},{1,2},{2,3},{3,0},{4,5},{5,6},{6,7},{7,4},{8,9},{9,10},{10,1... | collective-permute-start | bytes 2359304 | tf_op jit(solution)/shard_map/ppermute | solution.py:337
  8.0 1.7 %collective-permute-start.7 = (f32[128,1536]{1,0:T(8,128)}, f32[128,1536]{1,0:T(8,128)}, u32[]{:S(2)}, u32[]{:S(2)}) collective-permute-start(f32[128,1536]{1,0:T(8,128)} %get-tuple-element.89), channel_id=1, source_target_pairs={{0,3},{1,0},{2,1},{3,2},{4,7},{5,4},{6,5},{7,6},{8,11},{9,8},{10,9... | collective-permute-start | bytes 2359304 | tf_op jit(solution)/shard_map/ppermute | solution.py:337
  9.7 0.8 slice.8
  10.7 1.2 collective-permute-done
  11.9 2.0 %collective-permute-start.1 = (f32[136,128]{1,0:T(8,128)S(1)}, f32[136,128]{1,0:T(8,128)S(1)}, u32[]{:S(2)}, u32[]{:S(2)}) collective-permute-start(f32[136,128]{1,0:T(8,128)S(1)} %pad_maximum_fusion.own_ref), channel_id=1, source_target_pairs={{0,32},{16,48},{32,64},{48,80},{64,96},{80,112},{96,0},{112,16},{1... | collective-permute-start | bytes 208904 | tf_op jit(solution)/shard_map/ppermute | solution.py:329
  13.8 4.6 %collective-permute-done.1.one_ref = f32[136,128]{1,0:T(8,128)S(1)} collective-permute-done((f32[136,128]{1,0:T(8,128)S(1)}, f32[136,128]{1,0:T(8,128)S(1)}, u32[]{:S(2)}, u32[]{:S(2)}) %collective-permute-start.1) | collective-permute-done | bytes 69664 | tf_op jit(solution)/shard_map/ppermute | solution.py:329
  18.5 1.6 %collective-permute-start.2 = (f32[136,128]{1,0:T(8,128)S(1)}, f32[136,128]{1,0:T(8,128)}, u32[]{:S(2)}, u32[]{:S(2)}) collective-permute-start(f32[136,128]{1,0:T(8,128)S(1)} %pad_maximum_fusion.own_ref), channel_id=1, source_target_pairs={{0,64},{16,80},{32,96},{48,112},{64,0},{80,16},{96,32},{112,48},{1... | collective-permute-start | bytes 208904 | tf_op jit(solution)/shard_map/ppermute | solution.py:329
  20.1 1.9 %reshape.24.ta_ref = f32[8,12160]{1,0:T(8,128)} reshape(f32[2,4,12160]{2,1,0:T(4,128)} %param.8) | data formatting | bytes 778240 | tf_op jit(solution)/shard_map/reshape | solution.py:380
  22.0 2.4 %collective-permute-done.2.two_ref = f32[136,128]{1,0:T(8,128)} collective-permute-done((f32[136,128]{1,0:T(8,128)S(1)}, f32[136,128]{1,0:T(8,128)}, u32[]{:S(2)}, u32[]{:S(2)}) %collective-permute-start.2) | collective-permute-done | bytes 69664 | tf_op jit(solution)/shard_map/ppermute | solution.py:329
  24.4 1.8 %collective-permute-start.3 = (f32[136,128]{1,0:T(8,128)S(1)}, f32[136,128]{1,0:T(8,128)S(1)}, u32[]{:S(2)}, u32[]{:S(2)}) collective-permute-start(f32[136,128]{1,0:T(8,128)S(1)} %pad_maximum_fusion.own_ref), channel_id=1, source_target_pairs={{0,96},{16,112},{32,0},{48,16},{64,32},{80,48},{96,64},{112,80},{1... | collective-permute-start | bytes 208904 | tf_op jit(solution)/shard_map/ppermute | solution.py:329
  26.3 2.4 %collective-permute-done.3.three_ref = f32[136,128]{1,0:T(8,128)S(1)} collective-permute-done((f32[136,128]{1,0:T(8,128)S(1)}, f32[136,128]{1,0:T(8,128)S(1)}, u32[]{:S(2)}, u32[]{:S(2)}) %collective-permute-start.3) | collective-permute-done | bytes 69664 | tf_op jit(solution)/shard_map/ppermute | solution.py:329
  28.7 1.0 copy-done.7
  29.7 1.1 pack.1
  30.8 1.6 %collective-permute-start.8 = (f32[28,8,128]{2,1,0:T(8,128)S(1)}, f32[28,8,128]{2,1,0:T(8,128)S(1)}, u32[]{:S(2)}, u32[]{:S(2)}) collective-permute-start(f32[28,8,128]{2,1,0:T(8,128)S(1)} %get-tuple-element.47), channel_id=1, source_target_pairs={{0,4},{1,5},{2,6},{3,7},{4,8},{5,9},{6,10},{7,11},{8,12},{9,13},{1... | collective-permute-start | bytes 344072 | tf_op jit(solution)/shard_map/ppermute | solution.py:337
  32.4 2.2 %collective-permute-start.9 = (f32[28,8,128]{2,1,0:T(8,128)S(1)}, f32[28,8,128]{2,1,0:T(8,128)S(1)}, u32[]{:S(2)}, u32[]{:S(2)}) collective-permute-start(f32[28,8,128]{2,1,0:T(8,128)S(1)} %get-tuple-element.48), channel_id=1, source_target_pairs={{0,8},{1,9},{2,10},{3,11},{4,12},{5,13},{6,14},{7,15},{8,0},{9,1},... | collective-permute-start | bytes 344072 | tf_op jit(solution)/shard_map/ppermute | solution.py:337
  34.6 1.2 collective-permute-start.10
  36.1 2.7 %collective-permute-start.12 = (f32[28,8,128]{2,1,0:T(8,128)S(1)}, f32[28,8,128]{2,1,0:T(8,128)S(1)}, u32[]{:S(2)}, u32[]{:S(2)}) collective-permute-start(f32[28,8,128]{2,1,0:T(8,128)S(1)} %get-tuple-element.52), channel_id=1, source_target_pairs={{0,2},{1,3},{2,0},{3,1},{4,6},{5,7},{6,4},{7,5},{8,10},{9,11},{10,... | collective-permute-start | bytes 344072 | tf_op jit(solution)/shard_map/ppermute | solution.py:337
  38.8 1.4 %collective-permute-start.13 = (f32[28,8,128]{2,1,0:T(8,128)S(1)}, f32[28,8,128]{2,1,0:T(8,128)S(1)}, u32[]{:S(2)}, u32[]{:S(2)}) collective-permute-start(f32[28,8,128]{2,1,0:T(8,128)S(1)} %get-tuple-element.53), channel_id=1, source_target_pairs={{0,3},{1,0},{2,1},{3,2},{4,7},{5,4},{6,5},{7,6},{8,11},{9,8},{10,9... | collective-permute-start | bytes 344072 | tf_op jit(solution)/shard_map/ppermute | solution.py:337
  40.2 2.8 %collective-permute-done.11.refs_5_ = f32[28,8,128]{2,1,0:T(8,128)S(1)} collective-permute-done((f32[28,8,128]{2,1,0:T(8,128)S(1)}, f32[28,8,128]{2,1,0:T(8,128)S(1)}, u32[]{:S(2)}, u32[]{:S(2)}) %collective-permute-start.11) | collective-permute-done | bytes 114720 | tf_op jit(solution)/shard_map/ppermute | solution.py:337
  43.0 0.9 collective-permute-done.13.refs_7_
  43.9 1.3 collective-permute-start.14
  45.2 2.9 %collective-permute-start.15 = (f32[4,28,8,128]{3,2,1,0:T(8,128)S(1)}, f32[4,28,8,128]{3,2,1,0:T(8,128)S(1)}, u32[]{:S(2)}, u32[]{:S(2)}) collective-permute-start(f32[4,28,8,128]{3,2,1,0:T(8,128)S(1)} %get-tuple-element.54.refs_0_), channel_id=1, source_target_pairs={{0,2},{1,3},{2,0},{3,1},{4,6},{5,7},{6,4},{7,5},{8,10},{9,11},{10,... | collective-permute-start | bytes 1376264 | tf_op jit(solution)/shard_map/ppermute | solution.py:337
  48.5 0.8 collective-permute-start.17
  49.3 2.6 %collective-permute-start.18 = (f32[4,28,8,128]{3,2,1,0:T(8,128)S(1)}, f32[4,28,8,128]{3,2,1,0:T(8,128)S(1)}, u32[]{:S(2)}, u32[]{:S(2)}) collective-permute-start(f32[4,28,8,128]{3,2,1,0:T(8,128)S(1)} %get-tuple-element.55.refs_4_), channel_id=1, source_target_pairs={{0,8},{1,9},{2,10},{3,11},{4,12},{5,13},{6,14},{7,15},{8,0},{9,1},... | collective-permute-start | bytes 1376264 | tf_op jit(solution)/shard_map/ppermute | solution.py:337
  51.9 6.7 %collective-permute-done.14.refs_1_.refs_0_ = f32[4,28,8,128]{3,2,1,0:T(8,128)S(1)} collective-permute-done((f32[4,28,8,128]{3,2,1,0:T(8,128)S(1)}, f32[4,28,8,128]{3,2,1,0:T(8,128)S(1)}, u32[]{:S(2)}, u32[]{:S(2)}) %collective-permute-start.14) | collective-permute-done | bytes 458784 | tf_op jit(solution)/shard_map/ppermute | solution.py:337
  58.6 1.3 collective-permute-start.19
  60.0 4.0 %collective-permute-done.15.refs_2_ = f32[4,28,8,128]{3,2,1,0:T(8,128)S(1)} collective-permute-done((f32[4,28,8,128]{3,2,1,0:T(8,128)S(1)}, f32[4,28,8,128]{3,2,1,0:T(8,128)S(1)}, u32[]{:S(2)}, u32[]{:S(2)}) %collective-permute-start.15) | collective-permute-done | bytes 458784 | tf_op jit(solution)/shard_map/ppermute | solution.py:337
  64.0 3.8 %collective-permute-done.19.refs_7_ = f32[4,28,8,128]{3,2,1,0:T(8,128)S(1)} collective-permute-done((f32[4,28,8,128]{3,2,1,0:T(8,128)S(1)}, f32[4,28,8,128]{3,2,1,0:T(8,128)S(1)}, u32[]{:S(2)}, u32[]{:S(2)}) %collective-permute-start.19) | collective-permute-done | bytes 458784 | tf_op jit(solution)/shard_map/ppermute | solution.py:337
  68.2 0.8 cut.1
  69.1 2.6 %collective-permute-start.21 = (f32[128,1536]{1,0:T(8,128)S(1)}, f32[128,1536]{1,0:T(8,128)S(1)}, u32[]{:S(2)}, u32[]{:S(2)}) collective-permute-start(f32[128,1536]{1,0:T(8,128)S(1)} %get-tuple-element.67), channel_id=1, source_target_pairs={{0,8},{1,9},{2,10},{3,11},{4,12},{5,13},{6,14},{7,15},{8,0},{9,1},... | collective-permute-start | bytes 2359304 | tf_op jit(solution)/shard_map/ppermute | solution.py:337
  71.7 1.5 %collective-permute-start.22 = (f32[128,1536]{1,0:T(8,128)S(1)}, f32[128,1536]{1,0:T(8,128)S(1)}, u32[]{:S(2)}, u32[]{:S(2)}) collective-permute-start(f32[128,1536]{1,0:T(8,128)S(1)} %get-tuple-element.68), channel_id=1, source_target_pairs={{0,2},{1,3},{2,0},{3,1},{4,6},{5,7},{6,4},{7,5},{8,10},{9,11},{10,... | collective-permute-start | bytes 2359304 | tf_op jit(solution)/shard_map/ppermute | solution.py:337
  73.2 4.6 %forward.1 = (f32[128,512]{1,0:T(8,128)S(1)}, f32[128,512]{1,0:T(8,128)S(1)}, f32[2,4,1024]{2,1,0:T(4,128)}) custom-call(s32[4]{0:T(128)S(1)} %pad_add_fusion.place_ref, f32[32,16,8,128]{3,2,1,0:T(8,128)S(1)} %get-tuple-element.56.mine_ref.refs_0_, f32[32,16,8,128]{3,2,1,0:T(8,128)S(1)} %collective-permute-done.20.other_ref.refs_1_, ...), custom_call_target="tpu_custom_call" | custom-call | bytes 21000000 | tf_op jit(solution)/shard_map/forward/pallas_call | solution.py:312
  77.8 5.7 %early.1 = (f32[4,4,32,128]{3,2,1,0:T(8,128)S(1)}, f32[128,1536]{1,0:T(8,128)S(1)}, f32[128,1536]{1,0:T(8,128)S(1)}) custom-call(s32[4]{0:T(128)S(1)} %pad_add_fusion.place_ref, f32[128,512]{1,0:T(8,128)S(1)} %get-tuple-element.58.refs_0_, f32[128,512]{1,0:T(8,128)S(1)} %get-tuple-element.59.refs_1_, f32[128,1536]{1,0:T(8,128)S(1)} %get-tuple-element.60.refs_2_, ...), custom_call_target="tpu_custom_call" | custom-call | bytes 21000000 | tf_op jit(solution)/shard_map/early/pallas_call | solution.py:312
  83.5 7.1 %collective-permute-done.21.refs_7_ = f32[128,1536]{1,0:T(8,128)S(1)} collective-permute-done((f32[128,1536]{1,0:T(8,128)S(1)}, f32[128,1536]{1,0:T(8,128)S(1)}, u32[]{:S(2)}, u32[]{:S(2)}) %collective-permute-start.21) | collective-permute-done | bytes 786464 | tf_op jit(solution)/shard_map/ppermute | solution.py:337
  90.6 2.3 %collective-permute-done.22.refs_8_ = f32[128,1536]{1,0:T(8,128)S(1)} collective-permute-done((f32[128,1536]{1,0:T(8,128)S(1)}, f32[128,1536]{1,0:T(8,128)S(1)}, u32[]{:S(2)}, u32[]{:S(2)}) %collective-permute-start.22) | collective-permute-done | bytes 786464 | tf_op jit(solution)/shard_map/ppermute | solution.py:337
  92.8 3.0 %late.1 = (f32[32,1536]{1,0:T(8,128)S(1)}, f32[32,1536]{1,0:T(8,128)S(1)}, f32[32,1536]{1,0:T(8,128)}, f32[32,1536]{1,0:T(8,128)}, f32[32,2048]{1,0:T(8,128)S(1)...) custom-call(s32[4]{0:T(128)S(1)} %pad_add_fusion.place_ref, ...), custom_call_target="tpu_custom_call" | custom-call | bytes 10500000 | tf_op jit(solution)/shard_map/late/pallas_call | solution.py:312
  95.9 1.0 collective-permute-start.23
  97.0 1.4 collective-permute-start.27
  98.3 2.1 %collective-permute-start.28 = (f32[32,2048]{1,0:T(8,128)}, f32[32,2048]{1,0:T(8,128)}, u32[]{:S(2)}, u32[]{:S(2)}) collective-permute-start(f32[32,2048]{1,0:T(8,128)} %get-tuple-element.76), channel_id=1, source_target_pairs={{0,4},{1,5},{2,6},{3,7},{4,8},{5,9},{6,10},{7,11},{8,12},{9,13},{1... | collective-permute-start | bytes 786440 | tf_op jit(solution)/shard_map/ppermute | solution.py:337
  100.4 2.6 %collective-permute-start.24 = (f32[32,1536]{1,0:T(8,128)}, f32[32,1536]{1,0:T(8,128)}, u32[]{:S(2)}, u32[]{:S(2)}) collective-permute-start(f32[32,1536]{1,0:T(8,128)} %get-tuple-element.71), channel_id=1, source_target_pairs={{0,2},{1,3},{2,0},{3,1},{4,6},{5,7},{6,4},{7,5},{8,10},{9,11},{10,... | collective-permute-start | bytes 589832 | tf_op jit(solution)/shard_map/ppermute | solution.py:337
  103.6 0.6 constant_dynamic-slice_fusion
  104.2 1.4 reshape.25.refs_3_
  105.6 1.6 %copy-done.4 = f32[32,16,8,128]{3,2,1,0:T(8,128)S(1)} copy-done((f32[32,16,8,128]{3,2,1,0:T(8,128)S(1)}, f32[32,16,8,128]{3,2,1,0:T(8,128)}, u32[]{:S(2)}) %copy-start.4) | copy-done | bytes 2097176
  107.2 1.2 copy-done.6
  108.4 0.8 copy-done.9
  109.6 2.0 %collective-permute-done.25.refs_3_ = f32[32,1536]{1,0:T(8,128)} collective-permute-done((f32[32,1536]{1,0:T(8,128)}, f32[32,1536]{1,0:T(8,128)}, u32[]{:S(2)}, u32[]{:S(2)}) %collective-permute-start.25) | collective-permute-done | bytes 196640 | tf_op jit(solution)/shard_map/ppermute | solution.py:337
  111.9 1.4 middle.1
  113.3 1.1 collective-permute-start.32
  114.5 2.0 %collective-permute-start.33 = (f32[8,4096]{1,0:T(8,128)S(1)}, f32[8,4096]{1,0:T(8,128)S(1)}, u32[]{:S(2)}, u32[]{:S(2)}) collective-permute-start(f32[8,4096]{1,0:T(8,128)S(1)} %get-tuple-element.84), channel_id=1, source_target_pairs={{0,2},{1,3},{2,0},{3,1},{4,6},{5,7},{6,4},{7,5},{8,10},{9,11},{10,... | collective-permute-start | bytes 393224 | tf_op jit(solution)/shard_map/ppermute | solution.py:337
  116.5 0.9 collective-permute-start.34
  117.4 1.5 %collective-permute-start.29 = (f32[8,1536]{1,0:T(8,128)S(1)}, f32[8,1536]{1,0:T(8,128)S(1)}, u32[]{:S(2)}, u32[]{:S(2)}) collective-permute-start(f32[8,1536]{1,0:T(8,128)S(1)} %get-tuple-element.79), channel_id=1, source_target_pairs={{0,12},{1,13},{2,14},{3,15},{4,0},{5,1},{6,2},{7,3},{8,4},{9,5},{1... | collective-permute-start | bytes 147464 | tf_op jit(solution)/shard_map/ppermute | solution.py:337
  119.1 2.3 %collective-permute-done.33.refs_2_.refs_6_ = f32[8,4096]{1,0:T(8,128)S(1)} collective-permute-done((f32[8,4096]{1,0:T(8,128)S(1)}, f32[8,4096]{1,0:T(8,128)S(1)}, u32[]{:S(2)}, u32[]{:S(2)}) %collective-permute-start.33) | collective-permute-done | bytes 131104 | tf_op jit(solution)/shard_map/ppermute | solution.py:337
  121.5 1.4 collective-permute-done.34.refs_3_.refs_7_
  122.9 0.8 last.1.refs_8_
  123.8 2.2 %collective-permute-start.30 = (f32[8,1536]{1,0:T(8,128)S(1)}, f32[8,1536]{1,0:T(8,128)S(1)}, u32[]{:S(2)}, u32[]{:S(2)}) collective-permute-start(f32[8,1536]{1,0:T(8,128)S(1)} %get-tuple-element.80), channel_id=1, source_target_pairs={{0,8},{1,9},{2,10},{3,11},{4,12},{5,13},{6,14},{7,15},{8,0},{9,1},... | collective-permute-start | bytes 147464 | tf_op jit(solution)/shard_map/ppermute | solution.py:337
  126.0 2.2 %collective-permute-start.31 = (f32[8,1536]{1,0:T(8,128)S(1)}, f32[8,1536]{1,0:T(8,128)S(1)}, u32[]{:S(2)}, u32[]{:S(2)}) collective-permute-start(f32[8,1536]{1,0:T(8,128)S(1)} %get-tuple-element.81), channel_id=1, source_target_pairs={{0,4},{1,5},{2,6},{3,7},{4,8},{5,9},{6,10},{7,11},{8,12},{9,13},{1... | collective-permute-start | bytes 147464 | tf_op jit(solution)/shard_map/ppermute | solution.py:337
  128.2 1.1 collective-permute-start.36
  129.3 3.8 %collective-permute-start.37 = (f32[8,8,128]{2,1,0:T(8,128)S(1)}, f32[8,8,128]{2,1,0:T(8,128)S(1)}, u32[]{:S(2)}, u32[]{:S(2)}) collective-permute-start(f32[8,8,128]{2,1,0:T(8,128)S(1)} %add.101.refs_0_), channel_id=1, source_target_pairs={{0,64},{16,80},{32,96},{48,112},{64,0},{80,16},{96,32},{112,48},{1... | collective-permute-start | bytes 98312 | tf_op jit(solution)/shard_map/ppermute | solution.py:329
  133.1 0.8 collective-permute-start.38
  133.9 1.4 finish.1
  135.3 1.7 %collective-permute-done.38.refs_3_ = f32[8,8,128]{2,1,0:T(8,128)S(1)} collective-permute-done((f32[8,8,128]{2,1,0:T(8,128)S(1)}, f32[8,8,128]{2,1,0:T(8,128)S(1)}, u32[]{:S(2)}, u32[]{:S(2)}) %collective-permute-start.38) | collective-permute-done | bytes 32800 | tf_op jit(solution)/shard_map/ppermute | solution.py:329
  137.0 4.6 %backward.1 = f32[2,4,1024]{2,1,0:T(4,128)} custom-call(s32[4]{0:T(128)S(1)} %pad_add_fusion.place_ref, f32[8,1024]{1,0:T(8,128)S(1)} %get-tuple-element.86.loads_ref, f32[8,8,128]{2,1,0:T(8,128)S(1)} %add.101.refs_0_, f32[8,8,128]{2,1,0:T(8,128)S(1)} %collective-permute-done.36.refs_1_, f32[8,8,128]{2,1,0:T(8,128)S(1)} %collective-permute-done.37.refs_2_, ...), custom_call_target="tpu_custom_call" | custom-call | bytes 21000000 | tf_op jit(solution)/shard_map/backward/pallas_call | solution.py:312
  (62 shorter events, 3.7 us)
Async XLA Ops:
  0.6 102.9 %copy-start = (f32[2,64,1024]{2,1,0:T(8,128)S(1)}, f32[2,64,1024]{2,1,0:T(8,128)}, u32[]{:S(2)}) copy-start(f32[2,64,1024]{2,1,0:T(8,128)} %param.9) | copy-start | bytes 1572868
  0.7 11.1 %slice-start.2 = ((f32[2,4,12288]{2,1,0:T(4,128)}), f32[2,4,128]{2,1,0:T(4,128)S(1)}, s32[]{:S(2)}) async-start(f32[2,4,12288]{2,1,0:T(4,128)} %loads_ref.1), calls=%async_computation.2 | async-start | bytes 8192 | tf_op jit(solution)/shard_map/slice | solution.py:371
  0.8 67.5 %slice-start = ((s8[6291456]{0:T(1024)(128)(4,1)}), s8[2097152]{0:T(1024)(128)(4,1)S(1)}, s32[]{:S(2)}) async-start(s8[6291456]{0:T(1024)(128)(4,1)} %bitcast.13), calls=%async_computation | async-start | bytes 4194304
  4.4 24.3 %collective-permute-start.4 = (f32[128,1536]{1,0:T(8,128)}, f32[128,1536]{1,0:T(8,128)S(1)}, u32[]{:S(2)}, u32[]{:S(2)}) collective-permute-start(f32[128,1536]{1,0:T(8,128)} %get-tuple-element.92), channel_id=1, source_target_pairs={{0,4},{1,5},{2,6},{3,7},{4,8},{5,9},{6,10},{7,11},{8,12},{9,13},{1... | collective-permute-start | bytes 2359304 | tf_op jit(solution)/shard_map/ppermute | solution.py:337
  6.0 22.7 %collective-permute-start.5 = (f32[128,1536]{1,0:T(8,128)}, f32[128,1536]{1,0:T(8,128)}, u32[]{:S(2)}, u32[]{:S(2)}) collective-permute-start(f32[128,1536]{1,0:T(8,128)} %get-tuple-element.91), channel_id=1, source_target_pairs={{0,1},{1,2},{2,3},{3,0},{4,5},{5,6},{6,7},{7,4},{8,9},{9,10},{10,1... | collective-permute-start | bytes 2359304 | tf_op jit(solution)/shard_map/ppermute | solution.py:337
  7.5 21.2 %collective-permute-start.6 = (f32[128,1536]{1,0:T(8,128)}, f32[128,1536]{1,0:T(8,128)}, u32[]{:S(2)}, u32[]{:S(2)}) collective-permute-start(f32[128,1536]{1,0:T(8,128)} %get-tuple-element.90), channel_id=1, source_target_pairs={{0,12},{1,13},{2,14},{3,15},{4,0},{5,1},{6,2},{7,3},{8,4},{9,5},{1... | collective-permute-start | bytes 2359304 | tf_op jit(solution)/shard_map/ppermute | solution.py:337
  8.0 20.8 %collective-permute-start.7 = (f32[128,1536]{1,0:T(8,128)}, f32[128,1536]{1,0:T(8,128)}, u32[]{:S(2)}, u32[]{:S(2)}) collective-permute-start(f32[128,1536]{1,0:T(8,128)} %get-tuple-element.89), channel_id=1, source_target_pairs={{0,3},{1,0},{2,1},{3,2},{4,7},{5,4},{6,5},{7,6},{8,11},{9,8},{10,9... | collective-permute-start | bytes 2359304 | tf_op jit(solution)/shard_map/ppermute | solution.py:337
  10.6 1.3 collective-permute-start
  11.9 6.6 %collective-permute-start.1 = (f32[136,128]{1,0:T(8,128)S(1)}, f32[136,128]{1,0:T(8,128)S(1)}, u32[]{:S(2)}, u32[]{:S(2)}) collective-permute-start(f32[136,128]{1,0:T(8,128)S(1)} %pad_maximum_fusion.own_ref), channel_id=1, source_target_pairs={{0,32},{16,48},{32,64},{48,80},{64,96},{80,112},{96,0},{112,16},{1... | collective-permute-start | bytes 208904 | tf_op jit(solution)/shard_map/ppermute | solution.py:329
  18.5 5.9 %collective-permute-start.2 = (f32[136,128]{1,0:T(8,128)S(1)}, f32[136,128]{1,0:T(8,128)}, u32[]{:S(2)}, u32[]{:S(2)}) collective-permute-start(f32[136,128]{1,0:T(8,128)S(1)} %pad_maximum_fusion.own_ref), channel_id=1, source_target_pairs={{0,64},{16,80},{32,96},{48,112},{64,0},{80,16},{96,32},{112,48},{1... | collective-permute-start | bytes 208904 | tf_op jit(solution)/shard_map/ppermute | solution.py:329
  24.4 4.3 %collective-permute-start.3 = (f32[136,128]{1,0:T(8,128)S(1)}, f32[136,128]{1,0:T(8,128)S(1)}, u32[]{:S(2)}, u32[]{:S(2)}) collective-permute-start(f32[136,128]{1,0:T(8,128)S(1)} %pad_maximum_fusion.own_ref), channel_id=1, source_target_pairs={{0,96},{16,112},{32,0},{48,16},{64,32},{80,48},{96,64},{112,80},{1... | collective-permute-start | bytes 208904 | tf_op jit(solution)/shard_map/ppermute | solution.py:329
  26.3 42.0 %slice-start.1 = ((s8[6291456]{0:T(1024)(128)(4,1)}), s8[4194304]{0:T(1024)(128)(4,1)S(1)}, s32[]{:S(2)}) async-start(s8[6291456]{0:T(1024)(128)(4,1)} %bitcast.13), calls=%async_computation.1 | async-start | bytes 8388608
  28.7 1.0 copy-start.7
  30.8 8.0 %collective-permute-start.8 = (f32[28,8,128]{2,1,0:T(8,128)S(1)}, f32[28,8,128]{2,1,0:T(8,128)S(1)}, u32[]{:S(2)}, u32[]{:S(2)}) collective-permute-start(f32[28,8,128]{2,1,0:T(8,128)S(1)} %get-tuple-element.47), channel_id=1, source_target_pairs={{0,4},{1,5},{2,6},{3,7},{4,8},{5,9},{6,10},{7,11},{8,12},{9,13},{1... | collective-permute-start | bytes 344072 | tf_op jit(solution)/shard_map/ppermute | solution.py:337
  32.4 7.8 %collective-permute-start.9 = (f32[28,8,128]{2,1,0:T(8,128)S(1)}, f32[28,8,128]{2,1,0:T(8,128)S(1)}, u32[]{:S(2)}, u32[]{:S(2)}) collective-permute-start(f32[28,8,128]{2,1,0:T(8,128)S(1)} %get-tuple-element.48), channel_id=1, source_target_pairs={{0,8},{1,9},{2,10},{3,11},{4,12},{5,13},{6,14},{7,15},{8,0},{9,1},... | collective-permute-start | bytes 344072 | tf_op jit(solution)/shard_map/ppermute | solution.py:337
  34.6 5.7 %collective-permute-start.10 = (f32[28,8,128]{2,1,0:T(8,128)S(1)}, f32[28,8,128]{2,1,0:T(8,128)S(1)}, u32[]{:S(2)}, u32[]{:S(2)}) collective-permute-start(f32[28,8,128]{2,1,0:T(8,128)S(1)} %get-tuple-element.49), channel_id=1, source_target_pairs={{0,12},{1,13},{2,14},{3,15},{4,0},{5,1},{6,2},{7,3},{8,4},{9,5},{1... | collective-permute-start | bytes 344072 | tf_op jit(solution)/shard_map/ppermute | solution.py:337
  35.8 7.2 %collective-permute-start.11 = (f32[28,8,128]{2,1,0:T(8,128)S(1)}, f32[28,8,128]{2,1,0:T(8,128)S(1)}, u32[]{:S(2)}, u32[]{:S(2)}) collective-permute-start(f32[28,8,128]{2,1,0:T(8,128)S(1)} %get-tuple-element.51), channel_id=1, source_target_pairs={{0,1},{1,2},{2,3},{3,0},{4,5},{5,6},{6,7},{7,4},{8,9},{9,10},{10,1... | collective-permute-start | bytes 344072 | tf_op jit(solution)/shard_map/ppermute | solution.py:337
  36.1 7.0 %collective-permute-start.12 = (f32[28,8,128]{2,1,0:T(8,128)S(1)}, f32[28,8,128]{2,1,0:T(8,128)S(1)}, u32[]{:S(2)}, u32[]{:S(2)}) collective-permute-start(f32[28,8,128]{2,1,0:T(8,128)S(1)} %get-tuple-element.52), channel_id=1, source_target_pairs={{0,2},{1,3},{2,0},{3,1},{4,6},{5,7},{6,4},{7,5},{8,10},{9,11},{10,... | collective-permute-start | bytes 344072 | tf_op jit(solution)/shard_map/ppermute | solution.py:337
  38.8 5.1 %collective-permute-start.13 = (f32[28,8,128]{2,1,0:T(8,128)S(1)}, f32[28,8,128]{2,1,0:T(8,128)S(1)}, u32[]{:S(2)}, u32[]{:S(2)}) collective-permute-start(f32[28,8,128]{2,1,0:T(8,128)S(1)} %get-tuple-element.53), channel_id=1, source_target_pairs={{0,3},{1,0},{2,1},{3,2},{4,7},{5,4},{6,5},{7,6},{8,11},{9,8},{10,9... | collective-permute-start | bytes 344072 | tf_op jit(solution)/shard_map/ppermute | solution.py:337
  43.9 14.7 %collective-permute-start.14 = (f32[4,28,8,128]{3,2,1,0:T(8,128)S(1)}, f32[4,28,8,128]{3,2,1,0:T(8,128)S(1)}, u32[]{:S(2)}, u32[]{:S(2)}) collective-permute-start(f32[4,28,8,128]{3,2,1,0:T(8,128)S(1)} %get-tuple-element.54.refs_0_), channel_id=1, source_target_pairs={{0,1},{1,2},{2,3},{3,0},{4,5},{5,6},{6,7},{7,4},{8,9},{9,10},{10,1... | collective-permute-start | bytes 1376264 | tf_op jit(solution)/shard_map/ppermute | solution.py:337
  45.2 18.7 %collective-permute-start.15 = (f32[4,28,8,128]{3,2,1,0:T(8,128)S(1)}, f32[4,28,8,128]{3,2,1,0:T(8,128)S(1)}, u32[]{:S(2)}, u32[]{:S(2)}) collective-permute-start(f32[4,28,8,128]{3,2,1,0:T(8,128)S(1)} %get-tuple-element.54.refs_0_), channel_id=1, source_target_pairs={{0,2},{1,3},{2,0},{3,1},{4,6},{5,7},{6,4},{7,5},{8,10},{9,11},{10,... | collective-permute-start | bytes 1376264 | tf_op jit(solution)/shard_map/ppermute | solution.py:337
  48.1 15.8 %collective-permute-start.16 = (f32[4,28,8,128]{3,2,1,0:T(8,128)S(1)}, f32[4,28,8,128]{3,2,1,0:T(8,128)S(1)}, u32[]{:S(2)}, u32[]{:S(2)}) collective-permute-start(f32[4,28,8,128]{3,2,1,0:T(8,128)S(1)} %get-tuple-element.54.refs_0_), channel_id=1, source_target_pairs={{0,3},{1,0},{2,1},{3,2},{4,7},{5,4},{6,5},{7,6},{8,11},{9,8},{10,9... | collective-permute-start | bytes 1376264 | tf_op jit(solution)/shard_map/ppermute | solution.py:337
  48.5 15.5 %collective-permute-start.17 = (f32[4,28,8,128]{3,2,1,0:T(8,128)S(1)}, f32[4,28,8,128]{3,2,1,0:T(8,128)S(1)}, u32[]{:S(2)}, u32[]{:S(2)}) collective-permute-start(f32[4,28,8,128]{3,2,1,0:T(8,128)S(1)} %get-tuple-element.55.refs_4_), channel_id=1, source_target_pairs={{0,4},{1,5},{2,6},{3,7},{4,8},{5,9},{6,10},{7,11},{8,12},{9,13},{1... | collective-permute-start | bytes 1376264 | tf_op jit(solution)/shard_map/ppermute | solution.py:337
  49.3 14.7 %collective-permute-start.18 = (f32[4,28,8,128]{3,2,1,0:T(8,128)S(1)}, f32[4,28,8,128]{3,2,1,0:T(8,128)S(1)}, u32[]{:S(2)}, u32[]{:S(2)}) collective-permute-start(f32[4,28,8,128]{3,2,1,0:T(8,128)S(1)} %get-tuple-element.55.refs_4_), channel_id=1, source_target_pairs={{0,8},{1,9},{2,10},{3,11},{4,12},{5,13},{6,14},{7,15},{8,0},{9,1},... | collective-permute-start | bytes 1376264 | tf_op jit(solution)/shard_map/ppermute | solution.py:337
  58.6 9.1 %collective-permute-start.19 = (f32[4,28,8,128]{3,2,1,0:T(8,128)S(1)}, f32[4,28,8,128]{3,2,1,0:T(8,128)S(1)}, u32[]{:S(2)}, u32[]{:S(2)}) collective-permute-start(f32[4,28,8,128]{3,2,1,0:T(8,128)S(1)} %get-tuple-element.55.refs_4_), channel_id=1, source_target_pairs={{0,12},{1,13},{2,14},{3,15},{4,0},{5,1},{6,2},{7,3},{8,4},{9,5},{1... | collective-permute-start | bytes 1376264 | tf_op jit(solution)/shard_map/ppermute | solution.py:337
  68.1 5.1 %copy-start.1 = (f32[32,16,8,128]{3,2,1,0:T(8,128)}, f32[32,16,8,128]{3,2,1,0:T(8,128)S(1)}, u32[]{:S(2)}) copy-start(f32[32,16,8,128]{3,2,1,0:T(8,128)S(1)} %get-tuple-element.56.mine_ref.refs_0_) | copy-start | bytes 6291460
  68.1 5.1 %copy-start.5 = (f32[2,8,128,128]{3,2,1,0:T(8,128)S(1)}, f32[2,8,128,128]{3,2,1,0:T(8,128)}, u32[]{:S(2)}) copy-start(f32[2,8,128,128]{3,2,1,0:T(8,128)} %refs_2_.1) | copy-start | bytes 3145732
  68.1 5.1 %collective-permute-start.20 = (f32[32,16,8,128]{3,2,1,0:T(8,128)S(1)}, f32[32,16,8,128]{3,2,1,0:T(8,128)S(1)}, u32[]{:S(2)}, u32[]{:S(2)}) collective-permute-start(f32[32,16,8,128]{3,2,1,0:T(8,128)S(1)} %get-tuple-element.56.mine_ref.refs_0_), channel_id=1, source_target_pairs={{0,16},{16,0},{32,48},{48,32},{64,80},{80,64},{96,112},{112,96},{1... | collective-permute-start | bytes 6291464 | tf_op jit(solution)/shard_map/ppermute | solution.py:325
  69.1 21.5 %collective-permute-start.21 = (f32[128,1536]{1,0:T(8,128)S(1)}, f32[128,1536]{1,0:T(8,128)S(1)}, u32[]{:S(2)}, u32[]{:S(2)}) collective-permute-start(f32[128,1536]{1,0:T(8,128)S(1)} %get-tuple-element.67), channel_id=1, source_target_pairs={{0,8},{1,9},{2,10},{3,11},{4,12},{5,13},{6,14},{7,15},{8,0},{9,1},... | collective-permute-start | bytes 2359304 | tf_op jit(solution)/shard_map/ppermute | solution.py:337
  71.7 21.1 %collective-permute-start.22 = (f32[128,1536]{1,0:T(8,128)S(1)}, f32[128,1536]{1,0:T(8,128)S(1)}, u32[]{:S(2)}, u32[]{:S(2)}) collective-permute-start(f32[128,1536]{1,0:T(8,128)S(1)} %get-tuple-element.68), channel_id=1, source_target_pairs={{0,2},{1,3},{2,0},{3,1},{4,6},{5,7},{6,4},{7,5},{8,10},{9,11},{10,... | collective-permute-start | bytes 2359304 | tf_op jit(solution)/shard_map/ppermute | solution.py:337
  73.2 4.6 %copy-start.3 = (f32[32,16,8,128]{3,2,1,0:T(8,128)}, f32[32,16,8,128]{3,2,1,0:T(8,128)S(1)}, u32[]{:S(2)}) copy-start(f32[32,16,8,128]{3,2,1,0:T(8,128)S(1)} %collective-permute-done.20.other_ref.refs_1_) | copy-start | bytes 6291460
  92.8 12.7 %copy-start.2 = (f32[32,16,8,128]{3,2,1,0:T(8,128)S(1)}, f32[32,16,8,128]{3,2,1,0:T(8,128)}, u32[]{:S(2)}) copy-start(f32[32,16,8,128]{3,2,1,0:T(8,128)} %copy-done.1) | copy-start | bytes 6291460
  95.9 7.2 %collective-permute-start.23 = (f32[32,1536]{1,0:T(8,128)S(1)}, f32[32,1536]{1,0:T(8,128)S(1)}, u32[]{:S(2)}, u32[]{:S(2)}) collective-permute-start(f32[32,1536]{1,0:T(8,128)S(1)} %get-tuple-element.70), channel_id=1, source_target_pairs={{0,3},{1,0},{2,1},{3,2},{4,7},{5,4},{6,5},{7,6},{8,11},{9,8},{10,9... | collective-permute-start | bytes 589832 | tf_op jit(solution)/shard_map/ppermute | solution.py:337
  96.8 14.8 %collective-permute-start.26 = (f32[32,2048]{1,0:T(8,128)}, f32[32,2048]{1,0:T(8,128)S(1)}, u32[]{:S(2)}, u32[]{:S(2)}) collective-permute-start(f32[32,2048]{1,0:T(8,128)} %get-tuple-element.74), channel_id=1, source_target_pairs={{0,12},{1,13},{2,14},{3,15},{4,0},{5,1},{6,2},{7,3},{8,4},{9,5},{1... | collective-permute-start | bytes 786440 | tf_op jit(solution)/shard_map/ppermute | solution.py:337
  97.0 14.6 %collective-permute-start.27 = (f32[32,2048]{1,0:T(8,128)}, f32[32,2048]{1,0:T(8,128)}, u32[]{:S(2)}, u32[]{:S(2)}) collective-permute-start(f32[32,2048]{1,0:T(8,128)} %get-tuple-element.75), channel_id=1, source_target_pairs={{0,8},{1,9},{2,10},{3,11},{4,12},{5,13},{6,14},{7,15},{8,0},{9,1},... | collective-permute-start | bytes 786440 | tf_op jit(solution)/shard_map/ppermute | solution.py:337
  98.3 13.6 %collective-permute-start.28 = (f32[32,2048]{1,0:T(8,128)}, f32[32,2048]{1,0:T(8,128)}, u32[]{:S(2)}, u32[]{:S(2)}) collective-permute-start(f32[32,2048]{1,0:T(8,128)} %get-tuple-element.76), channel_id=1, source_target_pairs={{0,4},{1,5},{2,6},{3,7},{4,8},{5,9},{6,10},{7,11},{8,12},{9,13},{1... | collective-permute-start | bytes 786440 | tf_op jit(solution)/shard_map/ppermute | solution.py:337
  100.4 9.2 %collective-permute-start.24 = (f32[32,1536]{1,0:T(8,128)}, f32[32,1536]{1,0:T(8,128)}, u32[]{:S(2)}, u32[]{:S(2)}) collective-permute-start(f32[32,1536]{1,0:T(8,128)} %get-tuple-element.71), channel_id=1, source_target_pairs={{0,2},{1,3},{2,0},{3,1},{4,6},{5,7},{6,4},{7,5},{8,10},{9,11},{10,... | collective-permute-start | bytes 589832 | tf_op jit(solution)/shard_map/ppermute | solution.py:337
  103.0 8.5 %collective-permute-start.25 = (f32[32,1536]{1,0:T(8,128)}, f32[32,1536]{1,0:T(8,128)}, u32[]{:S(2)}, u32[]{:S(2)}) collective-permute-start(f32[32,1536]{1,0:T(8,128)} %get-tuple-element.72), channel_id=1, source_target_pairs={{0,1},{1,2},{2,3},{3,0},{4,5},{5,6},{6,7},{7,4},{8,9},{9,10},{10,1... | collective-permute-start | bytes 589832 | tf_op jit(solution)/shard_map/ppermute | solution.py:337
  105.6 1.6 %copy-start.4 = (f32[32,16,8,128]{3,2,1,0:T(8,128)S(1)}, f32[32,16,8,128]{3,2,1,0:T(8,128)}, u32[]{:S(2)}) copy-start(f32[32,16,8,128]{3,2,1,0:T(8,128)} %copy-done.3) | copy-start | bytes 6291460
  107.2 1.2 copy-start.6
  108.4 0.8 copy-start.9
  111.9 21.9 %copy-start.8 = (f32[2,4,12288]{2,1,0:T(4,128)S(1)}, f32[2,4,12288]{2,1,0:T(4,128)}, u32[]{:S(2)}) copy-start(f32[2,4,12288]{2,1,0:T(4,128)} %loads_ref.1) | copy-start | bytes 1179652
  113.3 5.8 %collective-permute-start.32 = (f32[8,4096]{1,0:T(8,128)S(1)}, f32[8,4096]{1,0:T(8,128)S(1)}, u32[]{:S(2)}, u32[]{:S(2)}) collective-permute-start(f32[8,4096]{1,0:T(8,128)S(1)} %get-tuple-element.83), channel_id=1, source_target_pairs={{0,3},{1,0},{2,1},{3,2},{4,7},{5,4},{6,5},{7,6},{8,11},{9,8},{10,9... | collective-permute-start | bytes 393224 | tf_op jit(solution)/shard_map/ppermute | solution.py:337
  114.5 7.0 %collective-permute-start.33 = (f32[8,4096]{1,0:T(8,128)S(1)}, f32[8,4096]{1,0:T(8,128)S(1)}, u32[]{:S(2)}, u32[]{:S(2)}) collective-permute-start(f32[8,4096]{1,0:T(8,128)S(1)} %get-tuple-element.84), channel_id=1, source_target_pairs={{0,2},{1,3},{2,0},{3,1},{4,6},{5,7},{6,4},{7,5},{8,10},{9,11},{10,... | collective-permute-start | bytes 393224 | tf_op jit(solution)/shard_map/ppermute | solution.py:337
  116.5 6.4 %collective-permute-start.34 = (f32[8,4096]{1,0:T(8,128)S(1)}, f32[8,4096]{1,0:T(8,128)S(1)}, u32[]{:S(2)}, u32[]{:S(2)}) collective-permute-start(f32[8,4096]{1,0:T(8,128)S(1)} %get-tuple-element.85), channel_id=1, source_target_pairs={{0,1},{1,2},{2,3},{3,0},{4,5},{5,6},{6,7},{7,4},{8,9},{9,10},{10,1... | collective-permute-start | bytes 393224 | tf_op jit(solution)/shard_map/ppermute | solution.py:337
  117.4 15.7 %collective-permute-start.29 = (f32[8,1536]{1,0:T(8,128)S(1)}, f32[8,1536]{1,0:T(8,128)S(1)}, u32[]{:S(2)}, u32[]{:S(2)}) collective-permute-start(f32[8,1536]{1,0:T(8,128)S(1)} %get-tuple-element.79), channel_id=1, source_target_pairs={{0,12},{1,13},{2,14},{3,15},{4,0},{5,1},{6,2},{7,3},{8,4},{9,5},{1... | collective-permute-start | bytes 147464 | tf_op jit(solution)/shard_map/ppermute | solution.py:337
  123.7 4.5 %collective-permute-start.35 = (f32[8,8,128]{2,1,0:T(8,128)S(1)}, f32[8,8,128]{2,1,0:T(8,128)S(1)}, u32[]{:S(2)}, u32[]{:S(2)}) collective-permute-start(f32[8,8,128]{2,1,0:T(8,128)S(1)} %last.1.refs_8_), channel_id=1, source_target_pairs={{0,16},{16,0},{32,48},{48,32},{64,80},{80,64},{96,112},{112,96},{1... | collective-permute-start | bytes 98312 | tf_op jit(solution)/shard_map/ppermute | solution.py:325
  123.8 10.1 %collective-permute-start.30 = (f32[8,1536]{1,0:T(8,128)S(1)}, f32[8,1536]{1,0:T(8,128)S(1)}, u32[]{:S(2)}, u32[]{:S(2)}) collective-permute-start(f32[8,1536]{1,0:T(8,128)S(1)} %get-tuple-element.80), channel_id=1, source_target_pairs={{0,8},{1,9},{2,10},{3,11},{4,12},{5,13},{6,14},{7,15},{8,0},{9,1},... | collective-permute-start | bytes 147464 | tf_op jit(solution)/shard_map/ppermute | solution.py:337
  126.0 7.9 %collective-permute-start.31 = (f32[8,1536]{1,0:T(8,128)S(1)}, f32[8,1536]{1,0:T(8,128)S(1)}, u32[]{:S(2)}, u32[]{:S(2)}) collective-permute-start(f32[8,1536]{1,0:T(8,128)S(1)} %get-tuple-element.81), channel_id=1, source_target_pairs={{0,4},{1,5},{2,6},{3,7},{4,8},{5,9},{6,10},{7,11},{8,12},{9,13},{1... | collective-permute-start | bytes 147464 | tf_op jit(solution)/shard_map/ppermute | solution.py:337
  128.2 7.1 %collective-permute-start.36 = (f32[8,8,128]{2,1,0:T(8,128)S(1)}, f32[8,8,128]{2,1,0:T(8,128)S(1)}, u32[]{:S(2)}, u32[]{:S(2)}) collective-permute-start(f32[8,8,128]{2,1,0:T(8,128)S(1)} %add.101.refs_0_), channel_id=1, source_target_pairs={{0,32},{16,48},{32,64},{48,80},{64,96},{80,112},{96,0},{112,16},{1... | collective-permute-start | bytes 98312 | tf_op jit(solution)/shard_map/ppermute | solution.py:329
  129.3 6.0 %collective-permute-start.37 = (f32[8,8,128]{2,1,0:T(8,128)S(1)}, f32[8,8,128]{2,1,0:T(8,128)S(1)}, u32[]{:S(2)}, u32[]{:S(2)}) collective-permute-start(f32[8,8,128]{2,1,0:T(8,128)S(1)} %add.101.refs_0_), channel_id=1, source_target_pairs={{0,64},{16,80},{32,96},{48,112},{64,0},{80,16},{96,32},{112,48},{1... | collective-permute-start | bytes 98312 | tf_op jit(solution)/shard_map/ppermute | solution.py:329
  133.1 3.9 %collective-permute-start.38 = (f32[8,8,128]{2,1,0:T(8,128)S(1)}, f32[8,8,128]{2,1,0:T(8,128)S(1)}, u32[]{:S(2)}, u32[]{:S(2)}) collective-permute-start(f32[8,8,128]{2,1,0:T(8,128)S(1)} %add.101.refs_0_), channel_id=1, source_target_pairs={{0,96},{16,112},{32,0},{48,16},{64,32},{80,48},{96,64},{112,80},{1... | collective-permute-start | bytes 98312 | tf_op jit(solution)/shard_map/ppermute | solution.py:329

commit v5 on v4

--- a/solution.py
+++ b/solution.py
@@ -224,26 +224,20 @@
         out[dy, index, :, half * 64 : half * 64 + 64] = q[dy * 32 : dy * 32 + 32, :64]
 
 
-def early_kernel(place_ref, *refs):
-    zout, touts = refs[-3], refs[-2:]
-    for half in range(2):
-        ta = split(refs[2 + half][...])
+def zsum_kernel(place_ref, *refs):
+    for half in range(2):
+        ta = split(refs[half][...])
+        for by in range(SIDE):
+            zsum_term(place_ref, ta, half, by, refs[2 + half * SIDE + by], refs[-1])
+
+
+def trail_kernel(*refs):
+    zsums, outs = refs[2], refs[-2 * SIDE :]
+    for half in range(2):
         total = None
-        for i, by in enumerate((0, 1, 3)):
-            piece = refs[4 + half * 3 + i]
-            zsum_term(place_ref, ta, half, by, piece, zout)
-            term = trail_term(refs[half], by, piece)
+        for by in range(SIDE):
+            term = trail_term(refs[half], by, refs[3 + half * SIDE + by])
             total = term if total is None else total + term
-        touts[half][...] = total
-
-
-def late_kernel(place_ref, *refs):
-    zin, tins, pieces, outs = refs[4], refs[5:7], refs[7:9], refs[-2 * SIDE - 1 : -1]
-    zsums = refs[-1]
-    zsums[...] = zin[...]
-    for half in range(2):
-        zsum_term(place_ref, split(refs[2 + half][...]), half, 2, pieces[half], zsums)
-        total = tins[half][...] + trail_term(refs[half], 2, pieces[half])
         for by in range(SIDE):
             outs[half * SIDE + by][:, :QUARTER] = -total[by * 32 : by * 32 + 32]
     for dy in range(SIDE):
@@ -380,38 +374,33 @@
         [place, *slabs, trail_adjoint.reshape(8, TRAIL_LOCAL)],
         after=one + three,
     )
-    heard = [to_all(messages[half * SIDE : half * SIDE + SIDE], AXES[half][0]) for half in range(2)]
-    first_lines = call(line_kernel, "line", [(SIDE, MESSAGE, 8, NB)] * 2, heard[0] + heard[1])
-    lines = to_all([first_lines[0]] * SIDE, AXES[0][1]) + to_all([first_lines[1]] * SIDE, AXES[1][1])
-    late = cut(place, factor, (0, 2), [lines[1], lines[5]])
+    late = cut(place, factor, (0, 2), [early[0]])
     two = [up(late[2 * half + 1], AXES[half][0], 2) for half in range(2)]
     pieces = [[late[2 * half], one[half], two[half], three[half]] for half in range(2)]
+    heard = [to_all(messages[half * SIDE : half * SIDE + SIDE], AXES[half][0]) for half in range(2)]
+    first_lines = call(line_kernel, "line", [(SIDE, MESSAGE, 8, NB)] * 2, heard[0] + heard[1], after=two)
+    lines = to_all([first_lines[0]] * SIDE, AXES[0][1]) + to_all([first_lines[1]] * SIDE, AXES[1][1])
     blocks, ta_first, ta_second = call(
         repack_kernel, "repack", [(TILES, COLS_AXIS, 8, NB)] + [(NB, QUARTER)] * 2, lines
     )
     window = (blocks, to_other_core(blocks))
+    (zsums,) = call(
+        zsum_kernel, "zsum", [(SIDE, SIDE, 32, NB)], [place, ta_first, ta_second, *pieces[0], *pieces[1]]
+    )
     *trail_x, sol = call(
         forward_kernel,
         "forward",
         [(NB, SIDE * NB)] * 2 + [(2, PER_COL, STEPS * NB)],
         [place, *window, diag_inverse],
         [pltpu.VMEM((STEPS, NB, NB), F32)] * 2,
+        after=[zsums],
         us=6,
     )
-    zpart, *tparts = call(
-        early_kernel,
-        "early",
-        [(SIDE, SIDE, 32, NB)] + [(NB, QUARTER)] * 2,
-        [place, *trail_x, ta_first, ta_second] + [pieces[half][by] for half in range(2) for by in (0, 1, 3)],
-        us=6,
-    )
     sent = call(
-        late_kernel,
-        "late",
+        trail_kernel,
+        "trail",
         [(32, QUARTER)] * SIDE + [(32, QUARTER + SIDE * NB)] * SIDE,
-        [place, *trail_x, ta_first, ta_second, zpart, *tparts, pieces[0][2], pieces[1][2]],
-        [pltpu.VMEM((SIDE, SIDE, 32, NB), F32)],
-        us=3,
+        [*trail_x, zsums, *pieces[0], *pieces[1]],
     )
     mine = lax.dynamic_slice_in_dim(adjoint_loads, col * PER_COL, PER_COL, 1).reshape(8, STEPS * NB)
     held = call(
@@ -436,12 +425,12 @@
         last_kernel, "last", [(STEPS, 8, NB)], [place, *met[1]], [pltpu.VMEM((COLS_AXIS, 8, NB), F32)]
     )
     zchip = zown + to_other_core(zown)
-    zsums = [zchip] + [up_z(zchip, by) for by in (1, 2, 3)]
+    chips = [zchip] + [up_z(zchip, by) for by in (1, 2, 3)]
     (adj,) = call(
         backward_kernel,
         "backward",
         [(2, PER_COL, STEPS * NB)],
-        [place, held[3], *zsums, *held[:3]],
+        [place, held[3], *chips, *held[:3]],
         [pltpu.VMEM((STEPS, 8, NB), F32)],
         us=6,
     )

time: 142 us -> 155 us (1.092)
  starting transfers between devices: 57.1 us -> 62.2 us
  local copies, waits for them, and re-layouts: 13 us -> 17.8 us
  Pallas kernels: 24.1 us -> 25.9 us
    ppermute x30, waiting for transfers between devices: 33.9 us -> 44.8 us  [up(): return lax.ppermute(array, 'col', [(c, moved(c)) for c in range(COLS_AXIS)])]
    ppermute x6, waiting for transfers between devices: 11.2 us -> 1.42 us  [up_z(): lax.ppermute(array, 'row', [(r, (r + 2 * by) % ROWS_AXIS) for r in range(...]
    unnamed x24 -> x46, local copies, waits for them, and re-layouts: 4.61 us -> 12.4 us
    ppermute x6, starting transfers between devices: 11.1 us -> 14 us  [up_z(): lax.ppermute(array, 'row', [(r, (r + 2 * by) % ROWS_AXIS) for r in range(...]
    pallas_call x12, Pallas kernels: 24.1 us -> 25.9 us  [call(): pl.pallas_call(kernel, out_shape=[jax.ShapeDtypeStruct(shape, F32) for sh...]
    ppermute x30, starting transfers between devices: 45.8 us -> 47.5 us  [up(): return lax.ppermute(array, 'col', [(c, moved(c)) for c in range(COLS_AXIS)])]
  transfers between devices with their start and end apart: 39 -> 39, of which waited for: 18 -> 17; matrix products, arithmetic and copies ran while one was open for 3% -> 1% of each run, Pallas kernels for 10% -> 6%
where the time goes in v5:
time: 155 us; the launch traced here: 154 us
  starting transfers between devices  62.2 us (40%)
  waiting for transfers between devices  47.4 us (31%)
  Pallas kernels  25.9 us (17%)
  local copies, waits for them, and re-layouts  17.8 us (11%)
    ppermute x30, starting transfers between devices, up(): return lax.ppermute(array, 'col', [(c, moved(c)) for c in range(COLS_AXIS)])  47.5 us
    ppermute x30, waiting for transfers between devices, up(): return lax.ppermute(array, 'col', [(c, moved(c)) for c in range(COLS_AXIS)])  44.8 us
    pallas_call x12, Pallas kernels, call(): pl.pallas_call(kernel, out_shape=[jax.ShapeDtypeStruct(shape, F32) for sh...  25.9 us
    ppermute x6, starting transfers between devices, up_z(): lax.ppermute(array, 'row', [(r, (r + 2 * by) % ROWS_AXIS) for r in range(...  14 us
    unnamed x46, local copies, waits for them, and re-layouts  12.4 us
    dynamic_slice x1, local copies, waits for them, and re-layouts, quarter_of(): lax.dynamic_slice(factor, (0, NB + FIRST[half] + (place[2 + half] + by) %...  3.39 us
  transfers between devices with their start and end apart: 39, of which 17 were waited for; matrix products, arithmetic and copies ran while one was open for 1% of the time, Pallas kernels for 6%

profile of v5, /device:TPU:8, one launch (start us, length us, event | category | flops | bytes accessed | tf_op | source)
XLA Modules:
  0.0 154.4 jit_solution(16096721929889443998)
XLA Ops:
  0.8 3.4 %constant_dynamic-slice_fusion.1 = (f32[128,1536]{1,0:T(8,128)}, f32[128,1536]{1,0:T(8,128)}, f32[128,1536]{1,0:T(8,128)}, f32[128,1536]{1,0:T(8,128)S(1)}) fusion(f32[128,12288]{1,0:T(8,128)} %bitcast.11, s32[]{:T(128)S(6)} %select_n.71, s32[]{:T(128)S(6)} %select_n.69, s32[]{:T(128)S(6)} %select_n.67, s32[]{:T(128)S(6)} %select_n.65), kind=kLoop, calls=%fused_computation.4 | loop fusion | bytes 6291472 | tf_op jit(solution)/shard_map/dynamic_slice | solution.py:354
  4.1 1.6 %collective-permute-start.4 = (f32[128,1536]{1,0:T(8,128)S(1)}, f32[128,1536]{1,0:T(8,128)S(1)}, u32[]{:S(2)}, u32[]{:S(2)}) collective-permute-start(f32[128,1536]{1,0:T(8,128)S(1)} %get-tuple-element.86.refs_0_), channel_id=1, source_target_pairs={{0,4},{1,5},{2,6},{3,7},{4,8},{5,9},{6,10},{7,11},{8,12},{9,13},{1... | collective-permute-start | bytes 2359304 | tf_op jit(solution)/shard_map/ppermute | solution.py:331
  5.7 0.8 slice.8
  6.7 1.2 collective-permute-done
  7.9 2.0 %collective-permute-start.1 = (f32[136,128]{1,0:T(8,128)S(1)}, f32[136,128]{1,0:T(8,128)S(1)}, u32[]{:S(2)}, u32[]{:S(2)}) collective-permute-start(f32[136,128]{1,0:T(8,128)S(1)} %pad_maximum_fusion.own_ref), channel_id=1, source_target_pairs={{0,32},{16,48},{32,64},{48,80},{64,96},{80,112},{96,0},{112,16},{1... | collective-permute-start | bytes 208904 | tf_op jit(solution)/shard_map/ppermute | solution.py:323
  9.9 3.6 %collective-permute-start.2 = (f32[136,128]{1,0:T(8,128)S(1)}, f32[136,128]{1,0:T(8,128)S(1)}, u32[]{:S(2)}, u32[]{:S(2)}) collective-permute-start(f32[136,128]{1,0:T(8,128)S(1)} %pad_maximum_fusion.own_ref), channel_id=1, source_target_pairs={{0,64},{16,80},{32,96},{48,112},{64,0},{80,16},{96,32},{112,48},{1... | collective-permute-start | bytes 208904 | tf_op jit(solution)/shard_map/ppermute | solution.py:323
  13.4 1.5 collective-permute-start.5
  15.4 1.9 %collective-permute-start.7 = (f32[128,1536]{1,0:T(8,128)}, f32[128,1536]{1,0:T(8,128)}, u32[]{:S(2)}, u32[]{:S(2)}) collective-permute-start(f32[128,1536]{1,0:T(8,128)} %get-tuple-element.83), channel_id=1, source_target_pairs={{0,3},{1,0},{2,1},{3,2},{4,7},{5,4},{6,5},{7,6},{8,11},{9,8},{10,9... | collective-permute-start | bytes 2359304 | tf_op jit(solution)/shard_map/ppermute | solution.py:331
  17.2 2.5 %collective-permute-start.3 = (f32[136,128]{1,0:T(8,128)S(1)}, f32[136,128]{1,0:T(8,128)S(1)}, u32[]{:S(2)}, u32[]{:S(2)}) collective-permute-start(f32[136,128]{1,0:T(8,128)S(1)} %pad_maximum_fusion.own_ref), channel_id=1, source_target_pairs={{0,96},{16,112},{32,0},{48,16},{64,32},{80,48},{96,64},{112,80},{1... | collective-permute-start | bytes 208904 | tf_op jit(solution)/shard_map/ppermute | solution.py:323
  19.8 2.8 %copy-done.1 = f32[2,1,8,8,12288]{4,3,2,1,0:T(8,128)S(1)} copy-done((f32[2,1,8,8,12288]{4,3,2,1,0:T(8,128)S(1)}, f32[2,1,8,8,12288]{4,3,2,1,0:T(8,128)}, u32[]{:S(2)}) %copy-start.1) | copy-done | bytes 6291480
  22.6 2.1 %cut.1 = (f32[128,1536]{1,0:T(8,128)S(1)}, f32[128,1536]{1,0:T(8,128)}, f32[128,1536]{1,0:T(8,128)S(1)}, f32[128,1536]{1,0:T(8,128)}) custom-call(s32[4]{0:T(128)S(1)} %pad_add_fusion.place_ref, f32[128,12288]{1,0:T(8,128)S(1)} %bitcast.13, f32[128,1536]{1,0:T(8,128)S(1)} %get-tuple-element.86.refs_0_), custom_call_target="tpu_custom_call" | custom-call | bytes 3500000 | tf_op jit(solution)/shard_map/cut/pallas_call | solution.py:306
  24.7 0.9 copy-done.10
  25.6 0.9 copy-done.12
  27.1 0.9 collective-permute-start.14
  28.0 1.6 %collective-permute-start.15 = (f32[128,1536]{1,0:T(8,128)}, f32[128,1536]{1,0:T(8,128)S(1)}, u32[]{:S(2)}, u32[]{:S(2)}) collective-permute-start(f32[128,1536]{1,0:T(8,128)} %get-tuple-element.52), channel_id=1, source_target_pairs={{0,2},{1,3},{2,0},{3,1},{4,6},{5,7},{6,4},{7,5},{8,10},{9,11},{10,... | collective-permute-start | bytes 2359304 | tf_op jit(solution)/shard_map/ppermute | solution.py:331
  29.6 1.1 reshape.24.ta_ref
  30.8 3.7 %collective-permute-done.5.refs_1_.refs_7_.refs_8_ = f32[128,1536]{1,0:T(8,128)} collective-permute-done((f32[128,1536]{1,0:T(8,128)}, f32[128,1536]{1,0:T(8,128)}, u32[]{:S(2)}, u32[]{:S(2)}) %collective-permute-start.5) | collective-permute-done | bytes 786464 | tf_op jit(solution)/shard_map/ppermute | solution.py:331
  35.0 17.3 %collective-permute-done.7.refs_3_.refs_9_.refs_10_ = f32[128,1536]{1,0:T(8,128)} collective-permute-done((f32[128,1536]{1,0:T(8,128)}, f32[128,1536]{1,0:T(8,128)}, u32[]{:S(2)}, u32[]{:S(2)}) %collective-permute-start.7) | collective-permute-done | bytes 786464 | tf_op jit(solution)/shard_map/ppermute | solution.py:331
  52.3 0.9 copy-done.22
  53.2 0.7 pack.1
  54.1 5.6 %collective-permute-start.12 = (f32[28,8,128]{2,1,0:T(8,128)S(1)}, f32[28,8,128]{2,1,0:T(8,128)S(1)}, u32[]{:S(2)}, u32[]{:S(2)}) collective-permute-start(f32[28,8,128]{2,1,0:T(8,128)S(1)} %get-tuple-element.49), channel_id=1, source_target_pairs={{0,2},{1,3},{2,0},{3,1},{4,6},{5,7},{6,4},{7,5},{8,10},{9,11},{10,... | collective-permute-start | bytes 344072 | tf_op jit(solution)/shard_map/ppermute | solution.py:331
  59.7 1.6 %collective-permute-start.8 = (f32[28,8,128]{2,1,0:T(8,128)S(1)}, f32[28,8,128]{2,1,0:T(8,128)S(1)}, u32[]{:S(2)}, u32[]{:S(2)}) collective-permute-start(f32[28,8,128]{2,1,0:T(8,128)S(1)} %get-tuple-element.44), channel_id=1, source_target_pairs={{0,4},{1,5},{2,6},{3,7},{4,8},{5,9},{6,10},{7,11},{8,12},{9,13},{1... | collective-permute-start | bytes 344072 | tf_op jit(solution)/shard_map/ppermute | solution.py:331
  61.4 2.3 %collective-permute-start.9 = (f32[28,8,128]{2,1,0:T(8,128)S(1)}, f32[28,8,128]{2,1,0:T(8,128)S(1)}, u32[]{:S(2)}, u32[]{:S(2)}) collective-permute-start(f32[28,8,128]{2,1,0:T(8,128)S(1)} %get-tuple-element.45), channel_id=1, source_target_pairs={{0,8},{1,9},{2,10},{3,11},{4,12},{5,13},{6,14},{7,15},{8,0},{9,1},... | collective-permute-start | bytes 344072 | tf_op jit(solution)/shard_map/ppermute | solution.py:331
  63.7 0.9 collective-permute-done.12.refs_6_
  64.5 1.2 collective-permute-done.13.refs_7_
  65.7 2.0 %collective-permute-done.9.refs_2_ = f32[28,8,128]{2,1,0:T(8,128)S(1)} collective-permute-done((f32[28,8,128]{2,1,0:T(8,128)S(1)}, f32[28,8,128]{2,1,0:T(8,128)S(1)}, u32[]{:S(2)}, u32[]{:S(2)}) %collective-permute-start.9) | collective-permute-done | bytes 114720 | tf_op jit(solution)/shard_map/ppermute | solution.py:331
  67.8 3.2 %collective-permute-start.16 = (f32[4,28,8,128]{3,2,1,0:T(8,128)S(1)}, f32[4,28,8,128]{3,2,1,0:T(8,128)S(1)}, u32[]{:S(2)}, u32[]{:S(2)}) collective-permute-start(f32[4,28,8,128]{3,2,1,0:T(8,128)S(1)} %get-tuple-element.53.refs_0_), channel_id=1, source_target_pairs={{0,1},{1,2},{2,3},{3,0},{4,5},{5,6},{6,7},{7,4},{8,9},{9,10},{10,1... | collective-permute-start | bytes 1376264 | tf_op jit(solution)/shard_map/ppermute | solution.py:331
  71.1 2.7 %collective-permute-start.18 = (f32[4,28,8,128]{3,2,1,0:T(8,128)S(1)}, f32[4,28,8,128]{3,2,1,0:T(8,128)S(1)}, u32[]{:S(2)}, u32[]{:S(2)}) collective-permute-start(f32[4,28,8,128]{3,2,1,0:T(8,128)S(1)} %get-tuple-element.53.refs_0_), channel_id=1, source_target_pairs={{0,3},{1,0},{2,1},{3,2},{4,7},{5,4},{6,5},{7,6},{8,11},{9,8},{10,9... | collective-permute-start | bytes 1376264 | tf_op jit(solution)/shard_map/ppermute | solution.py:331
  73.8 1.7 %collective-permute-start.19 = (f32[4,28,8,128]{3,2,1,0:T(8,128)S(1)}, f32[4,28,8,128]{3,2,1,0:T(8,128)S(1)}, u32[]{:S(2)}, u32[]{:S(2)}) collective-permute-start(f32[4,28,8,128]{3,2,1,0:T(8,128)S(1)} %get-tuple-element.54.refs_4_), channel_id=1, source_target_pairs={{0,4},{1,5},{2,6},{3,7},{4,8},{5,9},{6,10},{7,11},{8,12},{9,13},{1... | collective-permute-start | bytes 1376264 | tf_op jit(solution)/shard_map/ppermute | solution.py:331
  75.5 3.0 %collective-permute-start.20 = (f32[4,28,8,128]{3,2,1,0:T(8,128)S(1)}, f32[4,28,8,128]{3,2,1,0:T(8,128)S(1)}, u32[]{:S(2)}, u32[]{:S(2)}) collective-permute-start(f32[4,28,8,128]{3,2,1,0:T(8,128)S(1)} %get-tuple-element.54.refs_4_), channel_id=1, source_target_pairs={{0,8},{1,9},{2,10},{3,11},{4,12},{5,13},{6,14},{7,15},{8,0},{9,1},... | collective-permute-start | bytes 1376264 | tf_op jit(solution)/shard_map/ppermute | solution.py:331
  78.5 2.2 %collective-permute-start.21 = (f32[4,28,8,128]{3,2,1,0:T(8,128)S(1)}, f32[4,28,8,128]{3,2,1,0:T(8,128)S(1)}, u32[]{:S(2)}, u32[]{:S(2)}) collective-permute-start(f32[4,28,8,128]{3,2,1,0:T(8,128)S(1)} %get-tuple-element.54.refs_4_), channel_id=1, source_target_pairs={{0,12},{1,13},{2,14},{3,15},{4,0},{5,1},{6,2},{7,3},{8,4},{9,5},{1... | collective-permute-start | bytes 1376264 | tf_op jit(solution)/shard_map/ppermute | solution.py:331
  80.7 2.7 %collective-permute-done.17.refs_2_ = f32[4,28,8,128]{3,2,1,0:T(8,128)S(1)} collective-permute-done((f32[4,28,8,128]{3,2,1,0:T(8,128)S(1)}, f32[4,28,8,128]{3,2,1,0:T(8,128)S(1)}, u32[]{:S(2)}, u32[]{:S(2)}) %collective-permute-start.17) | collective-permute-done | bytes 458784 | tf_op jit(solution)/shard_map/ppermute | solution.py:331
  83.5 2.1 %collective-permute-done.20.refs_6_ = f32[4,28,8,128]{3,2,1,0:T(8,128)S(1)} collective-permute-done((f32[4,28,8,128]{3,2,1,0:T(8,128)S(1)}, f32[4,28,8,128]{3,2,1,0:T(8,128)S(1)}, u32[]{:S(2)}, u32[]{:S(2)}) %collective-permute-start.20) | collective-permute-done | bytes 458784 | tf_op jit(solution)/shard_map/ppermute | solution.py:331
  85.6 4.8 %collective-permute-done.21.refs_7_ = f32[4,28,8,128]{3,2,1,0:T(8,128)S(1)} collective-permute-done((f32[4,28,8,128]{3,2,1,0:T(8,128)S(1)}, f32[4,28,8,128]{3,2,1,0:T(8,128)S(1)}, u32[]{:S(2)}, u32[]{:S(2)}) %collective-permute-start.21) | collective-permute-done | bytes 458784 | tf_op jit(solution)/shard_map/ppermute | solution.py:331
  91.5 4.6 %zsum.1.refs_0_.refs_2_ = f32[4,4,32,128]{3,2,1,0:T(8,128)S(1)} custom-call(s32[4]{0:T(128)S(1)} %pad_add_fusion.place_ref, f32[128,1536]{1,0:T(8,128)S(1)} %get-tuple-element.56.refs_0_, f32[128,1536]{1,0:T(8,128)S(1)} %get-tuple-element.57.refs_1_, f32[128,1536]{1,0:T(8,128)S(1)} %copy-done.11, f32[128,1536]{1,0:T(8,128)S(1)} %copy-done.7, ...), custom_call_target="tpu_custom_call" | custom-call | bytes 3500000 | tf_op jit(solution)/shard_map/zsum/pallas_call | solution.py:306
  96.2 4.6 %forward.1 = (f32[128,512]{1,0:T(8,128)S(1)}, f32[128,512]{1,0:T(8,128)S(1)}, f32[2,4,1024]{2,1,0:T(4,128)}) custom-call(s32[4]{0:T(128)S(1)} %pad_add_fusion.place_ref, f32[32,16,8,128]{3,2,1,0:T(8,128)S(1)} %get-tuple-element.55.mine_ref.refs_0_, f32[32,16,8,128]{3,2,1,0:T(8,128)S(1)} %collective-permute-done.22.other_ref.refs_1_, ...), custom_call_target="tpu_custom_call" | custom-call | bytes 21000000 | tf_op jit(solution)/shard_map/forward/pallas_call | solution.py:306
  100.8 5.1 %trail.1 = (f32[32,1536]{1,0:T(8,128)S(1)}, f32[32,1536]{1,0:T(8,128)S(1)}, f32[32,1536]{1,0:T(8,128)}, f32[32,1536]{1,0:T(8,128)}, f32[32,2048]{1,0:T(8,128)S(1...) custom-call(f32[128,512]{1,0:T(8,128)S(1)} %get-tuple-element.61.refs_0_, ...), custom_call_target="tpu_custom_call" | custom-call | bytes 3500000 | tf_op jit(solution)/shard_map/trail/pallas_call | solution.py:306
  106.5 0.7 copy-done.17
  107.2 1.3 collective-permute-start.23
  108.6 1.6 %collective-permute-start.26 = (f32[32,2048]{1,0:T(8,128)}, f32[32,2048]{1,0:T(8,128)S(1)}, u32[]{:S(2)}, u32[]{:S(2)}) collective-permute-start(f32[32,2048]{1,0:T(8,128)} %get-tuple-element.68), channel_id=1, source_target_pairs={{0,12},{1,13},{2,14},{3,15},{4,0},{5,1},{6,2},{7,3},{8,4},{9,5},{1... | collective-permute-start | bytes 786440 | tf_op jit(solution)/shard_map/ppermute | solution.py:331
  110.1 1.5 collective-permute-start.27
  111.6 2.6 %collective-permute-start.28 = (f32[32,2048]{1,0:T(8,128)}, f32[32,2048]{1,0:T(8,128)S(1)}, u32[]{:S(2)}, u32[]{:S(2)}) collective-permute-start(f32[32,2048]{1,0:T(8,128)} %get-tuple-element.70), channel_id=1, source_target_pairs={{0,4},{1,5},{2,6},{3,7},{4,8},{5,9},{6,10},{7,11},{8,12},{9,13},{1... | collective-permute-start | bytes 786440 | tf_op jit(solution)/shard_map/ppermute | solution.py:331
  114.2 1.6 %collective-permute-start.24 = (f32[32,1536]{1,0:T(8,128)}, f32[32,1536]{1,0:T(8,128)}, u32[]{:S(2)}, u32[]{:S(2)}) collective-permute-start(f32[32,1536]{1,0:T(8,128)} %get-tuple-element.65), channel_id=1, source_target_pairs={{0,2},{1,3},{2,0},{3,1},{4,6},{5,7},{6,4},{7,5},{8,10},{9,11},{10,... | collective-permute-start | bytes 589832 | tf_op jit(solution)/shard_map/ppermute | solution.py:331
  116.6 1.6 %copy-done.3 = f32[32,16,8,128]{3,2,1,0:T(8,128)S(1)} copy-done((f32[32,16,8,128]{3,2,1,0:T(8,128)S(1)}, f32[32,16,8,128]{3,2,1,0:T(8,128)}, u32[]{:S(2)}) %copy-start.3) | copy-done | bytes 2097176
  118.2 1.2 copy-done.9
  119.4 0.9 copy-done.15
  120.8 3.1 %collective-permute-done.24.refs_2_ = f32[32,1536]{1,0:T(8,128)} collective-permute-done((f32[32,1536]{1,0:T(8,128)}, f32[32,1536]{1,0:T(8,128)}, u32[]{:S(2)}, u32[]{:S(2)}) %collective-permute-start.24) | collective-permute-done | bytes 196640 | tf_op jit(solution)/shard_map/ppermute | solution.py:331
  123.9 2.1 %collective-permute-done.25.refs_3_ = f32[32,1536]{1,0:T(8,128)} collective-permute-done((f32[32,1536]{1,0:T(8,128)}, f32[32,1536]{1,0:T(8,128)}, u32[]{:S(2)}, u32[]{:S(2)}) %collective-permute-start.25) | collective-permute-done | bytes 196640 | tf_op jit(solution)/shard_map/ppermute | solution.py:331
  126.0 1.2 middle.1
  127.8 1.6 %collective-permute-start.33 = (f32[8,4096]{1,0:T(8,128)S(1)}, f32[8,4096]{1,0:T(8,128)S(1)}, u32[]{:S(2)}, u32[]{:S(2)}) collective-permute-start(f32[8,4096]{1,0:T(8,128)S(1)} %get-tuple-element.78), channel_id=1, source_target_pairs={{0,2},{1,3},{2,0},{3,1},{4,6},{5,7},{6,4},{7,5},{8,10},{9,11},{10,... | collective-permute-start | bytes 393224 | tf_op jit(solution)/shard_map/ppermute | solution.py:331
  129.5 0.9 collective-permute-start.34
  130.3 1.8 %collective-permute-start.29 = (f32[8,1536]{1,0:T(8,128)S(1)}, f32[8,1536]{1,0:T(8,128)S(1)}, u32[]{:S(2)}, u32[]{:S(2)}) collective-permute-start(f32[8,1536]{1,0:T(8,128)S(1)} %get-tuple-element.73), channel_id=1, source_target_pairs={{0,12},{1,13},{2,14},{3,15},{4,0},{5,1},{6,2},{7,3},{8,4},{9,5},{1... | collective-permute-start | bytes 147464 | tf_op jit(solution)/shard_map/ppermute | solution.py:331
  132.1 1.0 collective-permute-done.32.refs_1_.refs_5_
  133.1 2.2 %collective-permute-done.33.refs_2_.refs_6_ = f32[8,4096]{1,0:T(8,128)S(1)} collective-permute-done((f32[8,4096]{1,0:T(8,128)S(1)}, f32[8,4096]{1,0:T(8,128)S(1)}, u32[]{:S(2)}, u32[]{:S(2)}) %collective-permute-start.33) | collective-permute-done | bytes 131104 | tf_op jit(solution)/shard_map/ppermute | solution.py:331
  135.3 1.0 collective-permute-done.34.refs_3_.refs_7_
  136.3 0.8 last.1.refs_8_
  137.5 1.5 collective-permute-start.30
  139.0 2.0 %collective-permute-start.31 = (f32[8,1536]{1,0:T(8,128)S(1)}, f32[8,1536]{1,0:T(8,128)S(1)}, u32[]{:S(2)}, u32[]{:S(2)}) collective-permute-start(f32[8,1536]{1,0:T(8,128)S(1)} %get-tuple-element.75), channel_id=1, source_target_pairs={{0,4},{1,5},{2,6},{3,7},{4,8},{5,9},{6,10},{7,11},{8,12},{9,13},{1... | collective-permute-start | bytes 147464 | tf_op jit(solution)/shard_map/ppermute | solution.py:331
  141.0 1.8 %collective-permute-start.36 = (f32[8,8,128]{2,1,0:T(8,128)S(1)}, f32[8,8,128]{2,1,0:T(8,128)S(1)}, u32[]{:S(2)}, u32[]{:S(2)}) collective-permute-start(f32[8,8,128]{2,1,0:T(8,128)S(1)} %add.101.refs_0_), channel_id=1, source_target_pairs={{0,32},{16,48},{32,64},{48,80},{64,96},{80,112},{96,0},{112,16},{1... | collective-permute-start | bytes 98312 | tf_op jit(solution)/shard_map/ppermute | solution.py:323
  142.8 3.1 %collective-permute-start.37 = (f32[8,8,128]{2,1,0:T(8,128)S(1)}, f32[8,8,128]{2,1,0:T(8,128)S(1)}, u32[]{:S(2)}, u32[]{:S(2)}) collective-permute-start(f32[8,8,128]{2,1,0:T(8,128)S(1)} %add.101.refs_0_), channel_id=1, source_target_pairs={{0,64},{16,80},{32,96},{48,112},{64,0},{80,16},{96,32},{112,48},{1... | collective-permute-start | bytes 98312 | tf_op jit(solution)/shard_map/ppermute | solution.py:323
  145.9 1.1 collective-permute-start.38
  147.0 1.4 finish.1
  148.4 1.4 collective-permute-done.38.refs_3_
  149.8 4.6 %backward.1 = f32[2,4,1024]{2,1,0:T(4,128)} custom-call(s32[4]{0:T(128)S(1)} %pad_add_fusion.place_ref, f32[8,1024]{1,0:T(8,128)S(1)} %get-tuple-element.80.loads_ref, f32[8,8,128]{2,1,0:T(8,128)S(1)} %add.101.refs_0_, f32[8,8,128]{2,1,0:T(8,128)S(1)} %collective-permute-done.36.refs_1_, f32[8,8,128]{2,1,0:T(8,128)S(1)} %collective-permute-done.37.refs_2_, ...), custom_call_target="tpu_custom_call" | custom-call | bytes 21000000 | tf_op jit(solution)/shard_map/backward/pallas_call | solution.py:306
  (83 shorter events, 6.2 us)
Async XLA Ops:
  0.6 115.9 %copy-start = (f32[2,64,1024]{2,1,0:T(8,128)S(1)}, f32[2,64,1024]{2,1,0:T(8,128)}, u32[]{:S(2)}) copy-start(f32[2,64,1024]{2,1,0:T(8,128)} %param.9) | copy-start | bytes 1572868
  0.7 7.1 %slice-start = ((f32[2,4,12288]{2,1,0:T(4,128)}), f32[2,4,128]{2,1,0:T(4,128)S(1)}, s32[]{:S(2)}) async-start(f32[2,4,12288]{2,1,0:T(4,128)} %loads_ref.1), calls=%async_computation | async-start | bytes 8192 | tf_op jit(solution)/shard_map/slice | solution.py:365
  4.1 23.9 %collective-permute-start.4 = (f32[128,1536]{1,0:T(8,128)S(1)}, f32[128,1536]{1,0:T(8,128)S(1)}, u32[]{:S(2)}, u32[]{:S(2)}) collective-permute-start(f32[128,1536]{1,0:T(8,128)S(1)} %get-tuple-element.86.refs_0_), channel_id=1, source_target_pairs={{0,4},{1,5},{2,6},{3,7},{4,8},{5,9},{6,10},{7,11},{8,12},{9,13},{1... | collective-permute-start | bytes 2359304 | tf_op jit(solution)/shard_map/ppermute | solution.py:331
  6.6 1.3 collective-permute-start
  7.9 7.5 %collective-permute-start.1 = (f32[136,128]{1,0:T(8,128)S(1)}, f32[136,128]{1,0:T(8,128)S(1)}, u32[]{:S(2)}, u32[]{:S(2)}) collective-permute-start(f32[136,128]{1,0:T(8,128)S(1)} %pad_maximum_fusion.own_ref), channel_id=1, source_target_pairs={{0,32},{16,48},{32,64},{48,80},{64,96},{80,112},{96,0},{112,16},{1... | collective-permute-start | bytes 208904 | tf_op jit(solution)/shard_map/ppermute | solution.py:323
  9.9 7.4 %collective-permute-start.2 = (f32[136,128]{1,0:T(8,128)S(1)}, f32[136,128]{1,0:T(8,128)S(1)}, u32[]{:S(2)}, u32[]{:S(2)}) collective-permute-start(f32[136,128]{1,0:T(8,128)S(1)} %pad_maximum_fusion.own_ref), channel_id=1, source_target_pairs={{0,64},{16,80},{32,96},{48,112},{64,0},{80,16},{96,32},{112,48},{1... | collective-permute-start | bytes 208904 | tf_op jit(solution)/shard_map/ppermute | solution.py:323
  13.4 21.0 %collective-permute-start.5 = (f32[128,1536]{1,0:T(8,128)}, f32[128,1536]{1,0:T(8,128)}, u32[]{:S(2)}, u32[]{:S(2)}) collective-permute-start(f32[128,1536]{1,0:T(8,128)} %get-tuple-element.85), channel_id=1, source_target_pairs={{0,1},{1,2},{2,3},{3,0},{4,5},{5,6},{6,7},{7,4},{8,9},{9,10},{10,1... | collective-permute-start | bytes 2359304 | tf_op jit(solution)/shard_map/ppermute | solution.py:331
  14.9 20.1 %collective-permute-start.6 = (f32[128,1536]{1,0:T(8,128)}, f32[128,1536]{1,0:T(8,128)}, u32[]{:S(2)}, u32[]{:S(2)}) collective-permute-start(f32[128,1536]{1,0:T(8,128)} %get-tuple-element.84), channel_id=1, source_target_pairs={{0,12},{1,13},{2,14},{3,15},{4,0},{5,1},{6,2},{7,3},{8,4},{9,5},{1... | collective-permute-start | bytes 2359304 | tf_op jit(solution)/shard_map/ppermute | solution.py:331
  15.4 36.9 %collective-permute-start.7 = (f32[128,1536]{1,0:T(8,128)}, f32[128,1536]{1,0:T(8,128)}, u32[]{:S(2)}, u32[]{:S(2)}) collective-permute-start(f32[128,1536]{1,0:T(8,128)} %get-tuple-element.83), channel_id=1, source_target_pairs={{0,3},{1,0},{2,1},{3,2},{4,7},{5,4},{6,5},{7,6},{8,11},{9,8},{10,9... | collective-permute-start | bytes 2359304 | tf_op jit(solution)/shard_map/ppermute | solution.py:331
  17.2 9.2 %collective-permute-start.3 = (f32[136,128]{1,0:T(8,128)S(1)}, f32[136,128]{1,0:T(8,128)S(1)}, u32[]{:S(2)}, u32[]{:S(2)}) collective-permute-start(f32[136,128]{1,0:T(8,128)S(1)} %pad_maximum_fusion.own_ref), channel_id=1, source_target_pairs={{0,96},{16,112},{32,0},{48,16},{64,32},{80,48},{96,64},{112,80},{1... | collective-permute-start | bytes 208904 | tf_op jit(solution)/shard_map/ppermute | solution.py:323
  19.8 2.8 %copy-start.1 = (f32[2,1,8,8,12288]{4,3,2,1,0:T(8,128)S(1)}, f32[2,1,8,8,12288]{4,3,2,1,0:T(8,128)}, u32[]{:S(2)}) copy-start(f32[2,1,8,8,12288]{4,3,2,1,0:T(8,128)} %param.6) | copy-start | bytes 18874372
  24.7 0.9 copy-start.10
  25.6 0.9 copy-start.12
  26.5 0.6 copy-start.21
  27.1 32.6 %collective-permute-start.14 = (f32[128,1536]{1,0:T(8,128)}, f32[128,1536]{1,0:T(8,128)S(1)}, u32[]{:S(2)}, u32[]{:S(2)}) collective-permute-start(f32[128,1536]{1,0:T(8,128)} %get-tuple-element.51), channel_id=1, source_target_pairs={{0,8},{1,9},{2,10},{3,11},{4,12},{5,13},{6,14},{7,15},{8,0},{9,1},... | collective-permute-start | bytes 2359304 | tf_op jit(solution)/shard_map/ppermute | solution.py:331
  28.0 25.9 %copy-start.6 = (f32[128,1536]{1,0:T(8,128)}, f32[128,1536]{1,0:T(8,128)S(1)}, u32[]{:S(2)}) copy-start(f32[128,1536]{1,0:T(8,128)S(1)} %collective-permute-done.4.refs_0_.refs_3_.refs_4_) | copy-start | bytes 2359300
  28.0 31.7 %collective-permute-start.15 = (f32[128,1536]{1,0:T(8,128)}, f32[128,1536]{1,0:T(8,128)S(1)}, u32[]{:S(2)}, u32[]{:S(2)}) collective-permute-start(f32[128,1536]{1,0:T(8,128)} %get-tuple-element.52), channel_id=1, source_target_pairs={{0,2},{1,3},{2,0},{3,1},{4,6},{5,7},{6,4},{7,5},{8,10},{9,11},{10,... | collective-permute-start | bytes 2359304 | tf_op jit(solution)/shard_map/ppermute | solution.py:331
  52.3 0.9 copy-start.22
  53.9 7.5 %collective-permute-start.10 = (f32[28,8,128]{2,1,0:T(8,128)S(1)}, f32[28,8,128]{2,1,0:T(8,128)S(1)}, u32[]{:S(2)}, u32[]{:S(2)}) collective-permute-start(f32[28,8,128]{2,1,0:T(8,128)S(1)} %get-tuple-element.46), channel_id=1, source_target_pairs={{0,12},{1,13},{2,14},{3,15},{4,0},{5,1},{6,2},{7,3},{8,4},{9,5},{1... | collective-permute-start | bytes 344072 | tf_op jit(solution)/shard_map/ppermute | solution.py:331
  54.1 9.5 %collective-permute-start.11 = (f32[28,8,128]{2,1,0:T(8,128)S(1)}, f32[28,8,128]{2,1,0:T(8,128)S(1)}, u32[]{:S(2)}, u32[]{:S(2)}) collective-permute-start(f32[28,8,128]{2,1,0:T(8,128)S(1)} %get-tuple-element.48), channel_id=1, source_target_pairs={{0,1},{1,2},{2,3},{3,0},{4,5},{5,6},{6,7},{7,4},{8,9},{9,10},{10,1... | collective-permute-start | bytes 344072 | tf_op jit(solution)/shard_map/ppermute | solution.py:331
  54.1 10.4 %collective-permute-start.12 = (f32[28,8,128]{2,1,0:T(8,128)S(1)}, f32[28,8,128]{2,1,0:T(8,128)S(1)}, u32[]{:S(2)}, u32[]{:S(2)}) collective-permute-start(f32[28,8,128]{2,1,0:T(8,128)S(1)} %get-tuple-element.49), channel_id=1, source_target_pairs={{0,2},{1,3},{2,0},{3,1},{4,6},{5,7},{6,4},{7,5},{8,10},{9,11},{10,... | collective-permute-start | bytes 344072 | tf_op jit(solution)/shard_map/ppermute | solution.py:331
  59.7 6.0 %collective-permute-start.13 = (f32[28,8,128]{2,1,0:T(8,128)S(1)}, f32[28,8,128]{2,1,0:T(8,128)S(1)}, u32[]{:S(2)}, u32[]{:S(2)}) collective-permute-start(f32[28,8,128]{2,1,0:T(8,128)S(1)} %get-tuple-element.50), channel_id=1, source_target_pairs={{0,3},{1,0},{2,1},{3,2},{4,7},{5,4},{6,5},{7,6},{8,11},{9,8},{10,9... | collective-permute-start | bytes 344072 | tf_op jit(solution)/shard_map/ppermute | solution.py:331
  59.7 25.9 %copy-start.4 = (f32[128,1536]{1,0:T(8,128)}, f32[128,1536]{1,0:T(8,128)S(1)}, u32[]{:S(2)}) copy-start(f32[128,1536]{1,0:T(8,128)S(1)} %collective-permute-done.15.refs_9_.refs_8_) | copy-start | bytes 2359300
  59.7 6.0 %collective-permute-start.8 = (f32[28,8,128]{2,1,0:T(8,128)S(1)}, f32[28,8,128]{2,1,0:T(8,128)S(1)}, u32[]{:S(2)}, u32[]{:S(2)}) collective-permute-start(f32[28,8,128]{2,1,0:T(8,128)S(1)} %get-tuple-element.44), channel_id=1, source_target_pairs={{0,4},{1,5},{2,6},{3,7},{4,8},{5,9},{6,10},{7,11},{8,12},{9,13},{1... | collective-permute-start | bytes 344072 | tf_op jit(solution)/shard_map/ppermute | solution.py:331
  61.4 6.3 %collective-permute-start.9 = (f32[28,8,128]{2,1,0:T(8,128)S(1)}, f32[28,8,128]{2,1,0:T(8,128)S(1)}, u32[]{:S(2)}, u32[]{:S(2)}) collective-permute-start(f32[28,8,128]{2,1,0:T(8,128)S(1)} %get-tuple-element.45), channel_id=1, source_target_pairs={{0,8},{1,9},{2,10},{3,11},{4,12},{5,13},{6,14},{7,15},{8,0},{9,1},... | collective-permute-start | bytes 344072 | tf_op jit(solution)/shard_map/ppermute | solution.py:331
  67.8 23.3 %copy-start.7 = (f32[128,1536]{1,0:T(8,128)S(1)}, f32[128,1536]{1,0:T(8,128)}, u32[]{:S(2)}) copy-start(f32[128,1536]{1,0:T(8,128)} %copy-done.6) | copy-start | bytes 2359300
  67.8 23.3 %copy-start.11 = (f32[128,1536]{1,0:T(8,128)S(1)}, f32[128,1536]{1,0:T(8,128)}, u32[]{:S(2)}) copy-start(f32[128,1536]{1,0:T(8,128)} %copy-done.10) | copy-start | bytes 2359300
  67.8 23.3 %copy-start.13 = (f32[128,1536]{1,0:T(8,128)S(1)}, f32[128,1536]{1,0:T(8,128)}, u32[]{:S(2)}) copy-start(f32[128,1536]{1,0:T(8,128)} %copy-done.12) | copy-start | bytes 2359300
  67.8 10.7 %collective-permute-start.16 = (f32[4,28,8,128]{3,2,1,0:T(8,128)S(1)}, f32[4,28,8,128]{3,2,1,0:T(8,128)S(1)}, u32[]{:S(2)}, u32[]{:S(2)}) collective-permute-start(f32[4,28,8,128]{3,2,1,0:T(8,128)S(1)} %get-tuple-element.53.refs_0_), channel_id=1, source_target_pairs={{0,1},{1,2},{2,3},{3,0},{4,5},{5,6},{6,7},{7,4},{8,9},{9,10},{10,1... | collective-permute-start | bytes 1376264 | tf_op jit(solution)/shard_map/ppermute | solution.py:331
  71.0 12.4 %collective-permute-start.17 = (f32[4,28,8,128]{3,2,1,0:T(8,128)S(1)}, f32[4,28,8,128]{3,2,1,0:T(8,128)S(1)}, u32[]{:S(2)}, u32[]{:S(2)}) collective-permute-start(f32[4,28,8,128]{3,2,1,0:T(8,128)S(1)} %get-tuple-element.53.refs_0_), channel_id=1, source_target_pairs={{0,2},{1,3},{2,0},{3,1},{4,6},{5,7},{6,4},{7,5},{8,10},{9,11},{10,... | collective-permute-start | bytes 1376264 | tf_op jit(solution)/shard_map/ppermute | solution.py:331
  71.1 12.4 %collective-permute-start.18 = (f32[4,28,8,128]{3,2,1,0:T(8,128)S(1)}, f32[4,28,8,128]{3,2,1,0:T(8,128)S(1)}, u32[]{:S(2)}, u32[]{:S(2)}) collective-permute-start(f32[4,28,8,128]{3,2,1,0:T(8,128)S(1)} %get-tuple-element.53.refs_0_), channel_id=1, source_target_pairs={{0,3},{1,0},{2,1},{3,2},{4,7},{5,4},{6,5},{7,6},{8,11},{9,8},{10,9... | collective-permute-start | bytes 1376264 | tf_op jit(solution)/shard_map/ppermute | solution.py:331
  73.8 9.7 %collective-permute-start.19 = (f32[4,28,8,128]{3,2,1,0:T(8,128)S(1)}, f32[4,28,8,128]{3,2,1,0:T(8,128)S(1)}, u32[]{:S(2)}, u32[]{:S(2)}) collective-permute-start(f32[4,28,8,128]{3,2,1,0:T(8,128)S(1)} %get-tuple-element.54.refs_4_), channel_id=1, source_target_pairs={{0,4},{1,5},{2,6},{3,7},{4,8},{5,9},{6,10},{7,11},{8,12},{9,13},{1... | collective-permute-start | bytes 1376264 | tf_op jit(solution)/shard_map/ppermute | solution.py:331
  75.5 10.1 %collective-permute-start.20 = (f32[4,28,8,128]{3,2,1,0:T(8,128)S(1)}, f32[4,28,8,128]{3,2,1,0:T(8,128)S(1)}, u32[]{:S(2)}, u32[]{:S(2)}) collective-permute-start(f32[4,28,8,128]{3,2,1,0:T(8,128)S(1)} %get-tuple-element.54.refs_4_), channel_id=1, source_target_pairs={{0,8},{1,9},{2,10},{3,11},{4,12},{5,13},{6,14},{7,15},{8,0},{9,1},... | collective-permute-start | bytes 1376264 | tf_op jit(solution)/shard_map/ppermute | solution.py:331
  78.5 11.9 %collective-permute-start.21 = (f32[4,28,8,128]{3,2,1,0:T(8,128)S(1)}, f32[4,28,8,128]{3,2,1,0:T(8,128)S(1)}, u32[]{:S(2)}, u32[]{:S(2)}) collective-permute-start(f32[4,28,8,128]{3,2,1,0:T(8,128)S(1)} %get-tuple-element.54.refs_4_), channel_id=1, source_target_pairs={{0,12},{1,13},{2,14},{3,15},{4,0},{5,1},{6,2},{7,3},{8,4},{9,5},{1... | collective-permute-start | bytes 1376264 | tf_op jit(solution)/shard_map/ppermute | solution.py:331
  90.4 1.1 copy-start.5
  90.8 5.4 %collective-permute-start.22 = (f32[32,16,8,128]{3,2,1,0:T(8,128)S(1)}, f32[32,16,8,128]{3,2,1,0:T(8,128)S(1)}, u32[]{:S(2)}, u32[]{:S(2)}) collective-permute-start(f32[32,16,8,128]{3,2,1,0:T(8,128)S(1)} %get-tuple-element.55.mine_ref.refs_0_), channel_id=1, source_target_pairs={{0,16},{16,0},{32,48},{48,32},{64,80},{80,64},{96,112},{112,96},{1... | collective-permute-start | bytes 6291464 | tf_op jit(solution)/shard_map/ppermute | solution.py:319
  91.5 4.6 %copy-start.8 = (f32[2,8,128,128]{3,2,1,0:T(8,128)S(1)}, f32[2,8,128,128]{3,2,1,0:T(8,128)}, u32[]{:S(2)}) copy-start(f32[2,8,128,128]{3,2,1,0:T(8,128)} %refs_2_.1) | copy-start | bytes 3145732
  96.2 4.6 %copy-start.2 = (f32[32,16,8,128]{3,2,1,0:T(8,128)}, f32[32,16,8,128]{3,2,1,0:T(8,128)S(1)}, u32[]{:S(2)}) copy-start(f32[32,16,8,128]{3,2,1,0:T(8,128)S(1)} %collective-permute-done.22.other_ref.refs_1_) | copy-start | bytes 6291460
  105.8 0.7 copy-start.14
  106.5 0.7 copy-start.17
  107.2 8.6 %collective-permute-start.23 = (f32[32,1536]{1,0:T(8,128)S(1)}, f32[32,1536]{1,0:T(8,128)S(1)}, u32[]{:S(2)}, u32[]{:S(2)}) collective-permute-start(f32[32,1536]{1,0:T(8,128)S(1)} %get-tuple-element.64), channel_id=1, source_target_pairs={{0,3},{1,0},{2,1},{3,2},{4,7},{5,4},{6,5},{7,6},{8,11},{9,8},{10,9... | collective-permute-start | bytes 589832 | tf_op jit(solution)/shard_map/ppermute | solution.py:331
  108.6 17.4 %collective-permute-start.26 = (f32[32,2048]{1,0:T(8,128)}, f32[32,2048]{1,0:T(8,128)S(1)}, u32[]{:S(2)}, u32[]{:S(2)}) collective-permute-start(f32[32,2048]{1,0:T(8,128)} %get-tuple-element.68), channel_id=1, source_target_pairs={{0,12},{1,13},{2,14},{3,15},{4,0},{5,1},{6,2},{7,3},{8,4},{9,5},{1... | collective-permute-start | bytes 786440 | tf_op jit(solution)/shard_map/ppermute | solution.py:331
  110.1 15.8 %collective-permute-start.27 = (f32[32,2048]{1,0:T(8,128)}, f32[32,2048]{1,0:T(8,128)S(1)}, u32[]{:S(2)}, u32[]{:S(2)}) collective-permute-start(f32[32,2048]{1,0:T(8,128)} %get-tuple-element.69), channel_id=1, source_target_pairs={{0,8},{1,9},{2,10},{3,11},{4,12},{5,13},{6,14},{7,15},{8,0},{9,1},... | collective-permute-start | bytes 786440 | tf_op jit(solution)/shard_map/ppermute | solution.py:331
  111.6 14.4 %collective-permute-start.28 = (f32[32,2048]{1,0:T(8,128)}, f32[32,2048]{1,0:T(8,128)S(1)}, u32[]{:S(2)}, u32[]{:S(2)}) collective-permute-start(f32[32,2048]{1,0:T(8,128)} %get-tuple-element.70), channel_id=1, source_target_pairs={{0,4},{1,5},{2,6},{3,7},{4,8},{5,9},{6,10},{7,11},{8,12},{9,13},{1... | collective-permute-start | bytes 786440 | tf_op jit(solution)/shard_map/ppermute | solution.py:331
  114.2 9.6 %collective-permute-start.24 = (f32[32,1536]{1,0:T(8,128)}, f32[32,1536]{1,0:T(8,128)}, u32[]{:S(2)}, u32[]{:S(2)}) collective-permute-start(f32[32,1536]{1,0:T(8,128)} %get-tuple-element.65), channel_id=1, source_target_pairs={{0,2},{1,3},{2,0},{3,1},{4,6},{5,7},{6,4},{7,5},{8,10},{9,11},{10,... | collective-permute-start | bytes 589832 | tf_op jit(solution)/shard_map/ppermute | solution.py:331
  115.9 0.7 copy-start.19
  116.6 9.4 %collective-permute-start.25 = (f32[32,1536]{1,0:T(8,128)}, f32[32,1536]{1,0:T(8,128)}, u32[]{:S(2)}, u32[]{:S(2)}) collective-permute-start(f32[32,1536]{1,0:T(8,128)} %get-tuple-element.66), channel_id=1, source_target_pairs={{0,1},{1,2},{2,3},{3,0},{4,5},{5,6},{6,7},{7,4},{8,9},{9,10},{10,1... | collective-permute-start | bytes 589832 | tf_op jit(solution)/shard_map/ppermute | solution.py:331
  116.6 1.6 %copy-start.3 = (f32[32,16,8,128]{3,2,1,0:T(8,128)S(1)}, f32[32,16,8,128]{3,2,1,0:T(8,128)}, u32[]{:S(2)}) copy-start(f32[32,16,8,128]{3,2,1,0:T(8,128)} %copy-done.2) | copy-start | bytes 6291460
  118.2 1.2 copy-start.9
  119.4 0.9 copy-start.15
  120.3 5.6 %copy-start.18 = (f32[32,2048]{1,0:T(8,128)S(1)}, f32[32,2048]{1,0:T(8,128)}, u32[]{:S(2)}) copy-start(f32[32,2048]{1,0:T(8,128)} %copy-done.17) | copy-start | bytes 786436
  120.3 5.7 %copy-start.20 = (f32[32,1536]{1,0:T(8,128)S(1)}, f32[32,1536]{1,0:T(8,128)}, u32[]{:S(2)}) copy-start(f32[32,1536]{1,0:T(8,128)} %copy-done.19) | copy-start | bytes 589828
  126.0 21.0 %copy-start.16 = (f32[2,4,12288]{2,1,0:T(4,128)S(1)}, f32[2,4,12288]{2,1,0:T(4,128)}, u32[]{:S(2)}) copy-start(f32[2,4,12288]{2,1,0:T(4,128)} %loads_ref.1) | copy-start | bytes 1179652
  127.2 5.9 %collective-permute-start.32 = (f32[8,4096]{1,0:T(8,128)S(1)}, f32[8,4096]{1,0:T(8,128)S(1)}, u32[]{:S(2)}, u32[]{:S(2)}) collective-permute-start(f32[8,4096]{1,0:T(8,128)S(1)} %get-tuple-element.77), channel_id=1, source_target_pairs={{0,3},{1,0},{2,1},{3,2},{4,7},{5,4},{6,5},{7,6},{8,11},{9,8},{10,9... | collective-permute-start | bytes 393224 | tf_op jit(solution)/shard_map/ppermute | solution.py:331
  127.8 7.5 %collective-permute-start.33 = (f32[8,4096]{1,0:T(8,128)S(1)}, f32[8,4096]{1,0:T(8,128)S(1)}, u32[]{:S(2)}, u32[]{:S(2)}) collective-permute-start(f32[8,4096]{1,0:T(8,128)S(1)} %get-tuple-element.78), channel_id=1, source_target_pairs={{0,2},{1,3},{2,0},{3,1},{4,6},{5,7},{6,4},{7,5},{8,10},{9,11},{10,... | collective-permute-start | bytes 393224 | tf_op jit(solution)/shard_map/ppermute | solution.py:331
  129.5 6.9 %collective-permute-start.34 = (f32[8,4096]{1,0:T(8,128)S(1)}, f32[8,4096]{1,0:T(8,128)S(1)}, u32[]{:S(2)}, u32[]{:S(2)}) collective-permute-start(f32[8,4096]{1,0:T(8,128)S(1)} %get-tuple-element.79), channel_id=1, source_target_pairs={{0,1},{1,2},{2,3},{3,0},{4,5},{5,6},{6,7},{7,4},{8,9},{9,10},{10,1... | collective-permute-start | bytes 393224 | tf_op jit(solution)/shard_map/ppermute | solution.py:331
  130.3 15.6 %collective-permute-start.29 = (f32[8,1536]{1,0:T(8,128)S(1)}, f32[8,1536]{1,0:T(8,128)S(1)}, u32[]{:S(2)}, u32[]{:S(2)}) collective-permute-start(f32[8,1536]{1,0:T(8,128)S(1)} %get-tuple-element.73), channel_id=1, source_target_pairs={{0,12},{1,13},{2,14},{3,15},{4,0},{5,1},{6,2},{7,3},{8,4},{9,5},{1... | collective-permute-start | bytes 147464 | tf_op jit(solution)/shard_map/ppermute | solution.py:331
  137.2 3.8 %collective-permute-start.35 = (f32[8,8,128]{2,1,0:T(8,128)S(1)}, f32[8,8,128]{2,1,0:T(8,128)S(1)}, u32[]{:S(2)}, u32[]{:S(2)}) collective-permute-start(f32[8,8,128]{2,1,0:T(8,128)S(1)} %last.1.refs_8_), channel_id=1, source_target_pairs={{0,16},{16,0},{32,48},{48,32},{64,80},{80,64},{96,112},{112,96},{1... | collective-permute-start | bytes 98312 | tf_op jit(solution)/shard_map/ppermute | solution.py:319
  137.5 9.5 %collective-permute-start.30 = (f32[8,1536]{1,0:T(8,128)S(1)}, f32[8,1536]{1,0:T(8,128)S(1)}, u32[]{:S(2)}, u32[]{:S(2)}) collective-permute-start(f32[8,1536]{1,0:T(8,128)S(1)} %get-tuple-element.74), channel_id=1, source_target_pairs={{0,8},{1,9},{2,10},{3,11},{4,12},{5,13},{6,14},{7,15},{8,0},{9,1},... | collective-permute-start | bytes 147464 | tf_op jit(solution)/shard_map/ppermute | solution.py:331
  139.0 8.0 %collective-permute-start.31 = (f32[8,1536]{1,0:T(8,128)S(1)}, f32[8,1536]{1,0:T(8,128)S(1)}, u32[]{:S(2)}, u32[]{:S(2)}) collective-permute-start(f32[8,1536]{1,0:T(8,128)S(1)} %get-tuple-element.75), channel_id=1, source_target_pairs={{0,4},{1,5},{2,6},{3,7},{4,8},{5,9},{6,10},{7,11},{8,12},{9,13},{1... | collective-permute-start | bytes 147464 | tf_op jit(solution)/shard_map/ppermute | solution.py:331
  141.0 7.4 %collective-permute-start.36 = (f32[8,8,128]{2,1,0:T(8,128)S(1)}, f32[8,8,128]{2,1,0:T(8,128)S(1)}, u32[]{:S(2)}, u32[]{:S(2)}) collective-permute-start(f32[8,8,128]{2,1,0:T(8,128)S(1)} %add.101.refs_0_), channel_id=1, source_target_pairs={{0,32},{16,48},{32,64},{48,80},{64,96},{80,112},{96,0},{112,16},{1... | collective-permute-start | bytes 98312 | tf_op jit(solution)/shard_map/ppermute | solution.py:323
  142.8 5.6 %collective-permute-start.37 = (f32[8,8,128]{2,1,0:T(8,128)S(1)}, f32[8,8,128]{2,1,0:T(8,128)S(1)}, u32[]{:S(2)}, u32[]{:S(2)}) collective-permute-start(f32[8,8,128]{2,1,0:T(8,128)S(1)} %add.101.refs_0_), channel_id=1, source_target_pairs={{0,64},{16,80},{32,96},{48,112},{64,0},{80,16},{96,32},{112,48},{1... | collective-permute-start | bytes 98312 | tf_op jit(solution)/shard_map/ppermute | solution.py:323
  145.9 3.9 %collective-permute-start.38 = (f32[8,8,128]{2,1,0:T(8,128)S(1)}, f32[8,8,128]{2,1,0:T(8,128)S(1)}, u32[]{:S(2)}, u32[]{:S(2)}) collective-permute-start(f32[8,8,128]{2,1,0:T(8,128)S(1)} %add.101.refs_0_), channel_id=1, source_target_pairs={{0,96},{16,112},{32,0},{48,16},{64,32},{80,48},{96,64},{112,80},{1... | collective-permute-start | bytes 98312 | tf_op jit(solution)/shard_map/ppermute | solution.py:323

commit v6 on v4

--- a/solution.py
+++ b/solution.py
@@ -378,10 +378,10 @@
         "pack",
         [(MESSAGE, 8, NB)] * 8,
         [place, *slabs, trail_adjoint.reshape(8, TRAIL_LOCAL)],
-        after=one + three,
+        after=one,
     )
     heard = [to_all(messages[half * SIDE : half * SIDE + SIDE], AXES[half][0]) for half in range(2)]
-    first_lines = call(line_kernel, "line", [(SIDE, MESSAGE, 8, NB)] * 2, heard[0] + heard[1])
+    first_lines = call(line_kernel, "line", [(SIDE, MESSAGE, 8, NB)] * 2, heard[0] + heard[1], after=three)
     lines = to_all([first_lines[0]] * SIDE, AXES[0][1]) + to_all([first_lines[1]] * SIDE, AXES[1][1])
     late = cut(place, factor, (0, 2), [lines[1], lines[5]])
     two = [up(late[2 * half + 1], AXES[half][0], 2) for half in range(2)]

time: 142 us -> 141 us (level)
  no operation moved by 1% of the time
where the time goes in v6:
time: 141 us
  starting transfers between devices  55.8 us (40%)
  waiting for transfers between devices  46.8 us (33%)
  Pallas kernels  24.1 us (17%)
  local copies, waits for them, and re-layouts  13 us (9%)
    ppermute x30, starting transfers between devices, up(): return lax.ppermute(array, 'col', [(c, moved(c)) for c in range(COLS_AXIS)])  45.8 us
    ppermute x30, waiting for transfers between devices, up(): return lax.ppermute(array, 'col', [(c, moved(c)) for c in range(COLS_AXIS)])  33.9 us
    pallas_call x12, Pallas kernels, call(): pl.pallas_call(kernel, out_shape=[jax.ShapeDtypeStruct(shape, F32) for sh...  24.1 us
    ppermute x6, waiting for transfers between devices, up_z(): lax.ppermute(array, 'row', [(r, (r + 2 * by) % ROWS_AXIS) for r in range(...  11.8 us
    ppermute x6, starting transfers between devices, up_z(): lax.ppermute(array, 'row', [(r, (r + 2 * by) % ROWS_AXIS) for r in range(...  9.73 us
    unnamed x24, local copies, waits for them, and re-layouts  4.61 us
    dynamic_slice x1, local copies, waits for them, and re-layouts, quarter_of(): lax.dynamic_slice(factor, (0, NB + FIRST[half] + (place[2 + half] + by) %...  3.68 us
  transfers between devices with their start and end apart: 39, of which 18 were waited for; matrix products, arithmetic and copies ran while one was open for 3% of the time, Pallas kernels for 10%

profile of v6, /device:TPU:8, one launch (start us, length us, event | category | flops | bytes accessed | tf_op | source)
XLA Modules:
  0.0 140.8 jit_solution(13250582206766537260)
XLA Ops:
  0.8 3.7 %constant_dynamic-slice_fusion.1 = (f32[128,1536]{1,0:T(8,128)}, f32[128,1536]{1,0:T(8,128)}, f32[128,1536]{1,0:T(8,128)}, f32[128,1536]{1,0:T(8,128)}) fusion(f32[128,12288]{1,0:T(8,128)} %bitcast.11, s32[]{:T(128)S(6)} %select_n.71, s32[]{:T(128)S(6)} %select_n.69, s32[]{:T(128)S(6)} %select_n.67, s32[]{:T(128)S(6)} %select_n.65), kind=kLoop, calls=%fused_computation.4 | loop fusion | bytes 6291472 | tf_op jit(solution)/shard_map/dynamic_slice | solution.py:360
  4.4 1.6 %collective-permute-start.4 = (f32[128,1536]{1,0:T(8,128)}, f32[128,1536]{1,0:T(8,128)S(1)}, u32[]{:S(2)}, u32[]{:S(2)}) collective-permute-start(f32[128,1536]{1,0:T(8,128)} %get-tuple-element.92), channel_id=1, source_target_pairs={{0,4},{1,5},{2,6},{3,7},{4,8},{5,9},{6,10},{7,11},{8,12},{9,13},{1... | collective-permute-start | bytes 2359304 | tf_op jit(solution)/shard_map/ppermute | solution.py:337
  6.0 1.5 %collective-permute-start.5 = (f32[128,1536]{1,0:T(8,128)}, f32[128,1536]{1,0:T(8,128)}, u32[]{:S(2)}, u32[]{:S(2)}) collective-permute-start(f32[128,1536]{1,0:T(8,128)} %get-tuple-element.91), channel_id=1, source_target_pairs={{0,1},{1,2},{2,3},{3,0},{4,5},{5,6},{6,7},{7,4},{8,9},{9,10},{10,1... | collective-permute-start | bytes 2359304 | tf_op jit(solution)/shard_map/ppermute | solution.py:337
  8.0 1.7 %collective-permute-start.13 = (f32[128,1536]{1,0:T(8,128)}, f32[128,1536]{1,0:T(8,128)}, u32[]{:S(2)}, u32[]{:S(2)}) collective-permute-start(f32[128,1536]{1,0:T(8,128)} %get-tuple-element.89), channel_id=1, source_target_pairs={{0,3},{1,0},{2,1},{3,2},{4,7},{5,4},{6,5},{7,6},{8,11},{9,8},{10,9... | collective-permute-start | bytes 2359304 | tf_op jit(solution)/shard_map/ppermute | solution.py:337
  9.7 0.8 slice.8
  10.7 1.2 collective-permute-done
  11.9 2.0 %collective-permute-start.1 = (f32[136,128]{1,0:T(8,128)S(1)}, f32[136,128]{1,0:T(8,128)S(1)}, u32[]{:S(2)}, u32[]{:S(2)}) collective-permute-start(f32[136,128]{1,0:T(8,128)S(1)} %pad_maximum_fusion.own_ref), channel_id=1, source_target_pairs={{0,32},{16,48},{32,64},{48,80},{64,96},{80,112},{96,0},{112,16},{1... | collective-permute-start | bytes 208904 | tf_op jit(solution)/shard_map/ppermute | solution.py:329
  13.8 4.6 %collective-permute-done.1.one_ref = f32[136,128]{1,0:T(8,128)S(1)} collective-permute-done((f32[136,128]{1,0:T(8,128)S(1)}, f32[136,128]{1,0:T(8,128)S(1)}, u32[]{:S(2)}, u32[]{:S(2)}) %collective-permute-start.1) | collective-permute-done | bytes 69664 | tf_op jit(solution)/shard_map/ppermute | solution.py:329
  18.5 1.6 %collective-permute-start.2 = (f32[136,128]{1,0:T(8,128)S(1)}, f32[136,128]{1,0:T(8,128)}, u32[]{:S(2)}, u32[]{:S(2)}) collective-permute-start(f32[136,128]{1,0:T(8,128)S(1)} %pad_maximum_fusion.own_ref), channel_id=1, source_target_pairs={{0,64},{16,80},{32,96},{48,112},{64,0},{80,16},{96,32},{112,48},{1... | collective-permute-start | bytes 208904 | tf_op jit(solution)/shard_map/ppermute | solution.py:329
  20.1 1.9 %reshape.24.ta_ref = f32[8,12160]{1,0:T(8,128)} reshape(f32[2,4,12160]{2,1,0:T(4,128)} %param.8) | data formatting | bytes 778240 | tf_op jit(solution)/shard_map/reshape | solution.py:380
  22.0 2.4 %collective-permute-done.2.two_ref = f32[136,128]{1,0:T(8,128)} collective-permute-done((f32[136,128]{1,0:T(8,128)S(1)}, f32[136,128]{1,0:T(8,128)}, u32[]{:S(2)}, u32[]{:S(2)}) %collective-permute-start.2) | collective-permute-done | bytes 69664 | tf_op jit(solution)/shard_map/ppermute | solution.py:329
  24.4 1.8 %collective-permute-start.3 = (f32[136,128]{1,0:T(8,128)S(1)}, f32[136,128]{1,0:T(8,128)S(1)}, u32[]{:S(2)}, u32[]{:S(2)}) collective-permute-start(f32[136,128]{1,0:T(8,128)S(1)} %pad_maximum_fusion.own_ref), channel_id=1, source_target_pairs={{0,96},{16,112},{32,0},{48,16},{64,32},{80,48},{96,64},{112,80},{1... | collective-permute-start | bytes 208904 | tf_op jit(solution)/shard_map/ppermute | solution.py:329
  26.3 2.4 %collective-permute-done.3.three_ref = f32[136,128]{1,0:T(8,128)S(1)} collective-permute-done((f32[136,128]{1,0:T(8,128)S(1)}, f32[136,128]{1,0:T(8,128)S(1)}, u32[]{:S(2)}, u32[]{:S(2)}) %collective-permute-start.3) | collective-permute-done | bytes 69664 | tf_op jit(solution)/shard_map/ppermute | solution.py:329
  28.7 1.0 copy-done.7
  29.7 1.1 pack.1
  30.8 1.6 %collective-permute-start.6 = (f32[28,8,128]{2,1,0:T(8,128)S(1)}, f32[28,8,128]{2,1,0:T(8,128)S(1)}, u32[]{:S(2)}, u32[]{:S(2)}) collective-permute-start(f32[28,8,128]{2,1,0:T(8,128)S(1)} %get-tuple-element.47), channel_id=1, source_target_pairs={{0,4},{1,5},{2,6},{3,7},{4,8},{5,9},{6,10},{7,11},{8,12},{9,13},{1... | collective-permute-start | bytes 344072 | tf_op jit(solution)/shard_map/ppermute | solution.py:337
  32.4 2.2 %collective-permute-start.7 = (f32[28,8,128]{2,1,0:T(8,128)S(1)}, f32[28,8,128]{2,1,0:T(8,128)S(1)}, u32[]{:S(2)}, u32[]{:S(2)}) collective-permute-start(f32[28,8,128]{2,1,0:T(8,128)S(1)} %get-tuple-element.48), channel_id=1, source_target_pairs={{0,8},{1,9},{2,10},{3,11},{4,12},{5,13},{6,14},{7,15},{8,0},{9,1},... | collective-permute-start | bytes 344072 | tf_op jit(solution)/shard_map/ppermute | solution.py:337
  34.6 1.2 collective-permute-start.8
  36.1 2.7 %collective-permute-start.10 = (f32[28,8,128]{2,1,0:T(8,128)S(1)}, f32[28,8,128]{2,1,0:T(8,128)S(1)}, u32[]{:S(2)}, u32[]{:S(2)}) collective-permute-start(f32[28,8,128]{2,1,0:T(8,128)S(1)} %get-tuple-element.52), channel_id=1, source_target_pairs={{0,2},{1,3},{2,0},{3,1},{4,6},{5,7},{6,4},{7,5},{8,10},{9,11},{10,... | collective-permute-start | bytes 344072 | tf_op jit(solution)/shard_map/ppermute | solution.py:337
  38.8 1.4 %collective-permute-start.11 = (f32[28,8,128]{2,1,0:T(8,128)S(1)}, f32[28,8,128]{2,1,0:T(8,128)S(1)}, u32[]{:S(2)}, u32[]{:S(2)}) collective-permute-start(f32[28,8,128]{2,1,0:T(8,128)S(1)} %get-tuple-element.53), channel_id=1, source_target_pairs={{0,3},{1,0},{2,1},{3,2},{4,7},{5,4},{6,5},{7,6},{8,11},{9,8},{10,9... | collective-permute-start | bytes 344072 | tf_op jit(solution)/shard_map/ppermute | solution.py:337
  40.2 2.8 %collective-permute-done.9.refs_5_ = f32[28,8,128]{2,1,0:T(8,128)S(1)} collective-permute-done((f32[28,8,128]{2,1,0:T(8,128)S(1)}, f32[28,8,128]{2,1,0:T(8,128)S(1)}, u32[]{:S(2)}, u32[]{:S(2)}) %collective-permute-start.9) | collective-permute-done | bytes 114720 | tf_op jit(solution)/shard_map/ppermute | solution.py:337
  43.0 0.9 collective-permute-done.11.refs_7_
  43.9 1.3 collective-permute-start.14
  45.2 2.9 %collective-permute-start.15 = (f32[4,28,8,128]{3,2,1,0:T(8,128)S(1)}, f32[4,28,8,128]{3,2,1,0:T(8,128)S(1)}, u32[]{:S(2)}, u32[]{:S(2)}) collective-permute-start(f32[4,28,8,128]{3,2,1,0:T(8,128)S(1)} %get-tuple-element.54.refs_0_), channel_id=1, source_target_pairs={{0,2},{1,3},{2,0},{3,1},{4,6},{5,7},{6,4},{7,5},{8,10},{9,11},{10,... | collective-permute-start | bytes 1376264 | tf_op jit(solution)/shard_map/ppermute | solution.py:337
  48.4 0.8 collective-permute-start.17
  49.3 2.6 %collective-permute-start.18 = (f32[4,28,8,128]{3,2,1,0:T(8,128)S(1)}, f32[4,28,8,128]{3,2,1,0:T(8,128)S(1)}, u32[]{:S(2)}, u32[]{:S(2)}) collective-permute-start(f32[4,28,8,128]{3,2,1,0:T(8,128)S(1)} %get-tuple-element.55.refs_4_), channel_id=1, source_target_pairs={{0,8},{1,9},{2,10},{3,11},{4,12},{5,13},{6,14},{7,15},{8,0},{9,1},... | collective-permute-start | bytes 1376264 | tf_op jit(solution)/shard_map/ppermute | solution.py:337
  51.9 6.7 %collective-permute-done.14.refs_1_.refs_0_ = f32[4,28,8,128]{3,2,1,0:T(8,128)S(1)} collective-permute-done((f32[4,28,8,128]{3,2,1,0:T(8,128)S(1)}, f32[4,28,8,128]{3,2,1,0:T(8,128)S(1)}, u32[]{:S(2)}, u32[]{:S(2)}) %collective-permute-start.14) | collective-permute-done | bytes 458784 | tf_op jit(solution)/shard_map/ppermute | solution.py:337
  58.6 1.3 collective-permute-start.19
  59.9 4.0 %collective-permute-done.15.refs_2_ = f32[4,28,8,128]{3,2,1,0:T(8,128)S(1)} collective-permute-done((f32[4,28,8,128]{3,2,1,0:T(8,128)S(1)}, f32[4,28,8,128]{3,2,1,0:T(8,128)S(1)}, u32[]{:S(2)}, u32[]{:S(2)}) %collective-permute-start.15) | collective-permute-done | bytes 458784 | tf_op jit(solution)/shard_map/ppermute | solution.py:337
  64.0 3.8 %collective-permute-done.19.refs_7_ = f32[4,28,8,128]{3,2,1,0:T(8,128)S(1)} collective-permute-done((f32[4,28,8,128]{3,2,1,0:T(8,128)S(1)}, f32[4,28,8,128]{3,2,1,0:T(8,128)S(1)}, u32[]{:S(2)}, u32[]{:S(2)}) %collective-permute-start.19) | collective-permute-done | bytes 458784 | tf_op jit(solution)/shard_map/ppermute | solution.py:337
  68.2 0.8 cut.1
  69.1 2.6 %collective-permute-start.21 = (f32[128,1536]{1,0:T(8,128)S(1)}, f32[128,1536]{1,0:T(8,128)S(1)}, u32[]{:S(2)}, u32[]{:S(2)}) collective-permute-start(f32[128,1536]{1,0:T(8,128)S(1)} %get-tuple-element.67), channel_id=1, source_target_pairs={{0,8},{1,9},{2,10},{3,11},{4,12},{5,13},{6,14},{7,15},{8,0},{9,1},... | collective-permute-start | bytes 2359304 | tf_op jit(solution)/shard_map/ppermute | solution.py:337
  71.7 1.5 %collective-permute-start.22 = (f32[128,1536]{1,0:T(8,128)S(1)}, f32[128,1536]{1,0:T(8,128)S(1)}, u32[]{:S(2)}, u32[]{:S(2)}) collective-permute-start(f32[128,1536]{1,0:T(8,128)S(1)} %get-tuple-element.68), channel_id=1, source_target_pairs={{0,2},{1,3},{2,0},{3,1},{4,6},{5,7},{6,4},{7,5},{8,10},{9,11},{10,... | collective-permute-start | bytes 2359304 | tf_op jit(solution)/shard_map/ppermute | solution.py:337
  73.2 4.6 %forward.1 = (f32[128,512]{1,0:T(8,128)S(1)}, f32[128,512]{1,0:T(8,128)S(1)}, f32[2,4,1024]{2,1,0:T(4,128)}) custom-call(s32[4]{0:T(128)S(1)} %pad_add_fusion.place_ref, f32[32,16,8,128]{3,2,1,0:T(8,128)S(1)} %get-tuple-element.56.mine_ref.refs_0_, f32[32,16,8,128]{3,2,1,0:T(8,128)S(1)} %collective-permute-done.20.other_ref.refs_1_, ...), custom_call_target="tpu_custom_call" | custom-call | bytes 21000000 | tf_op jit(solution)/shard_map/forward/pallas_call | solution.py:312
  77.8 5.7 %early.1 = (f32[4,4,32,128]{3,2,1,0:T(8,128)S(1)}, f32[128,1536]{1,0:T(8,128)S(1)}, f32[128,1536]{1,0:T(8,128)S(1)}) custom-call(s32[4]{0:T(128)S(1)} %pad_add_fusion.place_ref, f32[128,512]{1,0:T(8,128)S(1)} %get-tuple-element.58.refs_0_, f32[128,512]{1,0:T(8,128)S(1)} %get-tuple-element.59.refs_1_, f32[128,1536]{1,0:T(8,128)S(1)} %get-tuple-element.60.refs_2_, ...), custom_call_target="tpu_custom_call" | custom-call | bytes 21000000 | tf_op jit(solution)/shard_map/early/pallas_call | solution.py:312
  83.4 7.1 %collective-permute-done.21.refs_7_ = f32[128,1536]{1,0:T(8,128)S(1)} collective-permute-done((f32[128,1536]{1,0:T(8,128)S(1)}, f32[128,1536]{1,0:T(8,128)S(1)}, u32[]{:S(2)}, u32[]{:S(2)}) %collective-permute-start.21) | collective-permute-done | bytes 786464 | tf_op jit(solution)/shard_map/ppermute | solution.py:337
  90.6 2.3 %collective-permute-done.22.refs_8_ = f32[128,1536]{1,0:T(8,128)S(1)} collective-permute-done((f32[128,1536]{1,0:T(8,128)S(1)}, f32[128,1536]{1,0:T(8,128)S(1)}, u32[]{:S(2)}, u32[]{:S(2)}) %collective-permute-start.22) | collective-permute-done | bytes 786464 | tf_op jit(solution)/shard_map/ppermute | solution.py:337
  92.8 3.0 %late.1 = (f32[32,1536]{1,0:T(8,128)S(1)}, f32[32,1536]{1,0:T(8,128)S(1)}, f32[32,1536]{1,0:T(8,128)}, f32[32,1536]{1,0:T(8,128)}, f32[32,2048]{1,0:T(8,128)S(1)...) custom-call(s32[4]{0:T(128)S(1)} %pad_add_fusion.place_ref, ...), custom_call_target="tpu_custom_call" | custom-call | bytes 10500000 | tf_op jit(solution)/shard_map/late/pallas_call | solution.py:312
  95.9 1.0 collective-permute-start.23
  96.9 1.4 collective-permute-start.27
  98.3 2.1 %collective-permute-start.28 = (f32[32,2048]{1,0:T(8,128)}, f32[32,2048]{1,0:T(8,128)}, u32[]{:S(2)}, u32[]{:S(2)}) collective-permute-start(f32[32,2048]{1,0:T(8,128)} %get-tuple-element.76), channel_id=1, source_target_pairs={{0,4},{1,5},{2,6},{3,7},{4,8},{5,9},{6,10},{7,11},{8,12},{9,13},{1... | collective-permute-start | bytes 786440 | tf_op jit(solution)/shard_map/ppermute | solution.py:337
  100.4 2.6 %collective-permute-start.24 = (f32[32,1536]{1,0:T(8,128)}, f32[32,1536]{1,0:T(8,128)}, u32[]{:S(2)}, u32[]{:S(2)}) collective-permute-start(f32[32,1536]{1,0:T(8,128)} %get-tuple-element.71), channel_id=1, source_target_pairs={{0,2},{1,3},{2,0},{3,1},{4,6},{5,7},{6,4},{7,5},{8,10},{9,11},{10,... | collective-permute-start | bytes 589832 | tf_op jit(solution)/shard_map/ppermute | solution.py:337
  103.0 0.5 collective-permute-start.25
  103.6 0.6 constant_dynamic-slice_fusion
  104.2 1.4 reshape.25.refs_3_
  105.6 1.6 %copy-done.4 = f32[32,16,8,128]{3,2,1,0:T(8,128)S(1)} copy-done((f32[32,16,8,128]{3,2,1,0:T(8,128)S(1)}, f32[32,16,8,128]{3,2,1,0:T(8,128)}, u32[]{:S(2)}) %copy-start.4) | copy-done | bytes 2097176
  107.2 1.2 copy-done.6
  108.4 0.8 copy-done.9
  109.6 2.0 %collective-permute-done.25.refs_3_ = f32[32,1536]{1,0:T(8,128)} collective-permute-done((f32[32,1536]{1,0:T(8,128)}, f32[32,1536]{1,0:T(8,128)}, u32[]{:S(2)}, u32[]{:S(2)}) %collective-permute-start.25) | collective-permute-done | bytes 196640 | tf_op jit(solution)/shard_map/ppermute | solution.py:337
  111.9 1.4 middle.1
  113.3 1.1 collective-permute-start.32
  114.5 2.0 %collective-permute-start.33 = (f32[8,4096]{1,0:T(8,128)S(1)}, f32[8,4096]{1,0:T(8,128)S(1)}, u32[]{:S(2)}, u32[]{:S(2)}) collective-permute-start(f32[8,4096]{1,0:T(8,128)S(1)} %get-tuple-element.84), channel_id=1, source_target_pairs={{0,2},{1,3},{2,0},{3,1},{4,6},{5,7},{6,4},{7,5},{8,10},{9,11},{10,... | collective-permute-start | bytes 393224 | tf_op jit(solution)/shard_map/ppermute | solution.py:337
  116.5 0.9 collective-permute-start.34
  117.4 1.5 %collective-permute-start.29 = (f32[8,1536]{1,0:T(8,128)S(1)}, f32[8,1536]{1,0:T(8,128)S(1)}, u32[]{:S(2)}, u32[]{:S(2)}) collective-permute-start(f32[8,1536]{1,0:T(8,128)S(1)} %get-tuple-element.79), channel_id=1, source_target_pairs={{0,12},{1,13},{2,14},{3,15},{4,0},{5,1},{6,2},{7,3},{8,4},{9,5},{1... | collective-permute-start | bytes 147464 | tf_op jit(solution)/shard_map/ppermute | solution.py:337
  119.2 2.3 %collective-permute-done.33.refs_2_.refs_6_ = f32[8,4096]{1,0:T(8,128)S(1)} collective-permute-done((f32[8,4096]{1,0:T(8,128)S(1)}, f32[8,4096]{1,0:T(8,128)S(1)}, u32[]{:S(2)}, u32[]{:S(2)}) %collective-permute-start.33) | collective-permute-done | bytes 131104 | tf_op jit(solution)/shard_map/ppermute | solution.py:337
  121.5 1.4 collective-permute-done.34.refs_3_.refs_7_
  122.8 0.8 last.1.refs_8_
  123.8 2.2 %collective-permute-start.30 = (f32[8,1536]{1,0:T(8,128)S(1)}, f32[8,1536]{1,0:T(8,128)S(1)}, u32[]{:S(2)}, u32[]{:S(2)}) collective-permute-start(f32[8,1536]{1,0:T(8,128)S(1)} %get-tuple-element.80), channel_id=1, source_target_pairs={{0,8},{1,9},{2,10},{3,11},{4,12},{5,13},{6,14},{7,15},{8,0},{9,1},... | collective-permute-start | bytes 147464 | tf_op jit(solution)/shard_map/ppermute | solution.py:337
  126.0 2.2 %collective-permute-start.31 = (f32[8,1536]{1,0:T(8,128)S(1)}, f32[8,1536]{1,0:T(8,128)S(1)}, u32[]{:S(2)}, u32[]{:S(2)}) collective-permute-start(f32[8,1536]{1,0:T(8,128)S(1)} %get-tuple-element.81), channel_id=1, source_target_pairs={{0,4},{1,5},{2,6},{3,7},{4,8},{5,9},{6,10},{7,11},{8,12},{9,13},{1... | collective-permute-start | bytes 147464 | tf_op jit(solution)/shard_map/ppermute | solution.py:337
  128.3 4.0 %collective-permute-start.37 = (f32[8,8,128]{2,1,0:T(8,128)S(1)}, f32[8,8,128]{2,1,0:T(8,128)S(1)}, u32[]{:S(2)}, u32[]{:S(2)}) collective-permute-start(f32[8,8,128]{2,1,0:T(8,128)S(1)} %add.101.refs_0_), channel_id=1, source_target_pairs={{0,64},{16,80},{32,96},{48,112},{64,0},{80,16},{96,32},{112,48},{1... | collective-permute-start | bytes 98312 | tf_op jit(solution)/shard_map/ppermute | solution.py:329
  132.5 1.4 finish.1
  133.9 0.6 collective-permute-done.37.refs_2_
  134.5 1.7 %collective-permute-done.38.refs_3_ = f32[8,8,128]{2,1,0:T(8,128)S(1)} collective-permute-done((f32[8,8,128]{2,1,0:T(8,128)S(1)}, f32[8,8,128]{2,1,0:T(8,128)S(1)}, u32[]{:S(2)}, u32[]{:S(2)}) %collective-permute-start.38) | collective-permute-done | bytes 32800 | tf_op jit(solution)/shard_map/ppermute | solution.py:329
  136.2 4.6 %backward.1 = f32[2,4,1024]{2,1,0:T(4,128)} custom-call(s32[4]{0:T(128)S(1)} %pad_add_fusion.place_ref, f32[8,1024]{1,0:T(8,128)S(1)} %get-tuple-element.86.loads_ref, f32[8,8,128]{2,1,0:T(8,128)S(1)} %add.101.refs_0_, f32[8,8,128]{2,1,0:T(8,128)S(1)} %collective-permute-done.36.refs_1_, f32[8,8,128]{2,1,0:T(8,128)S(1)} %collective-permute-done.37.refs_2_, ...), custom_call_target="tpu_custom_call" | custom-call | bytes 21000000 | tf_op jit(solution)/shard_map/backward/pallas_call | solution.py:312
  (62 shorter events, 3.4 us)
Async XLA Ops:
  0.6 102.9 %copy-start = (f32[2,64,1024]{2,1,0:T(8,128)S(1)}, f32[2,64,1024]{2,1,0:T(8,128)}, u32[]{:S(2)}) copy-start(f32[2,64,1024]{2,1,0:T(8,128)} %param.9) | copy-start | bytes 1572868
  0.7 11.1 %slice-start.2 = ((f32[2,4,12288]{2,1,0:T(4,128)}), f32[2,4,128]{2,1,0:T(4,128)S(1)}, s32[]{:S(2)}) async-start(f32[2,4,12288]{2,1,0:T(4,128)} %loads_ref.1), calls=%async_computation.2 | async-start | bytes 8192 | tf_op jit(solution)/shard_map/slice | solution.py:371
  0.8 67.5 %slice-start = ((s8[6291456]{0:T(1024)(128)(4,1)}), s8[2097152]{0:T(1024)(128)(4,1)S(1)}, s32[]{:S(2)}) async-start(s8[6291456]{0:T(1024)(128)(4,1)} %bitcast.13), calls=%async_computation | async-start | bytes 4194304
  4.4 24.3 %collective-permute-start.4 = (f32[128,1536]{1,0:T(8,128)}, f32[128,1536]{1,0:T(8,128)S(1)}, u32[]{:S(2)}, u32[]{:S(2)}) collective-permute-start(f32[128,1536]{1,0:T(8,128)} %get-tuple-element.92), channel_id=1, source_target_pairs={{0,4},{1,5},{2,6},{3,7},{4,8},{5,9},{6,10},{7,11},{8,12},{9,13},{1... | collective-permute-start | bytes 2359304 | tf_op jit(solution)/shard_map/ppermute | solution.py:337
  6.0 22.7 %collective-permute-start.5 = (f32[128,1536]{1,0:T(8,128)}, f32[128,1536]{1,0:T(8,128)}, u32[]{:S(2)}, u32[]{:S(2)}) collective-permute-start(f32[128,1536]{1,0:T(8,128)} %get-tuple-element.91), channel_id=1, source_target_pairs={{0,1},{1,2},{2,3},{3,0},{4,5},{5,6},{6,7},{7,4},{8,9},{9,10},{10,1... | collective-permute-start | bytes 2359304 | tf_op jit(solution)/shard_map/ppermute | solution.py:337
  7.5 28.3 %collective-permute-start.12 = (f32[128,1536]{1,0:T(8,128)}, f32[128,1536]{1,0:T(8,128)}, u32[]{:S(2)}, u32[]{:S(2)}) collective-permute-start(f32[128,1536]{1,0:T(8,128)} %get-tuple-element.90), channel_id=1, source_target_pairs={{0,12},{1,13},{2,14},{3,15},{4,0},{5,1},{6,2},{7,3},{8,4},{9,5},{1... | collective-permute-start | bytes 2359304 | tf_op jit(solution)/shard_map/ppermute | solution.py:337
  8.0 28.1 %collective-permute-start.13 = (f32[128,1536]{1,0:T(8,128)}, f32[128,1536]{1,0:T(8,128)}, u32[]{:S(2)}, u32[]{:S(2)}) collective-permute-start(f32[128,1536]{1,0:T(8,128)} %get-tuple-element.89), channel_id=1, source_target_pairs={{0,3},{1,0},{2,1},{3,2},{4,7},{5,4},{6,5},{7,6},{8,11},{9,8},{10,9... | collective-permute-start | bytes 2359304 | tf_op jit(solution)/shard_map/ppermute | solution.py:337
  10.6 1.3 collective-permute-start
  11.9 6.6 %collective-permute-start.1 = (f32[136,128]{1,0:T(8,128)S(1)}, f32[136,128]{1,0:T(8,128)S(1)}, u32[]{:S(2)}, u32[]{:S(2)}) collective-permute-start(f32[136,128]{1,0:T(8,128)S(1)} %pad_maximum_fusion.own_ref), channel_id=1, source_target_pairs={{0,32},{16,48},{32,64},{48,80},{64,96},{80,112},{96,0},{112,16},{1... | collective-permute-start | bytes 208904 | tf_op jit(solution)/shard_map/ppermute | solution.py:329
  18.5 5.9 %collective-permute-start.2 = (f32[136,128]{1,0:T(8,128)S(1)}, f32[136,128]{1,0:T(8,128)}, u32[]{:S(2)}, u32[]{:S(2)}) collective-permute-start(f32[136,128]{1,0:T(8,128)S(1)} %pad_maximum_fusion.own_ref), channel_id=1, source_target_pairs={{0,64},{16,80},{32,96},{48,112},{64,0},{80,16},{96,32},{112,48},{1... | collective-permute-start | bytes 208904 | tf_op jit(solution)/shard_map/ppermute | solution.py:329
  24.4 4.3 %collective-permute-start.3 = (f32[136,128]{1,0:T(8,128)S(1)}, f32[136,128]{1,0:T(8,128)S(1)}, u32[]{:S(2)}, u32[]{:S(2)}) collective-permute-start(f32[136,128]{1,0:T(8,128)S(1)} %pad_maximum_fusion.own_ref), channel_id=1, source_target_pairs={{0,96},{16,112},{32,0},{48,16},{64,32},{80,48},{96,64},{112,80},{1... | collective-permute-start | bytes 208904 | tf_op jit(solution)/shard_map/ppermute | solution.py:329
  26.3 41.9 %slice-start.1 = ((s8[6291456]{0:T(1024)(128)(4,1)}), s8[4194304]{0:T(1024)(128)(4,1)S(1)}, s32[]{:S(2)}) async-start(s8[6291456]{0:T(1024)(128)(4,1)} %bitcast.13), calls=%async_computation.1 | async-start | bytes 8388608
  28.7 1.0 copy-start.7
  30.8 8.0 %collective-permute-start.6 = (f32[28,8,128]{2,1,0:T(8,128)S(1)}, f32[28,8,128]{2,1,0:T(8,128)S(1)}, u32[]{:S(2)}, u32[]{:S(2)}) collective-permute-start(f32[28,8,128]{2,1,0:T(8,128)S(1)} %get-tuple-element.47), channel_id=1, source_target_pairs={{0,4},{1,5},{2,6},{3,7},{4,8},{5,9},{6,10},{7,11},{8,12},{9,13},{1... | collective-permute-start | bytes 344072 | tf_op jit(solution)/shard_map/ppermute | solution.py:337
  32.4 7.8 %collective-permute-start.7 = (f32[28,8,128]{2,1,0:T(8,128)S(1)}, f32[28,8,128]{2,1,0:T(8,128)S(1)}, u32[]{:S(2)}, u32[]{:S(2)}) collective-permute-start(f32[28,8,128]{2,1,0:T(8,128)S(1)} %get-tuple-element.48), channel_id=1, source_target_pairs={{0,8},{1,9},{2,10},{3,11},{4,12},{5,13},{6,14},{7,15},{8,0},{9,1},... | collective-permute-start | bytes 344072 | tf_op jit(solution)/shard_map/ppermute | solution.py:337
  34.6 5.7 %collective-permute-start.8 = (f32[28,8,128]{2,1,0:T(8,128)S(1)}, f32[28,8,128]{2,1,0:T(8,128)S(1)}, u32[]{:S(2)}, u32[]{:S(2)}) collective-permute-start(f32[28,8,128]{2,1,0:T(8,128)S(1)} %get-tuple-element.49), channel_id=1, source_target_pairs={{0,12},{1,13},{2,14},{3,15},{4,0},{5,1},{6,2},{7,3},{8,4},{9,5},{1... | collective-permute-start | bytes 344072 | tf_op jit(solution)/shard_map/ppermute | solution.py:337
  35.8 7.2 %collective-permute-start.9 = (f32[28,8,128]{2,1,0:T(8,128)S(1)}, f32[28,8,128]{2,1,0:T(8,128)S(1)}, u32[]{:S(2)}, u32[]{:S(2)}) collective-permute-start(f32[28,8,128]{2,1,0:T(8,128)S(1)} %get-tuple-element.51), channel_id=1, source_target_pairs={{0,1},{1,2},{2,3},{3,0},{4,5},{5,6},{6,7},{7,4},{8,9},{9,10},{10,1... | collective-permute-start | bytes 344072 | tf_op jit(solution)/shard_map/ppermute | solution.py:337
  36.1 7.0 %collective-permute-start.10 = (f32[28,8,128]{2,1,0:T(8,128)S(1)}, f32[28,8,128]{2,1,0:T(8,128)S(1)}, u32[]{:S(2)}, u32[]{:S(2)}) collective-permute-start(f32[28,8,128]{2,1,0:T(8,128)S(1)} %get-tuple-element.52), channel_id=1, source_target_pairs={{0,2},{1,3},{2,0},{3,1},{4,6},{5,7},{6,4},{7,5},{8,10},{9,11},{10,... | collective-permute-start | bytes 344072 | tf_op jit(solution)/shard_map/ppermute | solution.py:337
  38.8 5.1 %collective-permute-start.11 = (f32[28,8,128]{2,1,0:T(8,128)S(1)}, f32[28,8,128]{2,1,0:T(8,128)S(1)}, u32[]{:S(2)}, u32[]{:S(2)}) collective-permute-start(f32[28,8,128]{2,1,0:T(8,128)S(1)} %get-tuple-element.53), channel_id=1, source_target_pairs={{0,3},{1,0},{2,1},{3,2},{4,7},{5,4},{6,5},{7,6},{8,11},{9,8},{10,9... | collective-permute-start | bytes 344072 | tf_op jit(solution)/shard_map/ppermute | solution.py:337
  43.9 14.7 %collective-permute-start.14 = (f32[4,28,8,128]{3,2,1,0:T(8,128)S(1)}, f32[4,28,8,128]{3,2,1,0:T(8,128)S(1)}, u32[]{:S(2)}, u32[]{:S(2)}) collective-permute-start(f32[4,28,8,128]{3,2,1,0:T(8,128)S(1)} %get-tuple-element.54.refs_0_), channel_id=1, source_target_pairs={{0,1},{1,2},{2,3},{3,0},{4,5},{5,6},{6,7},{7,4},{8,9},{9,10},{10,1... | collective-permute-start | bytes 1376264 | tf_op jit(solution)/shard_map/ppermute | solution.py:337
  45.2 18.7 %collective-permute-start.15 = (f32[4,28,8,128]{3,2,1,0:T(8,128)S(1)}, f32[4,28,8,128]{3,2,1,0:T(8,128)S(1)}, u32[]{:S(2)}, u32[]{:S(2)}) collective-permute-start(f32[4,28,8,128]{3,2,1,0:T(8,128)S(1)} %get-tuple-element.54.refs_0_), channel_id=1, source_target_pairs={{0,2},{1,3},{2,0},{3,1},{4,6},{5,7},{6,4},{7,5},{8,10},{9,11},{10,... | collective-permute-start | bytes 1376264 | tf_op jit(solution)/shard_map/ppermute | solution.py:337
  48.1 15.8 %collective-permute-start.16 = (f32[4,28,8,128]{3,2,1,0:T(8,128)S(1)}, f32[4,28,8,128]{3,2,1,0:T(8,128)S(1)}, u32[]{:S(2)}, u32[]{:S(2)}) collective-permute-start(f32[4,28,8,128]{3,2,1,0:T(8,128)S(1)} %get-tuple-element.54.refs_0_), channel_id=1, source_target_pairs={{0,3},{1,0},{2,1},{3,2},{4,7},{5,4},{6,5},{7,6},{8,11},{9,8},{10,9... | collective-permute-start | bytes 1376264 | tf_op jit(solution)/shard_map/ppermute | solution.py:337
  48.4 15.5 %collective-permute-start.17 = (f32[4,28,8,128]{3,2,1,0:T(8,128)S(1)}, f32[4,28,8,128]{3,2,1,0:T(8,128)S(1)}, u32[]{:S(2)}, u32[]{:S(2)}) collective-permute-start(f32[4,28,8,128]{3,2,1,0:T(8,128)S(1)} %get-tuple-element.55.refs_4_), channel_id=1, source_target_pairs={{0,4},{1,5},{2,6},{3,7},{4,8},{5,9},{6,10},{7,11},{8,12},{9,13},{1... | collective-permute-start | bytes 1376264 | tf_op jit(solution)/shard_map/ppermute | solution.py:337
  49.3 14.7 %collective-permute-start.18 = (f32[4,28,8,128]{3,2,1,0:T(8,128)S(1)}, f32[4,28,8,128]{3,2,1,0:T(8,128)S(1)}, u32[]{:S(2)}, u32[]{:S(2)}) collective-permute-start(f32[4,28,8,128]{3,2,1,0:T(8,128)S(1)} %get-tuple-element.55.refs_4_), channel_id=1, source_target_pairs={{0,8},{1,9},{2,10},{3,11},{4,12},{5,13},{6,14},{7,15},{8,0},{9,1},... | collective-permute-start | bytes 1376264 | tf_op jit(solution)/shard_map/ppermute | solution.py:337
  58.6 9.1 %collective-permute-start.19 = (f32[4,28,8,128]{3,2,1,0:T(8,128)S(1)}, f32[4,28,8,128]{3,2,1,0:T(8,128)S(1)}, u32[]{:S(2)}, u32[]{:S(2)}) collective-permute-start(f32[4,28,8,128]{3,2,1,0:T(8,128)S(1)} %get-tuple-element.55.refs_4_), channel_id=1, source_target_pairs={{0,12},{1,13},{2,14},{3,15},{4,0},{5,1},{6,2},{7,3},{8,4},{9,5},{1... | collective-permute-start | bytes 1376264 | tf_op jit(solution)/shard_map/ppermute | solution.py:337
  68.1 5.1 %copy-start.1 = (f32[32,16,8,128]{3,2,1,0:T(8,128)}, f32[32,16,8,128]{3,2,1,0:T(8,128)S(1)}, u32[]{:S(2)}) copy-start(f32[32,16,8,128]{3,2,1,0:T(8,128)S(1)} %get-tuple-element.56.mine_ref.refs_0_) | copy-start | bytes 6291460
  68.1 5.1 %copy-start.5 = (f32[2,8,128,128]{3,2,1,0:T(8,128)S(1)}, f32[2,8,128,128]{3,2,1,0:T(8,128)}, u32[]{:S(2)}) copy-start(f32[2,8,128,128]{3,2,1,0:T(8,128)} %refs_2_.1) | copy-start | bytes 3145732
  68.1 5.1 %collective-permute-start.20 = (f32[32,16,8,128]{3,2,1,0:T(8,128)S(1)}, f32[32,16,8,128]{3,2,1,0:T(8,128)S(1)}, u32[]{:S(2)}, u32[]{:S(2)}) collective-permute-start(f32[32,16,8,128]{3,2,1,0:T(8,128)S(1)} %get-tuple-element.56.mine_ref.refs_0_), channel_id=1, source_target_pairs={{0,16},{16,0},{32,48},{48,32},{64,80},{80,64},{96,112},{112,96},{1... | collective-permute-start | bytes 6291464 | tf_op jit(solution)/shard_map/ppermute | solution.py:325
  69.1 21.5 %collective-permute-start.21 = (f32[128,1536]{1,0:T(8,128)S(1)}, f32[128,1536]{1,0:T(8,128)S(1)}, u32[]{:S(2)}, u32[]{:S(2)}) collective-permute-start(f32[128,1536]{1,0:T(8,128)S(1)} %get-tuple-element.67), channel_id=1, source_target_pairs={{0,8},{1,9},{2,10},{3,11},{4,12},{5,13},{6,14},{7,15},{8,0},{9,1},... | collective-permute-start | bytes 2359304 | tf_op jit(solution)/shard_map/ppermute | solution.py:337
  71.7 21.1 %collective-permute-start.22 = (f32[128,1536]{1,0:T(8,128)S(1)}, f32[128,1536]{1,0:T(8,128)S(1)}, u32[]{:S(2)}, u32[]{:S(2)}) collective-permute-start(f32[128,1536]{1,0:T(8,128)S(1)} %get-tuple-element.68), channel_id=1, source_target_pairs={{0,2},{1,3},{2,0},{3,1},{4,6},{5,7},{6,4},{7,5},{8,10},{9,11},{10,... | collective-permute-start | bytes 2359304 | tf_op jit(solution)/shard_map/ppermute | solution.py:337
  73.2 4.6 %copy-start.3 = (f32[32,16,8,128]{3,2,1,0:T(8,128)}, f32[32,16,8,128]{3,2,1,0:T(8,128)S(1)}, u32[]{:S(2)}) copy-start(f32[32,16,8,128]{3,2,1,0:T(8,128)S(1)} %collective-permute-done.20.other_ref.refs_1_) | copy-start | bytes 6291460
  92.8 12.7 %copy-start.2 = (f32[32,16,8,128]{3,2,1,0:T(8,128)S(1)}, f32[32,16,8,128]{3,2,1,0:T(8,128)}, u32[]{:S(2)}) copy-start(f32[32,16,8,128]{3,2,1,0:T(8,128)} %copy-done.1) | copy-start | bytes 6291460
  95.9 7.2 %collective-permute-start.23 = (f32[32,1536]{1,0:T(8,128)S(1)}, f32[32,1536]{1,0:T(8,128)S(1)}, u32[]{:S(2)}, u32[]{:S(2)}) collective-permute-start(f32[32,1536]{1,0:T(8,128)S(1)} %get-tuple-element.70), channel_id=1, source_target_pairs={{0,3},{1,0},{2,1},{3,2},{4,7},{5,4},{6,5},{7,6},{8,11},{9,8},{10,9... | collective-permute-start | bytes 589832 | tf_op jit(solution)/shard_map/ppermute | solution.py:337
  96.8 14.8 %collective-permute-start.26 = (f32[32,2048]{1,0:T(8,128)}, f32[32,2048]{1,0:T(8,128)S(1)}, u32[]{:S(2)}, u32[]{:S(2)}) collective-permute-start(f32[32,2048]{1,0:T(8,128)} %get-tuple-element.74), channel_id=1, source_target_pairs={{0,12},{1,13},{2,14},{3,15},{4,0},{5,1},{6,2},{7,3},{8,4},{9,5},{1... | collective-permute-start | bytes 786440 | tf_op jit(solution)/shard_map/ppermute | solution.py:337
  96.9 14.6 %collective-permute-start.27 = (f32[32,2048]{1,0:T(8,128)}, f32[32,2048]{1,0:T(8,128)}, u32[]{:S(2)}, u32[]{:S(2)}) collective-permute-start(f32[32,2048]{1,0:T(8,128)} %get-tuple-element.75), channel_id=1, source_target_pairs={{0,8},{1,9},{2,10},{3,11},{4,12},{5,13},{6,14},{7,15},{8,0},{9,1},... | collective-permute-start | bytes 786440 | tf_op jit(solution)/shard_map/ppermute | solution.py:337
  98.3 13.6 %collective-permute-start.28 = (f32[32,2048]{1,0:T(8,128)}, f32[32,2048]{1,0:T(8,128)}, u32[]{:S(2)}, u32[]{:S(2)}) collective-permute-start(f32[32,2048]{1,0:T(8,128)} %get-tuple-element.76), channel_id=1, source_target_pairs={{0,4},{1,5},{2,6},{3,7},{4,8},{5,9},{6,10},{7,11},{8,12},{9,13},{1... | collective-permute-start | bytes 786440 | tf_op jit(solution)/shard_map/ppermute | solution.py:337
  100.4 9.2 %collective-permute-start.24 = (f32[32,1536]{1,0:T(8,128)}, f32[32,1536]{1,0:T(8,128)}, u32[]{:S(2)}, u32[]{:S(2)}) collective-permute-start(f32[32,1536]{1,0:T(8,128)} %get-tuple-element.71), channel_id=1, source_target_pairs={{0,2},{1,3},{2,0},{3,1},{4,6},{5,7},{6,4},{7,5},{8,10},{9,11},{10,... | collective-permute-start | bytes 589832 | tf_op jit(solution)/shard_map/ppermute | solution.py:337
  103.0 8.5 %collective-permute-start.25 = (f32[32,1536]{1,0:T(8,128)}, f32[32,1536]{1,0:T(8,128)}, u32[]{:S(2)}, u32[]{:S(2)}) collective-permute-start(f32[32,1536]{1,0:T(8,128)} %get-tuple-element.72), channel_id=1, source_target_pairs={{0,1},{1,2},{2,3},{3,0},{4,5},{5,6},{6,7},{7,4},{8,9},{9,10},{10,1... | collective-permute-start | bytes 589832 | tf_op jit(solution)/shard_map/ppermute | solution.py:337
  105.6 1.6 %copy-start.4 = (f32[32,16,8,128]{3,2,1,0:T(8,128)S(1)}, f32[32,16,8,128]{3,2,1,0:T(8,128)}, u32[]{:S(2)}) copy-start(f32[32,16,8,128]{3,2,1,0:T(8,128)} %copy-done.3) | copy-start | bytes 6291460
  107.2 1.2 copy-start.6
  108.4 0.8 copy-start.9
  111.9 20.6 %copy-start.8 = (f32[2,4,12288]{2,1,0:T(4,128)S(1)}, f32[2,4,12288]{2,1,0:T(4,128)}, u32[]{:S(2)}) copy-start(f32[2,4,12288]{2,1,0:T(4,128)} %loads_ref.1) | copy-start | bytes 1179652
  113.3 5.8 %collective-permute-start.32 = (f32[8,4096]{1,0:T(8,128)S(1)}, f32[8,4096]{1,0:T(8,128)S(1)}, u32[]{:S(2)}, u32[]{:S(2)}) collective-permute-start(f32[8,4096]{1,0:T(8,128)S(1)} %get-tuple-element.83), channel_id=1, source_target_pairs={{0,3},{1,0},{2,1},{3,2},{4,7},{5,4},{6,5},{7,6},{8,11},{9,8},{10,9... | collective-permute-start | bytes 393224 | tf_op jit(solution)/shard_map/ppermute | solution.py:337
  114.5 7.0 %collective-permute-start.33 = (f32[8,4096]{1,0:T(8,128)S(1)}, f32[8,4096]{1,0:T(8,128)S(1)}, u32[]{:S(2)}, u32[]{:S(2)}) collective-permute-start(f32[8,4096]{1,0:T(8,128)S(1)} %get-tuple-element.84), channel_id=1, source_target_pairs={{0,2},{1,3},{2,0},{3,1},{4,6},{5,7},{6,4},{7,5},{8,10},{9,11},{10,... | collective-permute-start | bytes 393224 | tf_op jit(solution)/shard_map/ppermute | solution.py:337
  116.5 6.4 %collective-permute-start.34 = (f32[8,4096]{1,0:T(8,128)S(1)}, f32[8,4096]{1,0:T(8,128)S(1)}, u32[]{:S(2)}, u32[]{:S(2)}) collective-permute-start(f32[8,4096]{1,0:T(8,128)S(1)} %get-tuple-element.85), channel_id=1, source_target_pairs={{0,1},{1,2},{2,3},{3,0},{4,5},{5,6},{6,7},{7,4},{8,9},{9,10},{10,1... | collective-permute-start | bytes 393224 | tf_op jit(solution)/shard_map/ppermute | solution.py:337
  117.4 14.9 %collective-permute-start.29 = (f32[8,1536]{1,0:T(8,128)S(1)}, f32[8,1536]{1,0:T(8,128)S(1)}, u32[]{:S(2)}, u32[]{:S(2)}) collective-permute-start(f32[8,1536]{1,0:T(8,128)S(1)} %get-tuple-element.79), channel_id=1, source_target_pairs={{0,12},{1,13},{2,14},{3,15},{4,0},{5,1},{6,2},{7,3},{8,4},{9,5},{1... | collective-permute-start | bytes 147464 | tf_op jit(solution)/shard_map/ppermute | solution.py:337
  123.7 4.5 %collective-permute-start.35 = (f32[8,8,128]{2,1,0:T(8,128)S(1)}, f32[8,8,128]{2,1,0:T(8,128)S(1)}, u32[]{:S(2)}, u32[]{:S(2)}) collective-permute-start(f32[8,8,128]{2,1,0:T(8,128)S(1)} %last.1.refs_8_), channel_id=1, source_target_pairs={{0,16},{16,0},{32,48},{48,32},{64,80},{80,64},{96,112},{112,96},{1... | collective-permute-start | bytes 98312 | tf_op jit(solution)/shard_map/ppermute | solution.py:325
  123.8 8.7 %collective-permute-start.30 = (f32[8,1536]{1,0:T(8,128)S(1)}, f32[8,1536]{1,0:T(8,128)S(1)}, u32[]{:S(2)}, u32[]{:S(2)}) collective-permute-start(f32[8,1536]{1,0:T(8,128)S(1)} %get-tuple-element.80), channel_id=1, source_target_pairs={{0,8},{1,9},{2,10},{3,11},{4,12},{5,13},{6,14},{7,15},{8,0},{9,1},... | collective-permute-start | bytes 147464 | tf_op jit(solution)/shard_map/ppermute | solution.py:337
  126.0 6.5 %collective-permute-start.31 = (f32[8,1536]{1,0:T(8,128)S(1)}, f32[8,1536]{1,0:T(8,128)S(1)}, u32[]{:S(2)}, u32[]{:S(2)}) collective-permute-start(f32[8,1536]{1,0:T(8,128)S(1)} %get-tuple-element.81), channel_id=1, source_target_pairs={{0,4},{1,5},{2,6},{3,7},{4,8},{5,9},{6,10},{7,11},{8,12},{9,13},{1... | collective-permute-start | bytes 147464 | tf_op jit(solution)/shard_map/ppermute | solution.py:337
  128.2 5.7 %collective-permute-start.36 = (f32[8,8,128]{2,1,0:T(8,128)S(1)}, f32[8,8,128]{2,1,0:T(8,128)S(1)}, u32[]{:S(2)}, u32[]{:S(2)}) collective-permute-start(f32[8,8,128]{2,1,0:T(8,128)S(1)} %add.101.refs_0_), channel_id=1, source_target_pairs={{0,32},{16,48},{32,64},{48,80},{64,96},{80,112},{96,0},{112,16},{1... | collective-permute-start | bytes 98312 | tf_op jit(solution)/shard_map/ppermute | solution.py:329
  128.3 6.2 %collective-permute-start.37 = (f32[8,8,128]{2,1,0:T(8,128)S(1)}, f32[8,8,128]{2,1,0:T(8,128)S(1)}, u32[]{:S(2)}, u32[]{:S(2)}) collective-permute-start(f32[8,8,128]{2,1,0:T(8,128)S(1)} %add.101.refs_0_), channel_id=1, source_target_pairs={{0,64},{16,80},{32,96},{48,112},{64,0},{80,16},{96,32},{112,48},{1... | collective-permute-start | bytes 98312 | tf_op jit(solution)/shard_map/ppermute | solution.py:329
  132.3 3.9 %collective-permute-start.38 = (f32[8,8,128]{2,1,0:T(8,128)S(1)}, f32[8,8,128]{2,1,0:T(8,128)S(1)}, u32[]{:S(2)}, u32[]{:S(2)}) collective-permute-start(f32[8,8,128]{2,1,0:T(8,128)S(1)} %add.101.refs_0_), channel_id=1, source_target_pairs={{0,96},{16,112},{32,0},{48,16},{64,32},{80,48},{96,64},{112,80},{1... | collective-permute-start | bytes 98312 | tf_op jit(solution)/shard_map/ppermute | solution.py:329
